TPU v7x, 256 devices: a whole 4x4x8 slice. The times are simulated.
256 devices in a mesh: seq: 32 (over z, y_lo, core), head: 8 (over y_hi, x).
Axes of the slice: x: 4, y: 4 (y_hi: 2, y_lo: 2; y = y_hi * 2 + y_lo), z: 8, core: 2. Of those that a mesh axis runs over, the one named last changes fastest.
Arguments:
- query_rows: bfloat16 [8192, 4096], P(('seq', 'head')), may hold values from -48 to 48
- key_rows: bfloat16 [8192, 4096], P(('seq', 'head')), may hold values from -4 to 4
- value_rows: bfloat16 [8192, 4096], P(('seq', 'head')), may hold values from -6 to 6
- grad_rows: bfloat16 [8192, 4096], P(('seq', 'head')), may hold values from -6 to 6
Outputs:
- attended: bfloat16 [8192, 4096], P(('seq', 'head'))
- query_grad: bfloat16 [8192, 4096], P(('seq', 'head'))
- key_grad: bfloat16 [8192, 4096], P(('seq', 'head'))
- value_grad: bfloat16 [8192, 4096], P(('seq', 'head'))
All inputs are finite; a program needn't handle non-finite values.
Results may differ from a plain program's by a relative error of at most 0.009.
Values may be sent and summed in bfloat16 or wider, within the bound.
No kernel may reach another device: no remote copies, remote signals or barrier semaphores. Data moves between devices by JAX's collectives and lax.ppermute only.
A program may use at most 128 MiB of HBM per device.

v0:
```python
import functools

import jax
import jax.numpy as jnp
from jax import lax
from jax.experimental import pallas as pl
from jax.experimental.pallas import tpu as pltpu
from jax.sharding import Mesh, PartitionSpec as P

HEAD_DIM = 128
PLANE = 32
ROWS = 32
TOKENS = PLANE * ROWS
SEG = 512
MID = 256
LOW = 384
SCALE = HEAD_DIM**-0.5
RATE = SCALE * 1.4426950408889634
NEG = -1e30
BF = jnp.bfloat16
F32 = jnp.float32


def nn(a, b):
    return jnp.dot(a, b, preferred_element_type=F32)


def nt(a, b):
    return lax.dot_general(a, b, (((1,), (1,)), ((), ())), preferred_element_type=F32)


def flip(a):
    return jnp.swapaxes(a, 0, 1)


def token_of(spot, offset, half):
    if half == 0:
        far = [2 * spot, 4 * (spot - 256), 8 * (spot - 384), 8 * (spot - 448)]
        tests = [spot < 256, spot < 384, spot < 448]
    else:
        far = [2 * (spot - 256), 4 * (spot - 128), 8 * (spot - 64), 8 * spot]
        tests = [spot >= 256, spot >= 128, spot >= 64]
    return jnp.where(
        tests[0],
        far[0] + ((offset + 1) & 1),
        jnp.where(
            tests[1],
            far[1] + ((offset + 2) & 3),
            jnp.where(tests[2], far[2] + ((offset + 4) & 7), far[3] + offset),
        ),
    )


def ordering(offset, half, first, count):
    spot = lax.broadcasted_iota(jnp.int32, (count, 1), 0) + first
    token = lax.broadcasted_iota(jnp.int32, (count, SEG), 1)
    return jnp.where(token_of(spot, offset, half) == token, 1.0, 0.0).astype(BF)


def unordering(offset, half, first, count):
    spot = lax.broadcasted_iota(jnp.int32, (1, count), 1) + first
    token = lax.broadcasted_iota(jnp.int32, (SEG, count), 0)
    return jnp.where(token_of(spot, offset, half) == token, 1.0, 0.0).astype(BF)


def head_offset():
    return lax.axis_index("plane") & 7


def pack_kernel(key_ref, value_ref, query_ref, grad_ref, out_ref):
    for index in range(out_ref.shape[0]):
        cut = slice(index * HEAD_DIM, (index + 1) * HEAD_DIM)
        out_ref[index, 0] = key_ref[:, cut]
        out_ref[index, 1] = value_ref[:, cut]
        out_ref[index, 2] = query_ref[:, cut]
        out_ref[index, 3] = grad_ref[:, cut]


def unpack_kernel(in_ref, att_ref, query_ref, key_ref, value_ref):
    for index in range(in_ref.shape[0]):
        cut = slice(index * HEAD_DIM, (index + 1) * HEAD_DIM)
        att_ref[:, cut] = in_ref[index, 0]
        query_ref[:, cut] = in_ref[index, 1]
        key_ref[:, cut] = in_ref[index, 2]
        value_ref[:, cut] = in_ref[index, 3]


def select_kernel(got_ref, out_ref):
    offset = head_offset()
    for half in range(2):
        rows = slice(half * 16, half * 16 + 16)
        pair = jnp.concatenate(
            [got_ref[rows, 0].reshape(SEG, HEAD_DIM), got_ref[rows, 1].reshape(SEG, HEAD_DIM)],
            axis=1,
        )
        picked = nn(ordering(offset, half, LOW if half == 0 else 0, 128), pair).astype(BF)
        out_ref[0, half * 128 : half * 128 + 128] = picked[:, :HEAD_DIM]
        out_ref[1, half * 128 : half * 128 + 128] = picked[:, HEAD_DIM:]


def segment_start(step):
    segment = step // 2
    start = jnp.where(segment == 2, 256, segment * SEG)
    return pl.multiple_of(start, 256), pl.multiple_of(start + (step % 2) * 256, 256)


def merge(peak, total, acc, peak_new, total_new, acc_new):
    best = jnp.maximum(peak, peak_new)
    left = jnp.exp2((peak - best) * RATE)
    right = jnp.exp2((peak_new - best) * RATE)
    return best, left * total + right * total_new, left * acc + right * acc_new


def local_kernel(got_ref, x_ref, mid_ref, stat_ref, comb_ref, mid_stat_ref, mid_acc_ref, vt, peak, total, acc):
    offset = head_offset()
    for half in range(2):
        rows = slice(half * 16, half * 16 + 16)
        four = jnp.concatenate(
            [got_ref[rows, index].reshape(SEG, HEAD_DIM) for index in range(4)], axis=1
        )
        ordered = nn(ordering(offset, half, 0, SEG), four).astype(BF)
        for index in range(4):
            x_ref[index, half * SEG : half * SEG + SEG] = ordered[
                :, index * HEAD_DIM : (index + 1) * HEAD_DIM
            ]
        vt[:, half * SEG : half * SEG + SEG] = flip(ordered[:, HEAD_DIM : 2 * HEAD_DIM])
    for index in range(4):
        mid_ref[index] = x_ref[index, LOW : LOW + MID]
    peak[...] = jnp.full_like(peak, NEG)
    total[...] = jnp.zeros_like(total)
    acc[...] = jnp.zeros_like(acc)

    def body(step, carry):
        start, first = segment_start(step)
        scores = nt(x_ref[0, pl.ds(start, SEG)], x_ref[2, pl.ds(first, 256)])
        top = jnp.max(scores, axis=0, keepdims=True)
        weights = jnp.exp2((scores - top) * RATE)
        cut = pl.ds(first, 256)
        peak[:, cut], total[:, cut], acc[:, cut] = merge(
            peak[:, cut],
            total[:, cut],
            acc[:, cut],
            top,
            jnp.sum(weights, axis=0, keepdims=True),
            nn(vt[:, pl.ds(start, SEG)], weights.astype(BF)),
        )
        return carry

    lax.fori_loop(0, 6, body, 0)
    mid_stat_ref[0:1] = peak[:, LOW : LOW + MID]
    mid_stat_ref[1:2] = total[:, LOW : LOW + MID]
    mid_acc_ref[...] = acc[:, LOW : LOW + MID]
    combined = acc[...] / total[...]
    comb_ref[...] = combined.astype(BF)
    stat_ref[0:1] = peak[...] * RATE + jnp.log2(total[...])
    stat_ref[1:2] = jnp.sum(flip(x_ref[3]).astype(F32) * combined, axis=0, keepdims=True)


def widen(part, filler):
    return pltpu.roll(jnp.concatenate([part, jnp.full_like(part, filler)], axis=1), 64, 1)


def narrow(whole):
    return pltpu.roll(whole, MID - 64, 1)[:, :128]


def forward_of(keys, values, queries):
    scores = nt(keys, queries)
    peak = jnp.max(scores, axis=0, keepdims=True)
    weights = jnp.exp2((scores - peak) * RATE)
    total = jnp.sum(weights, axis=0, keepdims=True)
    return peak, weights, total, nn(flip(values), weights.astype(BF))


def backward_of(probs, keys, values, queries, grads, dot):
    score_grad = (probs * (nt(values, grads) - dot)).astype(BF)
    return (
        nn(flip(keys), score_grad) * SCALE,
        nn(score_grad, queries) * SCALE,
        nn(probs.astype(BF), grads),
    )


def join(whole, part):
    return jnp.concatenate([whole[:64], whole[64:192] + part, whole[192:]], axis=0)


def far_kernel(mid_ref, stat_ref, acc_ref, one_ref, two_ref, three_ref,
               out_stat_ref, comb_ref, query_ref, own_ref, send_one_ref, send_two_ref, send_three_ref):
    keys2 = jnp.concatenate([mid_ref[0], one_ref[0]], axis=0)
    values2 = jnp.concatenate([mid_ref[1], one_ref[1]], axis=0)
    keys3 = jnp.concatenate([mid_ref[0, 64:192], one_ref[0, 64:192], two_ref[0], three_ref[0]], axis=0)
    values3 = jnp.concatenate([mid_ref[1, 64:192], one_ref[1, 64:192], two_ref[1], three_ref[1]], axis=0)
    queries2, grads2 = mid_ref[2], mid_ref[3]
    queries3, grads3 = mid_ref[2, 64:192], mid_ref[3, 64:192]
    peak2, weights2, total2, acc2 = forward_of(keys2, values2, queries2)
    peak3, weights3, total3, acc3 = forward_of(keys3, values3, queries3)
    state = merge(stat_ref[0:1], stat_ref[1:2], acc_ref[...], peak2, total2, acc2)
    peak, total, acc = merge(*state, widen(peak3, NEG), widen(total3, 0.0), widen(acc3, 0.0))
    combined = acc / total
    log_total = peak * RATE + jnp.log2(total)
    dot = jnp.sum(flip(grads2).astype(F32) * combined, axis=0, keepdims=True)
    out_stat_ref[0:1] = log_total
    out_stat_ref[1:2] = dot
    comb_ref[...] = combined.astype(BF)
    probs2 = weights2 * jnp.exp2(peak2 * RATE - log_total)
    probs3 = weights3 * jnp.exp2(peak3 * RATE - narrow(log_total))
    dq2, dk2, dv2 = backward_of(probs2, keys2, values2, queries2, grads2, dot)
    dq3, dk3, dv3 = backward_of(probs3, keys3, values3, queries3, grads3, narrow(dot))
    query_ref[...] = dq2 + widen(dq3, 0.0)
    for index, (near, far) in enumerate(((dk2, dk3), (dv2, dv3))):
        own_ref[index] = join(near[:MID], far[:128])
        send_one_ref[index] = join(near[MID:], far[128:256]).astype(BF)
        send_two_ref[index] = far[256:384].astype(BF)
        send_three_ref[index] = far[384:].astype(BF)


def back_kernel(x_ref, stat_ref, comb_ref, mid_stat_ref, mid_comb_ref, mid_query_ref,
                out_ref, mid_grad_ref, kt, stat, dq, dk, dv):
    offset = head_offset()
    kt[...] = flip(x_ref[0])
    stat[...] = stat_ref[...]
    stat[:, LOW : LOW + MID] = mid_stat_ref[...]
    dq[...] = jnp.zeros_like(dq)
    dk[...] = jnp.zeros_like(dk)
    dv[...] = jnp.zeros_like(dv)

    def body(step, carry):
        start, first = segment_start(step)
        keys, values = x_ref[0, pl.ds(start, SEG)], x_ref[1, pl.ds(start, SEG)]
        queries, grads = x_ref[2, pl.ds(first, 256)], x_ref[3, pl.ds(first, 256)]
        cut = pl.ds(first, 256)
        probs = jnp.exp2(nt(keys, queries) * RATE - stat[0:1, cut])
        score_grad = (probs * (nt(values, grads) - stat[1:2, cut])).astype(BF)
        dq[:, cut] += nn(kt[:, pl.ds(start, SEG)], score_grad)
        dk[pl.ds(start, SEG)] += nn(score_grad, queries)
        dv[pl.ds(start, SEG)] += nn(probs.astype(BF), grads)
        return carry

    lax.fori_loop(0, 6, body, 0)
    mid_grad_ref[0] = dk[LOW : LOW + MID] * SCALE
    mid_grad_ref[1] = dv[LOW : LOW + MID]
    query = dq[...] * SCALE
    query = jnp.concatenate(
        [query[:, :LOW], query[:, LOW : LOW + MID] + mid_query_ref[...], query[:, LOW + MID :]], axis=1
    ).astype(BF)
    comb = jnp.concatenate(
        [comb_ref[:, :LOW], mid_comb_ref[...], comb_ref[:, LOW + MID :]], axis=1
    )
    both = jnp.concatenate([comb, query], axis=0)
    for half in range(2):
        rows = slice(half * 16, half * 16 + 16)
        plain = nt(unordering(offset, half, 0, SEG), both[:, half * SEG : half * SEG + SEG]).astype(BF)
        out_ref[rows, 0] = plain[:, :HEAD_DIM].reshape(16, ROWS, HEAD_DIM)
        out_ref[rows, 1] = plain[:, HEAD_DIM:].reshape(16, ROWS, HEAD_DIM)
        outer = slice(0, LOW) if half == 0 else slice(LOW + MID, TOKENS)
        pair = jnp.concatenate([dk[outer] * SCALE, dv[outer]], axis=1).astype(BF)
        plain = nn(unordering(offset, half, 0 if half == 0 else 128, LOW), pair).astype(BF)
        out_ref[rows, 2] = plain[:, :HEAD_DIM].reshape(16, ROWS, HEAD_DIM)
        out_ref[rows, 3] = plain[:, HEAD_DIM:].reshape(16, ROWS, HEAD_DIM)


def finish_kernel(in_ref, mid_grad_ref, own_ref, one_ref, two_ref, three_ref, out_ref):
    offset = head_offset()
    grads = []
    for index in range(2):
        near = mid_grad_ref[index] + own_ref[index] + one_ref[index].astype(F32)
        far = two_ref[index].astype(F32) + three_ref[index].astype(F32)
        grads.append(join(near, far).astype(BF))
    pair = jnp.concatenate(grads, axis=1)
    for half in range(2):
        rows = slice(half * 16, half * 16 + 16)
        cut = slice(half * 128, half * 128 + 128)
        plain = nn(unordering(offset, half, LOW if half == 0 else 0, 128), pair[cut]).astype(BF)
        for index in range(2):
            part = plain[:, index * HEAD_DIM : (index + 1) * HEAD_DIM].reshape(16, ROWS, HEAD_DIM)
            out_ref[rows, index] = in_ref[rows, index] + part


def shape(dims, kind):
    return jax.ShapeDtypeStruct(dims, kind)


PARAMS = pltpu.CompilerParams(vmem_limit_bytes=32 * 1024 * 1024)


def whole(array):
    return pl.BlockSpec(array.shape, lambda: (0,) * len(array.shape))


def call(kernel, outs, args, scratch=(), flops=0):
    return pl.pallas_call(
        kernel,
        out_shape=outs,
        scratch_shapes=list(scratch),
        compiler_params=PARAMS,
        cost_estimate=pl.CostEstimate(flops=flops, bytes_accessed=2 << 20, transcendentals=0),
    )(*args)


def pack(arrays):
    step = 8
    return pl.pallas_call(
        pack_kernel,
        grid=(PLANE // step,),
        in_specs=[pl.BlockSpec((ROWS, step * HEAD_DIM), lambda i: (0, i))] * 4,
        out_specs=pl.BlockSpec((step, 4, ROWS, HEAD_DIM), lambda i: (i, 0, 0, 0)),
        out_shape=shape((PLANE, 4, ROWS, HEAD_DIM), BF),
        compiler_params=PARAMS,
    )(*arrays)


def unpack(packed):
    step = 8
    return pl.pallas_call(
        unpack_kernel,
        grid=(PLANE // step,),
        in_specs=[pl.BlockSpec((step, 4, ROWS, HEAD_DIM), lambda i: (i, 0, 0, 0))],
        out_specs=[pl.BlockSpec((ROWS, step * HEAD_DIM), lambda i: (0, i))] * 4,
        out_shape=[shape((ROWS, PLANE * HEAD_DIM), BF)] * 4,
        compiler_params=PARAMS,
    )(packed)


def plane_exchange(packed):
    return lax.all_to_all(packed, "plane", split_axis=0, concat_axis=0, tiled=True)


def z_exchange(block, apart):
    count = lax.axis_size("zed")
    return lax.ppermute(block, "zed", [(at, at ^ apart) for at in range(count)])


def per_device(query_rows, key_rows, value_rows, grad_rows):
    got = plane_exchange(pack([key_rows, value_rows, query_rows, grad_rows]))
    half_block = pl.BlockSpec((PLANE, 2, ROWS, HEAD_DIM), lambda i: (0, 0, 0, 0))
    near = pl.pallas_call(
        select_kernel,
        grid=(1,),
        in_specs=[half_block],
        out_specs=pl.BlockSpec((2, MID, HEAD_DIM), lambda i: (0, 0, 0)),
        out_shape=shape((2, MID, HEAD_DIM), BF),
        compiler_params=PARAMS,
    )(got)
    inner = near[:, 64:192]
    one = z_exchange(near, 1)
    two = z_exchange(inner, 2)
    three = z_exchange(inner, 3)
    ordered, mid, stat, comb, mid_stat, mid_acc = call(
        local_kernel,
        [
            shape((4, TOKENS, HEAD_DIM), BF),
            shape((4, MID, HEAD_DIM), BF),
            shape((2, TOKENS), F32),
            shape((HEAD_DIM, TOKENS), BF),
            shape((2, MID), F32),
            shape((HEAD_DIM, MID), F32),
        ],
        [got],
        [
            pltpu.VMEM((HEAD_DIM, TOKENS), BF),
            pltpu.VMEM((1, TOKENS), F32),
            pltpu.VMEM((1, TOKENS), F32),
            pltpu.VMEM((HEAD_DIM, TOKENS), F32),
        ],
        flops=3 * 4 * SEG * SEG * HEAD_DIM,
    )
    mid_out_stat, mid_comb, mid_query, own, send_one, send_two, send_three = call(
        far_kernel,
        [
            shape((2, MID), F32),
            shape((HEAD_DIM, MID), BF),
            shape((HEAD_DIM, MID), F32),
            shape((2, MID, HEAD_DIM), F32),
            shape((2, MID, HEAD_DIM), BF),
            shape((2, 128, HEAD_DIM), BF),
            shape((2, 128, HEAD_DIM), BF),
        ],
        [mid, mid_stat, mid_acc, one, two, three],
        flops=3 * 4 * SEG * SEG * HEAD_DIM,
    )
    back_one = z_exchange(send_one, 1)
    back_two = z_exchange(send_two, 2)
    back_three = z_exchange(send_three, 3)
    packed, mid_grad = call(
        back_kernel,
        [shape((PLANE, 4, ROWS, HEAD_DIM), BF), shape((2, MID, HEAD_DIM), F32)],
        [ordered, stat, comb, mid_out_stat, mid_comb, mid_query],
        [
            pltpu.VMEM((HEAD_DIM, TOKENS), BF),
            pltpu.VMEM((2, TOKENS), F32),
            pltpu.VMEM((HEAD_DIM, TOKENS), F32),
            pltpu.VMEM((TOKENS, HEAD_DIM), F32),
            pltpu.VMEM((TOKENS, HEAD_DIM), F32),
        ],
        flops=3 * 10 * SEG * SEG * HEAD_DIM,
    )
    upper_half = pl.BlockSpec((PLANE, 2, ROWS, HEAD_DIM), lambda i: (0, 1, 0, 0))
    mid_block = pl.BlockSpec((2, MID, HEAD_DIM), lambda i: (0, 0, 0))
    inner_block = pl.BlockSpec((2, 128, HEAD_DIM), lambda i: (0, 0, 0))
    packed = pl.pallas_call(
        finish_kernel,
        grid=(1,),
        in_specs=[upper_half, mid_block, mid_block, mid_block, inner_block, inner_block],
        out_specs=upper_half,
        out_shape=shape((PLANE, 4, ROWS, HEAD_DIM), BF),
        input_output_aliases={0: 0},
        compiler_params=PARAMS,
    )(packed, mid_grad, own, back_one, back_two, back_three)
    return tuple(unpack(plane_exchange(packed)))


def solution(mesh):
    planes = Mesh(mesh.devices.reshape(-1, PLANE), ("zed", "plane"))
    spec = P(("zed", "plane"), None)
    return jax.shard_map(
        per_device, mesh=planes, in_specs=(spec,) * 4, out_specs=(spec,) * 4, check_vma=False
    )
```

profile of v0, /device:TPU:1, one launch (start us, length us, event | category | flops | bytes accessed | tf_op | source)
XLA Modules:
  0.0 76.1 jit_solution(12723175593952827268)
XLA Ops:
  0.6 0.0 copy-start
  0.6 0.9 %copy-done = bf16[32,4096]{1,0:T(8,128)(2,1)S(1)} copy-done((bf16[32,4096]{1,0:T(8,128)(2,1)S(1)}, bf16[32,4096]{1,0:T(8,128)(2,1)}, u32[]{:S(2)}) %copy-start) | copy-done | bytes 262168
  1.6 0.0 copy-start.1
  1.6 0.9 %copy-done.1 = bf16[32,4096]{1,0:T(8,128)(2,1)S(1)} copy-done((bf16[32,4096]{1,0:T(8,128)(2,1)S(1)}, bf16[32,4096]{1,0:T(8,128)(2,1)}, u32[]{:S(2)}) %copy-start.1) | copy-done | bytes 262168
  2.5 0.0 copy-start.2
  2.5 0.9 %copy-done.2 = bf16[32,4096]{1,0:T(8,128)(2,1)S(1)} copy-done((bf16[32,4096]{1,0:T(8,128)(2,1)S(1)}, bf16[32,4096]{1,0:T(8,128)(2,1)}, u32[]{:S(2)}) %copy-start.2) | copy-done | bytes 262168
  3.5 0.0 copy-start.3
  3.5 0.9 %copy-done.3 = bf16[32,4096]{1,0:T(8,128)(2,1)S(1)} copy-done((bf16[32,4096]{1,0:T(8,128)(2,1)S(1)}, bf16[32,4096]{1,0:T(8,128)(2,1)}, u32[]{:S(2)}) %copy-start.3) | copy-done | bytes 262168
  4.4 0.4 shard_map.75
  4.8 24.9 %all_to_all.10.got_ref = bf16[32,4,32,128]{3,2,1,0:T(8,128)(2,1)S(1)} all-to-all(bf16[32,4,32,128]{3,2,1,0:T(8,128)(2,1)S(1)} %shard_map.75), channel_id=1, replica_groups=mesh['seq'=32,'head'=8] {'seq':(8)4,'head'}, dimensions={0} | all-to-all | bytes 2097152 | tf_op jit(solution)/shard_map/all_to_all | solution.py:326
  29.7 0.3 shard_map.77
  30.0 1.7 %collective-permute-start = (bf16[2,256,128]{2,1,0:T(8,128)(2,1)S(1)}, bf16[2,256,128]{2,1,0:T(8,128)(2,1)S(1)}, u32[]{:S(2)}, u32[]{:S(2)}) collective-permute-start(bf16[2,256,128]{2,1,0:T(8,128)(2,1)S(1)} %shard_map.77), channel_id=1, source_target_pairs={{0,32},{32,0},{64,96},{96,64},{128,160},{160,128},{192,224},{224,1... | collective-permute-start | bytes 393224 | tf_op jit(solution)/shard_map/ppermute | solution.py:331
  31.7 2.8 %collective-permute-start.2 = (bf16[2,128,128]{2,1,0:T(8,128)(2,1)S(1)}, bf16[2,128,128]{2,1,0:T(8,128)(2,1)S(1)}, u32[]{:S(2)}, u32[]{:S(2)}) collective-permute-start(bf16[2,128,128]{2,1,0:T(8,128)(2,1)S(1)} %slice.4), channel_id=1, source_target_pairs={{0,96},{32,64},{64,32},{96,0},{128,224},{160,192},{192,160},{224,1... | collective-permute-start | bytes 196616 | tf_op jit(solution)/shard_map/ppermute | solution.py:331
  34.5 0.3 collective-permute-start.1
  34.8 4.3 %shard_map.76 = (bf16[4,1024,128]{2,1,0:T(8,128)(2,1)S(1)}, bf16[4,256,128]{2,1,0:T(8,128)(2,1)S(1)}, f32[2,1024]{1,0:T(2,128)S(1)}, bf16[128,1024]{1,0:T(8,128)...) custom-call(bf16[32,4,32,128]{3,2,1,0:T(8,128)(2,1)S(1)} %all_to_all.10.got_ref), custom_call_target="tpu_custom_call" | custom-call | flops 402653184 | bytes 2097152 | tf_op jit(solution)/shard_map/pallas_call | solution.py:292
  39.1 0.0 collective-permute-done.2.three_ref
  39.1 2.6 %collective-permute-done.1.two_ref = bf16[2,128,128]{2,1,0:T(8,128)(2,1)S(1)} collective-permute-done((bf16[2,128,128]{2,1,0:T(8,128)(2,1)S(1)}, bf16[2,128,128]{2,1,0:T(8,128)(2,1)S(1)}, u32[]{:S(2)}, u32[]{:S(2)}) %collective-permute-start.1) | collective-permute-done | bytes 65568 | tf_op jit(solution)/shard_map/ppermute | solution.py:331
  41.7 0.0 collective-permute-done.one_ref
  41.7 1.6 %shard_map.78 = (f32[2,256]{1,0:T(2,128)S(1)}, bf16[128,256]{1,0:T(8,128)(2,1)S(1)}, f32[128,256]{1,0:T(8,128)S(1)}, f32[2,256,128]{2,1,0:T(8,128)S(1)}, bf16[2,...) custom-call(bf16[4,256,128]{2,1,0:T(8,128)(2,1)S(1)} %get-tuple-element.22.mid_ref, ...), custom_call_target="tpu_custom_call" | custom-call | flops 402653184 | bytes 2097152 | tf_op jit(solution)/shard_map/pallas_call | solution.py:292
  43.3 0.1 collective-permute-start.3
  43.4 0.9 %collective-permute-start.4 = (bf16[2,128,128]{2,1,0:T(8,128)(2,1)S(1)}, bf16[2,128,128]{2,1,0:T(8,128)(2,1)S(1)}, u32[]{:S(2)}, u32[]{:S(2)}) collective-permute-start(bf16[2,128,128]{2,1,0:T(8,128)(2,1)S(1)} %get-tuple-element.32), channel_id=1, source_target_pairs={{0,64},{32,96},{64,0},{96,32},{128,192},{160,224},{192,128},{224,1... | collective-permute-start | bytes 196616 | tf_op jit(solution)/shard_map/ppermute | solution.py:331
  44.3 2.6 %collective-permute-start.5 = (bf16[2,128,128]{2,1,0:T(8,128)(2,1)S(1)}, bf16[2,128,128]{2,1,0:T(8,128)(2,1)S(1)}, u32[]{:S(2)}, u32[]{:S(2)}) collective-permute-start(bf16[2,128,128]{2,1,0:T(8,128)(2,1)S(1)} %get-tuple-element.33), channel_id=1, source_target_pairs={{0,96},{32,64},{64,32},{96,0},{128,224},{160,192},{192,160},{224,1... | collective-permute-start | bytes 196616 | tf_op jit(solution)/shard_map/ppermute | solution.py:331
  46.9 4.7 %shard_map.79 = (bf16[32,4,32,128]{3,2,1,0:T(8,128)(2,1)S(1)}, f32[2,256,128]{2,1,0:T(8,128)S(1)}) custom-call(bf16[4,1024,128]{2,1,0:T(8,128)(2,1)S(1)} %get-tuple-element.19.x_ref, f32[2,1024]{1,0:T(2,128)S(1)} %get-tuple-element.20.stat_ref, bf16[128,1024]{1,0:T(8,128)(2,1)S(1)} %get-tuple-element.21.comb_ref, ...), custom_call_target="tpu_custom_call" | custom-call | flops 1006632960 | bytes 2097152 | tf_op jit(solution)/shard_map/pallas_call | solution.py:292
  51.6 0.0 collective-permute-done.4.two_ref
  51.6 0.0 collective-permute-done.5.three_ref
  51.6 0.0 collective-permute-done.3.one_ref
  51.6 0.4 shard_map.80
  52.1 22.4 %all_to_all.11.in_ref = bf16[32,4,32,128]{3,2,1,0:T(8,128)(2,1)S(1)} all-to-all(bf16[32,4,32,128]{3,2,1,0:T(8,128)(2,1)S(1)} %shard_map.80), channel_id=1, replica_groups=mesh['seq'=32,'head'=8] {'seq':(8)4,'head'}, dimensions={0} | all-to-all | bytes 2097152 | tf_op jit(solution)/shard_map/all_to_all | solution.py:326
  74.5 1.6 %shard_map.81 = (bf16[32,4096]{1,0:T(8,128)(2,1)}, bf16[32,4096]{1,0:T(8,128)(2,1)}, bf16[32,4096]{1,0:T(8,128)(2,1)}, bf16[32,4096]{1,0:T(8,128)(2,1)}) custom-call(bf16[32,4,32,128]{3,2,1,0:T(8,128)(2,1)S(1)} %all_to_all.11.in_ref), custom_call_target="tpu_custom_call" | custom-call | tf_op jit(solution)/shard_map/pallas_call | solution.py:315
  (1 shorter events, 0.0 us)
Async XLA Ops:
  0.6 1.0 %copy-start = (bf16[32,4096]{1,0:T(8,128)(2,1)S(1)}, bf16[32,4096]{1,0:T(8,128)(2,1)}, u32[]{:S(2)}) copy-start(bf16[32,4096]{1,0:T(8,128)(2,1)} %key_ref.1) | copy-start | bytes 786436
  1.6 0.9 %copy-start.1 = (bf16[32,4096]{1,0:T(8,128)(2,1)S(1)}, bf16[32,4096]{1,0:T(8,128)(2,1)}, u32[]{:S(2)}) copy-start(bf16[32,4096]{1,0:T(8,128)(2,1)} %value_ref.1) | copy-start | bytes 786436
  2.5 0.9 %copy-start.2 = (bf16[32,4096]{1,0:T(8,128)(2,1)S(1)}, bf16[32,4096]{1,0:T(8,128)(2,1)}, u32[]{:S(2)}) copy-start(bf16[32,4096]{1,0:T(8,128)(2,1)} %query_ref.1) | copy-start | bytes 786436
  3.5 0.9 %copy-start.3 = (bf16[32,4096]{1,0:T(8,128)(2,1)S(1)}, bf16[32,4096]{1,0:T(8,128)(2,1)}, u32[]{:S(2)}) copy-start(bf16[32,4096]{1,0:T(8,128)(2,1)} %grad_ref.1) | copy-start | bytes 786436
  30.0 11.7 %collective-permute-start = (bf16[2,256,128]{2,1,0:T(8,128)(2,1)S(1)}, bf16[2,256,128]{2,1,0:T(8,128)(2,1)S(1)}, u32[]{:S(2)}, u32[]{:S(2)}) collective-permute-start(bf16[2,256,128]{2,1,0:T(8,128)(2,1)S(1)} %shard_map.77), channel_id=1, source_target_pairs={{0,32},{32,0},{64,96},{96,64},{128,160},{160,128},{192,224},{224,1... | collective-permute-start | bytes 393224 | tf_op jit(solution)/shard_map/ppermute | solution.py:331
  31.7 7.3 %collective-permute-start.2 = (bf16[2,128,128]{2,1,0:T(8,128)(2,1)S(1)}, bf16[2,128,128]{2,1,0:T(8,128)(2,1)S(1)}, u32[]{:S(2)}, u32[]{:S(2)}) collective-permute-start(bf16[2,128,128]{2,1,0:T(8,128)(2,1)S(1)} %slice.4), channel_id=1, source_target_pairs={{0,96},{32,64},{64,32},{96,0},{128,224},{160,192},{192,160},{224,1... | collective-permute-start | bytes 196616 | tf_op jit(solution)/shard_map/ppermute | solution.py:331
  34.5 7.1 %collective-permute-start.1 = (bf16[2,128,128]{2,1,0:T(8,128)(2,1)S(1)}, bf16[2,128,128]{2,1,0:T(8,128)(2,1)S(1)}, u32[]{:S(2)}, u32[]{:S(2)}) collective-permute-start(bf16[2,128,128]{2,1,0:T(8,128)(2,1)S(1)} %slice.4), channel_id=1, source_target_pairs={{0,64},{32,96},{64,0},{96,32},{128,192},{160,224},{192,128},{224,1... | collective-permute-start | bytes 196616 | tf_op jit(solution)/shard_map/ppermute | solution.py:331
  43.3 8.4 %collective-permute-start.3 = (bf16[2,256,128]{2,1,0:T(8,128)(2,1)S(1)}, bf16[2,256,128]{2,1,0:T(8,128)(2,1)S(1)}, u32[]{:S(2)}, u32[]{:S(2)}) collective-permute-start(bf16[2,256,128]{2,1,0:T(8,128)(2,1)S(1)} %get-tuple-element.31), channel_id=1, source_target_pairs={{0,32},{32,0},{64,96},{96,64},{128,160},{160,128},{192,224},{224,1... | collective-permute-start | bytes 393224 | tf_op jit(solution)/shard_map/ppermute | solution.py:331
  43.4 8.2 %collective-permute-start.4 = (bf16[2,128,128]{2,1,0:T(8,128)(2,1)S(1)}, bf16[2,128,128]{2,1,0:T(8,128)(2,1)S(1)}, u32[]{:S(2)}, u32[]{:S(2)}) collective-permute-start(bf16[2,128,128]{2,1,0:T(8,128)(2,1)S(1)} %get-tuple-element.32), channel_id=1, source_target_pairs={{0,64},{32,96},{64,0},{96,32},{128,192},{160,224},{192,128},{224,1... | collective-permute-start | bytes 196616 | tf_op jit(solution)/shard_map/ppermute | solution.py:331
  44.3 7.3 %collective-permute-start.5 = (bf16[2,128,128]{2,1,0:T(8,128)(2,1)S(1)}, bf16[2,128,128]{2,1,0:T(8,128)(2,1)S(1)}, u32[]{:S(2)}, u32[]{:S(2)}) collective-permute-start(bf16[2,128,128]{2,1,0:T(8,128)(2,1)S(1)} %get-tuple-element.33), channel_id=1, source_target_pairs={{0,96},{32,64},{64,32},{96,0},{128,224},{160,192},{192,160},{224,1... | collective-permute-start | bytes 196616 | tf_op jit(solution)/shard_map/ppermute | solution.py:331
where the time goes:
time: 76.4 us; the launch traced here: 76.1 us
  blocking collectives  47.3 us (62%)
  Pallas kernels  13.2 us (17%)
  starting transfers between devices  8.44 us (11%)
  local copies, waits for them, and re-layouts  3.8 us (5%)
  waiting for transfers between devices  2.6 us (3%)
    all_to_all x2, blocking collectives, plane_exchange(): lax.all_to_all(packed, 'plane', split_axis=0, concat_axis=0, tiled=True)  47.3 us
    pallas_call x3, Pallas kernels, call(): pl.pallas_call(kernel, out_shape=outs, scratch_shapes=list(scratch), comp...  10.6 us
    ppermute x6, starting transfers between devices, z_exchange(): return lax.ppermute(block, 'zed', [(at, at ^ apart) for at in range(count)])  8.44 us
    unnamed x8, local copies, waits for them, and re-layouts  3.79 us
    ppermute x6, waiting for transfers between devices, z_exchange(): return lax.ppermute(block, 'zed', [(at, at ^ apart) for at in range(count)])  2.6 us
    pallas_call x1, Pallas kernels, unpack(): pl.pallas_call(unpack_kernel, grid=(PLANE // step,), in_specs=[pl.BlockSp...  1.59 us
  transfers between devices with their start and end apart: 6, of which 1 were waited for; matrix products, arithmetic and copies ran while one was open for 0% of the time, Pallas kernels for 12%

commit v1 on v0

--- a/solution.py
+++ b/solution.py
@@ -67,22 +67,28 @@
     return lax.axis_index("plane") & 7
 
 
-def pack_kernel(key_ref, value_ref, query_ref, grad_ref, out_ref):
-    for index in range(out_ref.shape[0]):
-        cut = slice(index * HEAD_DIM, (index + 1) * HEAD_DIM)
-        out_ref[index, 0] = key_ref[:, cut]
-        out_ref[index, 1] = value_ref[:, cut]
-        out_ref[index, 2] = query_ref[:, cut]
-        out_ref[index, 3] = grad_ref[:, cut]
-
-
-def unpack_kernel(in_ref, att_ref, query_ref, key_ref, value_ref):
-    for index in range(in_ref.shape[0]):
-        cut = slice(index * HEAD_DIM, (index + 1) * HEAD_DIM)
-        att_ref[:, cut] = in_ref[index, 0]
-        query_ref[:, cut] = in_ref[index, 1]
-        key_ref[:, cut] = in_ref[index, 2]
-        value_ref[:, cut] = in_ref[index, 3]
+def pack_kernel(key_ref, value_ref, query_ref, grad_ref, out_ref, held, arrived):
+    copies = [
+        pltpu.make_async_copy(source, held.at[index], arrived.at[index])
+        for index, source in enumerate((key_ref, value_ref, query_ref, grad_ref))
+    ]
+    for copy in copies:
+        copy.start()
+    for index, copy in enumerate(copies):
+        copy.wait()
+        for head in range(PLANE):
+            out_ref[head, index] = held[index, :, head * HEAD_DIM : (head + 1) * HEAD_DIM]
+
+
+def unpack_kernel(in_ref, att_ref, query_ref, key_ref, value_ref, held, sent):
+    copies = []
+    for index, target in enumerate((att_ref, query_ref, key_ref, value_ref)):
+        for head in range(PLANE):
+            held[index, :, head * HEAD_DIM : (head + 1) * HEAD_DIM] = in_ref[head, index]
+        copies.append(pltpu.make_async_copy(held.at[index], target, sent.at[index]))
+        copies[-1].start()
+    for copy in copies:
+        copy.wait()
 
 
 def select_kernel(got_ref, out_ref):
@@ -299,25 +305,27 @@
 
 
 def pack(arrays):
-    step = 8
     return pl.pallas_call(
         pack_kernel,
-        grid=(PLANE // step,),
-        in_specs=[pl.BlockSpec((ROWS, step * HEAD_DIM), lambda i: (0, i))] * 4,
-        out_specs=pl.BlockSpec((step, 4, ROWS, HEAD_DIM), lambda i: (i, 0, 0, 0)),
+        in_specs=[pl.BlockSpec(memory_space=pl.ANY)] * 4,
         out_shape=shape((PLANE, 4, ROWS, HEAD_DIM), BF),
+        scratch_shapes=[
+            pltpu.VMEM((4, ROWS, PLANE * HEAD_DIM), BF),
+            pltpu.SemaphoreType.DMA((4,)),
+        ],
         compiler_params=PARAMS,
-    )(*arrays)
+    )(*[pltpu.with_memory_space_constraint(array, pltpu.HBM) for array in arrays])
 
 
 def unpack(packed):
-    step = 8
     return pl.pallas_call(
         unpack_kernel,
-        grid=(PLANE // step,),
-        in_specs=[pl.BlockSpec((step, 4, ROWS, HEAD_DIM), lambda i: (i, 0, 0, 0))],
-        out_specs=[pl.BlockSpec((ROWS, step * HEAD_DIM), lambda i: (0, i))] * 4,
+        out_specs=[pl.BlockSpec(memory_space=pl.ANY)] * 4,
         out_shape=[shape((ROWS, PLANE * HEAD_DIM), BF)] * 4,
+        scratch_shapes=[
+            pltpu.VMEM((4, ROWS, PLANE * HEAD_DIM), BF),
+            pltpu.SemaphoreType.DMA((4,)),
+        ],
         compiler_params=PARAMS,
     )(packed)
 

time: 76.4 us -> 72.8 us (0.953)
  local copies, waits for them, and re-layouts: 3.8 us -> 0.01 us
    unnamed x8 -> x0, local copies, waits for them, and re-layouts: 3.79 us -> none
where the time goes in v1:
time: 72.8 us; the launch traced here: 72.6 us
  blocking collectives  47.3 us (65%)
  Pallas kernels  13.6 us (19%)
  starting transfers between devices  8.44 us (12%)
  waiting for transfers between devices  2.6 us (4%)
    all_to_all x2, blocking collectives, plane_exchange(): lax.all_to_all(packed, 'plane', split_axis=0, concat_axis=0, tiled=True)  47.3 us
    pallas_call x3, Pallas kernels, call(): pl.pallas_call(kernel, out_shape=outs, scratch_shapes=list(scratch), comp...  10.6 us
    ppermute x6, starting transfers between devices, z_exchange(): return lax.ppermute(block, 'zed', [(at, at ^ apart) for at in range(count)])  8.44 us
    ppermute x6, waiting for transfers between devices, z_exchange(): return lax.ppermute(block, 'zed', [(at, at ^ apart) for at in range(count)])  2.6 us
  transfers between devices with their start and end apart: 6, of which 1 were waited for; matrix products, arithmetic and copies ran while one was open for 0% of the time, Pallas kernels for 12%

profile of v1, /device:TPU:1, one launch (start us, length us, event | category | flops | bytes accessed | tf_op | source)
XLA Modules:
  0.0 72.6 jit_solution(4804396774490868159)
XLA Ops:
  0.6 1.3 %shard_map.75 = bf16[32,4,32,128]{3,2,1,0:T(8,128)(2,1)S(1)} custom-call(bf16[32,4096]{1,0:T(8,128)(2,1)} %key_ref.1, bf16[32,4096]{1,0:T(8,128)(2,1)} %value_ref.1, bf16[32,4096]{1,0:T(8,128)(2,1)} %query_ref.1, bf16[32,4096]{1,0:T(8,128)(2,1)} %grad_ref.1), custom_call_target="tpu_custom_call" | custom-call | tf_op jit(solution)/shard_map/pallas_call | solution.py:308
  1.9 24.9 %all_to_all.10.got_ref = bf16[32,4,32,128]{3,2,1,0:T(8,128)(2,1)S(1)} all-to-all(bf16[32,4,32,128]{3,2,1,0:T(8,128)(2,1)S(1)} %shard_map.75), channel_id=1, replica_groups=mesh['seq'=32,'head'=8] {'seq':(8)4,'head'}, dimensions={0} | all-to-all | bytes 2097152 | tf_op jit(solution)/shard_map/all_to_all | solution.py:334
  26.8 0.3 shard_map.77
  27.1 1.7 %collective-permute-start = (bf16[2,256,128]{2,1,0:T(8,128)(2,1)S(1)}, bf16[2,256,128]{2,1,0:T(8,128)(2,1)S(1)}, u32[]{:S(2)}, u32[]{:S(2)}) collective-permute-start(bf16[2,256,128]{2,1,0:T(8,128)(2,1)S(1)} %shard_map.77), channel_id=1, source_target_pairs={{0,32},{32,0},{64,96},{96,64},{128,160},{160,128},{192,224},{224,1... | collective-permute-start | bytes 393224 | tf_op jit(solution)/shard_map/ppermute | solution.py:339
  28.8 2.8 %collective-permute-start.2 = (bf16[2,128,128]{2,1,0:T(8,128)(2,1)S(1)}, bf16[2,128,128]{2,1,0:T(8,128)(2,1)S(1)}, u32[]{:S(2)}, u32[]{:S(2)}) collective-permute-start(bf16[2,128,128]{2,1,0:T(8,128)(2,1)S(1)} %slice.4), channel_id=1, source_target_pairs={{0,96},{32,64},{64,32},{96,0},{128,224},{160,192},{192,160},{224,1... | collective-permute-start | bytes 196616 | tf_op jit(solution)/shard_map/ppermute | solution.py:339
  31.6 0.3 collective-permute-start.1
  31.9 4.3 %shard_map.76 = (bf16[4,1024,128]{2,1,0:T(8,128)(2,1)S(1)}, bf16[4,256,128]{2,1,0:T(8,128)(2,1)S(1)}, f32[2,1024]{1,0:T(2,128)S(1)}, bf16[128,1024]{1,0:T(8,128)...) custom-call(bf16[32,4,32,128]{3,2,1,0:T(8,128)(2,1)S(1)} %all_to_all.10.got_ref), custom_call_target="tpu_custom_call" | custom-call | flops 402653184 | bytes 2097152 | tf_op jit(solution)/shard_map/pallas_call | solution.py:298
  36.2 0.0 collective-permute-done.2.three_ref
  36.2 2.6 %collective-permute-done.1.two_ref = bf16[2,128,128]{2,1,0:T(8,128)(2,1)S(1)} collective-permute-done((bf16[2,128,128]{2,1,0:T(8,128)(2,1)S(1)}, bf16[2,128,128]{2,1,0:T(8,128)(2,1)S(1)}, u32[]{:S(2)}, u32[]{:S(2)}) %collective-permute-start.1) | collective-permute-done | bytes 65568 | tf_op jit(solution)/shard_map/ppermute | solution.py:339
  38.8 0.0 collective-permute-done.one_ref
  38.8 1.6 %shard_map.78 = (f32[2,256]{1,0:T(2,128)S(1)}, bf16[128,256]{1,0:T(8,128)(2,1)S(1)}, f32[128,256]{1,0:T(8,128)S(1)}, f32[2,256,128]{2,1,0:T(8,128)S(1)}, bf16[2,...) custom-call(bf16[4,256,128]{2,1,0:T(8,128)(2,1)S(1)} %get-tuple-element.22.mid_ref, ...), custom_call_target="tpu_custom_call" | custom-call | flops 402653184 | bytes 2097152 | tf_op jit(solution)/shard_map/pallas_call | solution.py:298
  40.4 0.1 collective-permute-start.3
  40.5 0.9 %collective-permute-start.4 = (bf16[2,128,128]{2,1,0:T(8,128)(2,1)S(1)}, bf16[2,128,128]{2,1,0:T(8,128)(2,1)S(1)}, u32[]{:S(2)}, u32[]{:S(2)}) collective-permute-start(bf16[2,128,128]{2,1,0:T(8,128)(2,1)S(1)} %get-tuple-element.32), channel_id=1, source_target_pairs={{0,64},{32,96},{64,0},{96,32},{128,192},{160,224},{192,128},{224,1... | collective-permute-start | bytes 196616 | tf_op jit(solution)/shard_map/ppermute | solution.py:339
  41.4 2.6 %collective-permute-start.5 = (bf16[2,128,128]{2,1,0:T(8,128)(2,1)S(1)}, bf16[2,128,128]{2,1,0:T(8,128)(2,1)S(1)}, u32[]{:S(2)}, u32[]{:S(2)}) collective-permute-start(bf16[2,128,128]{2,1,0:T(8,128)(2,1)S(1)} %get-tuple-element.33), channel_id=1, source_target_pairs={{0,96},{32,64},{64,32},{96,0},{128,224},{160,192},{192,160},{224,1... | collective-permute-start | bytes 196616 | tf_op jit(solution)/shard_map/ppermute | solution.py:339
  44.0 4.7 %shard_map.79 = (bf16[32,4,32,128]{3,2,1,0:T(8,128)(2,1)S(1)}, f32[2,256,128]{2,1,0:T(8,128)S(1)}) custom-call(bf16[4,1024,128]{2,1,0:T(8,128)(2,1)S(1)} %get-tuple-element.19.x_ref, f32[2,1024]{1,0:T(2,128)S(1)} %get-tuple-element.20.stat_ref, bf16[128,1024]{1,0:T(8,128)(2,1)S(1)} %get-tuple-element.21.comb_ref, ...), custom_call_target="tpu_custom_call" | custom-call | flops 1006632960 | bytes 2097152 | tf_op jit(solution)/shard_map/pallas_call | solution.py:298
  48.7 0.0 collective-permute-done.4.two_ref
  48.7 0.0 collective-permute-done.5.three_ref
  48.7 0.0 collective-permute-done.3.one_ref
  48.7 0.4 shard_map.80
  49.2 22.4 %all_to_all.11.in_ref = bf16[32,4,32,128]{3,2,1,0:T(8,128)(2,1)S(1)} all-to-all(bf16[32,4,32,128]{3,2,1,0:T(8,128)(2,1)S(1)} %shard_map.80), channel_id=1, replica_groups=mesh['seq'=32,'head'=8] {'seq':(8)4,'head'}, dimensions={0} | all-to-all | bytes 2097152 | tf_op jit(solution)/shard_map/all_to_all | solution.py:334
  71.6 1.0 %shard_map.81 = (bf16[32,4096]{1,0:T(8,128)(2,1)}, bf16[32,4096]{1,0:T(8,128)(2,1)}, bf16[32,4096]{1,0:T(8,128)(2,1)}, bf16[32,4096]{1,0:T(8,128)(2,1)}) custom-call(bf16[32,4,32,128]{3,2,1,0:T(8,128)(2,1)S(1)} %all_to_all.11.in_ref), custom_call_target="tpu_custom_call" | custom-call | tf_op jit(solution)/shard_map/pallas_call | solution.py:321
  (1 shorter events, 0.0 us)
Async XLA Ops:
  27.1 11.7 %collective-permute-start = (bf16[2,256,128]{2,1,0:T(8,128)(2,1)S(1)}, bf16[2,256,128]{2,1,0:T(8,128)(2,1)S(1)}, u32[]{:S(2)}, u32[]{:S(2)}) collective-permute-start(bf16[2,256,128]{2,1,0:T(8,128)(2,1)S(1)} %shard_map.77), channel_id=1, source_target_pairs={{0,32},{32,0},{64,96},{96,64},{128,160},{160,128},{192,224},{224,1... | collective-permute-start | bytes 393224 | tf_op jit(solution)/shard_map/ppermute | solution.py:339
  28.8 7.3 %collective-permute-start.2 = (bf16[2,128,128]{2,1,0:T(8,128)(2,1)S(1)}, bf16[2,128,128]{2,1,0:T(8,128)(2,1)S(1)}, u32[]{:S(2)}, u32[]{:S(2)}) collective-permute-start(bf16[2,128,128]{2,1,0:T(8,128)(2,1)S(1)} %slice.4), channel_id=1, source_target_pairs={{0,96},{32,64},{64,32},{96,0},{128,224},{160,192},{192,160},{224,1... | collective-permute-start | bytes 196616 | tf_op jit(solution)/shard_map/ppermute | solution.py:339
  31.6 7.1 %collective-permute-start.1 = (bf16[2,128,128]{2,1,0:T(8,128)(2,1)S(1)}, bf16[2,128,128]{2,1,0:T(8,128)(2,1)S(1)}, u32[]{:S(2)}, u32[]{:S(2)}) collective-permute-start(bf16[2,128,128]{2,1,0:T(8,128)(2,1)S(1)} %slice.4), channel_id=1, source_target_pairs={{0,64},{32,96},{64,0},{96,32},{128,192},{160,224},{192,128},{224,1... | collective-permute-start | bytes 196616 | tf_op jit(solution)/shard_map/ppermute | solution.py:339
  40.4 8.4 %collective-permute-start.3 = (bf16[2,256,128]{2,1,0:T(8,128)(2,1)S(1)}, bf16[2,256,128]{2,1,0:T(8,128)(2,1)S(1)}, u32[]{:S(2)}, u32[]{:S(2)}) collective-permute-start(bf16[2,256,128]{2,1,0:T(8,128)(2,1)S(1)} %get-tuple-element.31), channel_id=1, source_target_pairs={{0,32},{32,0},{64,96},{96,64},{128,160},{160,128},{192,224},{224,1... | collective-permute-start | bytes 393224 | tf_op jit(solution)/shard_map/ppermute | solution.py:339
  40.5 8.2 %collective-permute-start.4 = (bf16[2,128,128]{2,1,0:T(8,128)(2,1)S(1)}, bf16[2,128,128]{2,1,0:T(8,128)(2,1)S(1)}, u32[]{:S(2)}, u32[]{:S(2)}) collective-permute-start(bf16[2,128,128]{2,1,0:T(8,128)(2,1)S(1)} %get-tuple-element.32), channel_id=1, source_target_pairs={{0,64},{32,96},{64,0},{96,32},{128,192},{160,224},{192,128},{224,1... | collective-permute-start | bytes 196616 | tf_op jit(solution)/shard_map/ppermute | solution.py:339
  41.4 7.3 %collective-permute-start.5 = (bf16[2,128,128]{2,1,0:T(8,128)(2,1)S(1)}, bf16[2,128,128]{2,1,0:T(8,128)(2,1)S(1)}, u32[]{:S(2)}, u32[]{:S(2)}) collective-permute-start(bf16[2,128,128]{2,1,0:T(8,128)(2,1)S(1)} %get-tuple-element.33), channel_id=1, source_target_pairs={{0,96},{32,64},{64,32},{96,0},{128,224},{160,192},{192,160},{224,1... | collective-permute-start | bytes 196616 | tf_op jit(solution)/shard_map/ppermute | solution.py:339

commit v2 on v1

--- a/solution.py
+++ b/solution.py
@@ -19,6 +19,15 @@
 NEG = -1e30
 BF = jnp.bfloat16
 F32 = jnp.float32
+
+ORDER = [
+    y_lo * 16 + core * 8 + y_hi * 4 + x
+    for x in range(4)
+    for y_lo in range(2)
+    for y_hi in range(2)
+    for core in range(2)
+]
+PLACE = [ORDER.index(device) for device in range(PLANE)]
 
 
 def nn(a, b):
@@ -64,7 +73,16 @@
 
 
 def head_offset():
-    return lax.axis_index("plane") & 7
+    return lax.axis_index("y_hi") * 4 + lax.axis_index("x")
+
+
+def half_of(ref, half, index):
+    return jnp.concatenate([ref[PLACE[block], index] for block in range(half * 16, half * 16 + 16)], axis=0)
+
+
+def put_half(ref, half, index, value):
+    for block in range(16):
+        ref[PLACE[half * 16 + block], index] = value[block * ROWS : block * ROWS + ROWS]
 
 
 def pack_kernel(key_ref, value_ref, query_ref, grad_ref, out_ref, held, arrived):
@@ -77,14 +95,14 @@
     for index, copy in enumerate(copies):
         copy.wait()
         for head in range(PLANE):
-            out_ref[head, index] = held[index, :, head * HEAD_DIM : (head + 1) * HEAD_DIM]
+            out_ref[PLACE[head], index] = held[index, :, head * HEAD_DIM : (head + 1) * HEAD_DIM]
 
 
 def unpack_kernel(in_ref, att_ref, query_ref, key_ref, value_ref, held, sent):
     copies = []
     for index, target in enumerate((att_ref, query_ref, key_ref, value_ref)):
         for head in range(PLANE):
-            held[index, :, head * HEAD_DIM : (head + 1) * HEAD_DIM] = in_ref[head, index]
+            held[index, :, head * HEAD_DIM : (head + 1) * HEAD_DIM] = in_ref[PLACE[head], index]
         copies.append(pltpu.make_async_copy(held.at[index], target, sent.at[index]))
         copies[-1].start()
     for copy in copies:
@@ -94,11 +112,7 @@
 def select_kernel(got_ref, out_ref):
     offset = head_offset()
     for half in range(2):
-        rows = slice(half * 16, half * 16 + 16)
-        pair = jnp.concatenate(
-            [got_ref[rows, 0].reshape(SEG, HEAD_DIM), got_ref[rows, 1].reshape(SEG, HEAD_DIM)],
-            axis=1,
-        )
+        pair = jnp.concatenate([half_of(got_ref, half, 0), half_of(got_ref, half, 1)], axis=1)
         picked = nn(ordering(offset, half, LOW if half == 0 else 0, 128), pair).astype(BF)
         out_ref[0, half * 128 : half * 128 + 128] = picked[:, :HEAD_DIM]
         out_ref[1, half * 128 : half * 128 + 128] = picked[:, HEAD_DIM:]
@@ -117,24 +131,36 @@
     return best, left * total + right * total_new, left * acc + right * acc_new
 
 
-def local_kernel(got_ref, x_ref, mid_ref, stat_ref, comb_ref, mid_stat_ref, mid_acc_ref, vt, peak, total, acc):
+def first_kernel(got_ref, x_ref, mid_ref, vt_ref, state_ref, acc_ref):
     offset = head_offset()
     for half in range(2):
-        rows = slice(half * 16, half * 16 + 16)
-        four = jnp.concatenate(
-            [got_ref[rows, index].reshape(SEG, HEAD_DIM) for index in range(4)], axis=1
-        )
+        four = jnp.concatenate([half_of(got_ref, half, index) for index in range(4)], axis=1)
         ordered = nn(ordering(offset, half, 0, SEG), four).astype(BF)
         for index in range(4):
             x_ref[index, half * SEG : half * SEG + SEG] = ordered[
                 :, index * HEAD_DIM : (index + 1) * HEAD_DIM
             ]
-        vt[:, half * SEG : half * SEG + SEG] = flip(ordered[:, HEAD_DIM : 2 * HEAD_DIM])
+        vt_ref[:, half * SEG : half * SEG + SEG] = flip(ordered[:, HEAD_DIM : 2 * HEAD_DIM])
     for index in range(4):
         mid_ref[index] = x_ref[index, LOW : LOW + MID]
-    peak[...] = jnp.full_like(peak, NEG)
-    total[...] = jnp.zeros_like(total)
-    acc[...] = jnp.zeros_like(acc)
+
+    def body(step, carry):
+        start, first = segment_start(step)
+        scores = nt(x_ref[0, pl.ds(start, SEG)], x_ref[2, pl.ds(first, 256)])
+        peak = jnp.max(scores, axis=0, keepdims=True)
+        weights = jnp.exp2((scores - peak) * RATE)
+        cut = pl.ds(first, 256)
+        state_ref[0:1, cut] = peak
+        state_ref[1:2, cut] = jnp.sum(weights, axis=0, keepdims=True)
+        acc_ref[:, cut] = nn(vt_ref[:, pl.ds(start, SEG)], weights.astype(BF))
+        return carry
+
+    lax.fori_loop(0, 4, body, 0, unroll=4)
+
+
+def second_kernel(x_ref, vt_ref, state_in, acc_in, stat_ref, comb_ref, mid_stat_ref, mid_acc_ref, state, acc):
+    state[...] = state_in[...]
+    acc[...] = acc_in[...]
 
     def body(step, carry):
         start, first = segment_start(step)
@@ -142,24 +168,28 @@
         top = jnp.max(scores, axis=0, keepdims=True)
         weights = jnp.exp2((scores - top) * RATE)
         cut = pl.ds(first, 256)
-        peak[:, cut], total[:, cut], acc[:, cut] = merge(
-            peak[:, cut],
-            total[:, cut],
+        state[0:1, cut], state[1:2, cut], acc[:, cut] = merge(
+            state[0:1, cut],
+            state[1:2, cut],
             acc[:, cut],
             top,
             jnp.sum(weights, axis=0, keepdims=True),
-            nn(vt[:, pl.ds(start, SEG)], weights.astype(BF)),
+            nn(vt_ref[:, pl.ds(start, SEG)], weights.astype(BF)),
         )
         return carry
 
-    lax.fori_loop(0, 6, body, 0)
-    mid_stat_ref[0:1] = peak[:, LOW : LOW + MID]
-    mid_stat_ref[1:2] = total[:, LOW : LOW + MID]
-    mid_acc_ref[...] = acc[:, LOW : LOW + MID]
-    combined = acc[...] / total[...]
+    lax.fori_loop(4, 6, body, 0, unroll=2)
+    combined = acc[...] / state[1:2]
     comb_ref[...] = combined.astype(BF)
-    stat_ref[0:1] = peak[...] * RATE + jnp.log2(total[...])
+    stat_ref[0:1] = state[0:1] * RATE + jnp.log2(state[1:2])
     stat_ref[1:2] = jnp.sum(flip(x_ref[3]).astype(F32) * combined, axis=0, keepdims=True)
+    middle = slice(LOW, LOW + MID)
+    near = (state[0:1, middle], state[1:2, middle], acc[:, middle])
+    near = merge(*near, *forward_of(x_ref[0, middle], vt_ref[:, middle], x_ref[2, middle]))
+    inner = slice(LOW + 64, LOW + 192)
+    peak, total, summed = forward_of(x_ref[0, inner], flip(x_ref[1, inner]), x_ref[2, inner])
+    near = merge(*near, widen(peak, NEG), widen(total, 0.0), widen(summed, 0.0))
+    mid_stat_ref[0:1], mid_stat_ref[1:2], mid_acc_ref[...] = near
 
 
 def widen(part, filler):
@@ -170,19 +200,23 @@
     return pltpu.roll(whole, MID - 64, 1)[:, :128]
 
 
-def forward_of(keys, values, queries):
+def forward_of(keys, values_flipped, queries):
     scores = nt(keys, queries)
     peak = jnp.max(scores, axis=0, keepdims=True)
     weights = jnp.exp2((scores - peak) * RATE)
-    total = jnp.sum(weights, axis=0, keepdims=True)
-    return peak, weights, total, nn(flip(values), weights.astype(BF))
-
-
-def backward_of(probs, keys, values, queries, grads, dot):
+    return (
+        peak,
+        jnp.sum(weights, axis=0, keepdims=True),
+        nn(values_flipped, weights.astype(BF)),
+    )
+
+
+def backward_of(keys, values, queries, grads, log_total, dot):
+    probs = jnp.exp2(nt(keys, queries) * RATE - log_total)
     score_grad = (probs * (nt(values, grads) - dot)).astype(BF)
     return (
-        nn(flip(keys), score_grad) * SCALE,
-        nn(score_grad, queries) * SCALE,
+        nn(flip(keys), score_grad),
+        nn(score_grad, queries),
         nn(probs.astype(BF), grads),
     )
 
@@ -191,34 +225,40 @@
     return jnp.concatenate([whole[:64], whole[64:192] + part, whole[192:]], axis=0)
 
 
+def forward_kernel(mid_ref, stat_ref, acc_ref, two_ref, three_ref, out_stat_ref, out_acc_ref):
+    keys = jnp.concatenate([two_ref[0], three_ref[0]], axis=0)
+    values = jnp.concatenate([two_ref[1], three_ref[1]], axis=0)
+    peak, total, summed = forward_of(keys, flip(values), mid_ref[2, 64:192])
+    out_stat_ref[0:1], out_stat_ref[1:2], out_acc_ref[...] = merge(
+        stat_ref[0:1], stat_ref[1:2], acc_ref[...],
+        widen(peak, NEG), widen(total, 0.0), widen(summed, 0.0),
+    )
+
+
 def far_kernel(mid_ref, stat_ref, acc_ref, one_ref, two_ref, three_ref,
-               out_stat_ref, comb_ref, query_ref, own_ref, send_one_ref, send_two_ref, send_three_ref):
-    keys2 = jnp.concatenate([mid_ref[0], one_ref[0]], axis=0)
-    values2 = jnp.concatenate([mid_ref[1], one_ref[1]], axis=0)
-    keys3 = jnp.concatenate([mid_ref[0, 64:192], one_ref[0, 64:192], two_ref[0], three_ref[0]], axis=0)
-    values3 = jnp.concatenate([mid_ref[1, 64:192], one_ref[1, 64:192], two_ref[1], three_ref[1]], axis=0)
-    queries2, grads2 = mid_ref[2], mid_ref[3]
+               out_stat_ref, comb_ref, query_ref, send_one_ref, send_two_ref, send_three_ref):
+    keys3 = jnp.concatenate([one_ref[0, 64:192], two_ref[0], three_ref[0]], axis=0)
+    values3 = jnp.concatenate([one_ref[1, 64:192], two_ref[1], three_ref[1]], axis=0)
+    grads2 = mid_ref[3]
     queries3, grads3 = mid_ref[2, 64:192], mid_ref[3, 64:192]
-    peak2, weights2, total2, acc2 = forward_of(keys2, values2, queries2)
-    peak3, weights3, total3, acc3 = forward_of(keys3, values3, queries3)
-    state = merge(stat_ref[0:1], stat_ref[1:2], acc_ref[...], peak2, total2, acc2)
-    peak, total, acc = merge(*state, widen(peak3, NEG), widen(total3, 0.0), widen(acc3, 0.0))
+    state = (stat_ref[0:1], stat_ref[1:2], acc_ref[...])
+    flipped = flip(one_ref[1])
+    state = merge(*state, *forward_of(one_ref[0], flipped, mid_ref[2]))
+    peak, total, summed = forward_of(one_ref[0, 64:192], flip(one_ref[1, 64:192]), queries3)
+    peak, total, acc = merge(*state, widen(peak, NEG), widen(total, 0.0), widen(summed, 0.0))
     combined = acc / total
     log_total = peak * RATE + jnp.log2(total)
     dot = jnp.sum(flip(grads2).astype(F32) * combined, axis=0, keepdims=True)
     out_stat_ref[0:1] = log_total
     out_stat_ref[1:2] = dot
     comb_ref[...] = combined.astype(BF)
-    probs2 = weights2 * jnp.exp2(peak2 * RATE - log_total)
-    probs3 = weights3 * jnp.exp2(peak3 * RATE - narrow(log_total))
-    dq2, dk2, dv2 = backward_of(probs2, keys2, values2, queries2, grads2, dot)
-    dq3, dk3, dv3 = backward_of(probs3, keys3, values3, queries3, grads3, narrow(dot))
+    dq2, dk2, dv2 = backward_of(one_ref[0], one_ref[1], mid_ref[2], grads2, log_total, dot)
+    dq3, dk3, dv3 = backward_of(keys3, values3, queries3, grads3, narrow(log_total), narrow(dot))
     query_ref[...] = dq2 + widen(dq3, 0.0)
-    for index, (near, far) in enumerate(((dk2, dk3), (dv2, dv3))):
-        own_ref[index] = join(near[:MID], far[:128])
-        send_one_ref[index] = join(near[MID:], far[128:256]).astype(BF)
-        send_two_ref[index] = far[256:384].astype(BF)
-        send_three_ref[index] = far[384:].astype(BF)
+    for index, (near, far, scale) in enumerate(((dk2, dk3, SCALE), (dv2, dv3, 1.0))):
+        send_one_ref[index] = (join(near, far[:128]) * scale).astype(BF)
+        send_two_ref[index] = (far[128:256] * scale).astype(BF)
+        send_three_ref[index] = (far[256:] * scale).astype(BF)
 
 
 def back_kernel(x_ref, stat_ref, comb_ref, mid_stat_ref, mid_comb_ref, mid_query_ref,
@@ -243,44 +283,51 @@
         dv[pl.ds(start, SEG)] += nn(probs.astype(BF), grads)
         return carry
 
-    lax.fori_loop(0, 6, body, 0)
+    lax.fori_loop(0, 6, body, 0, unroll=6)
+    for first, last in ((LOW, LOW + MID), (LOW + 64, LOW + 192)):
+        cut = slice(first, last)
+        log_total, dot = stat[0:1, LOW : LOW + MID], stat[1:2, LOW : LOW + MID]
+        if last - first < MID:
+            log_total, dot = narrow(log_total), narrow(dot)
+        part, key_part, value_part = backward_of(
+            x_ref[0, cut], x_ref[1, cut], x_ref[2, cut], x_ref[3, cut], log_total, dot
+        )
+        dq[:, LOW : LOW + MID] += part if last - first == MID else widen(part, 0.0)
+        dk[cut] += key_part
+        dv[cut] += value_part
     mid_grad_ref[0] = dk[LOW : LOW + MID] * SCALE
     mid_grad_ref[1] = dv[LOW : LOW + MID]
-    query = dq[...] * SCALE
-    query = jnp.concatenate(
-        [query[:, :LOW], query[:, LOW : LOW + MID] + mid_query_ref[...], query[:, LOW + MID :]], axis=1
-    ).astype(BF)
+    dq[:, LOW : LOW + MID] += mid_query_ref[...]
+    query = (dq[...] * SCALE).astype(BF)
     comb = jnp.concatenate(
         [comb_ref[:, :LOW], mid_comb_ref[...], comb_ref[:, LOW + MID :]], axis=1
     )
     both = jnp.concatenate([comb, query], axis=0)
     for half in range(2):
-        rows = slice(half * 16, half * 16 + 16)
         plain = nt(unordering(offset, half, 0, SEG), both[:, half * SEG : half * SEG + SEG]).astype(BF)
-        out_ref[rows, 0] = plain[:, :HEAD_DIM].reshape(16, ROWS, HEAD_DIM)
-        out_ref[rows, 1] = plain[:, HEAD_DIM:].reshape(16, ROWS, HEAD_DIM)
+        put_half(out_ref, half, 0, plain[:, :HEAD_DIM])
+        put_half(out_ref, half, 1, plain[:, HEAD_DIM:])
         outer = slice(0, LOW) if half == 0 else slice(LOW + MID, TOKENS)
         pair = jnp.concatenate([dk[outer] * SCALE, dv[outer]], axis=1).astype(BF)
         plain = nn(unordering(offset, half, 0 if half == 0 else 128, LOW), pair).astype(BF)
-        out_ref[rows, 2] = plain[:, :HEAD_DIM].reshape(16, ROWS, HEAD_DIM)
-        out_ref[rows, 3] = plain[:, HEAD_DIM:].reshape(16, ROWS, HEAD_DIM)
-
-
-def finish_kernel(in_ref, mid_grad_ref, own_ref, one_ref, two_ref, three_ref, out_ref):
+        put_half(out_ref, half, 2, plain[:, :HEAD_DIM])
+        put_half(out_ref, half, 3, plain[:, HEAD_DIM:])
+
+
+def finish_kernel(in_ref, mid_grad_ref, one_ref, two_ref, three_ref, out_ref):
     offset = head_offset()
     grads = []
     for index in range(2):
-        near = mid_grad_ref[index] + own_ref[index] + one_ref[index].astype(F32)
+        near = mid_grad_ref[index] + one_ref[index].astype(F32)
         far = two_ref[index].astype(F32) + three_ref[index].astype(F32)
         grads.append(join(near, far).astype(BF))
     pair = jnp.concatenate(grads, axis=1)
     for half in range(2):
-        rows = slice(half * 16, half * 16 + 16)
         cut = slice(half * 128, half * 128 + 128)
         plain = nn(unordering(offset, half, LOW if half == 0 else 0, 128), pair[cut]).astype(BF)
         for index in range(2):
-            part = plain[:, index * HEAD_DIM : (index + 1) * HEAD_DIM].reshape(16, ROWS, HEAD_DIM)
-            out_ref[rows, index] = in_ref[rows, index] + part
+            part = plain[:, index * HEAD_DIM : (index + 1) * HEAD_DIM]
+            put_half(out_ref, half, index, half_of(in_ref, half, index) + part)
 
 
 def shape(dims, kind):
@@ -331,7 +378,7 @@
 
 
 def plane_exchange(packed):
-    return lax.all_to_all(packed, "plane", split_axis=0, concat_axis=0, tiled=True)
+    return lax.all_to_all(packed, ("x", "y_lo", "y_hi", "core"), split_axis=0, concat_axis=0, tiled=True)
 
 
 def z_exchange(block, apart):
@@ -354,38 +401,48 @@
     one = z_exchange(near, 1)
     two = z_exchange(inner, 2)
     three = z_exchange(inner, 3)
-    ordered, mid, stat, comb, mid_stat, mid_acc = call(
-        local_kernel,
+    ordered, mid, vt, state, acc = call(
+        first_kernel,
         [
             shape((4, TOKENS, HEAD_DIM), BF),
             shape((4, MID, HEAD_DIM), BF),
+            shape((HEAD_DIM, TOKENS), BF),
+            shape((2, TOKENS), F32),
+            shape((HEAD_DIM, TOKENS), F32),
+        ],
+        [got],
+        flops=2 * 4 * SEG * SEG * HEAD_DIM,
+    )
+    stat, comb, mid_stat, mid_acc = call(
+        second_kernel,
+        [
             shape((2, TOKENS), F32),
             shape((HEAD_DIM, TOKENS), BF),
             shape((2, MID), F32),
             shape((HEAD_DIM, MID), F32),
         ],
-        [got],
-        [
-            pltpu.VMEM((HEAD_DIM, TOKENS), BF),
-            pltpu.VMEM((1, TOKENS), F32),
-            pltpu.VMEM((1, TOKENS), F32),
-            pltpu.VMEM((HEAD_DIM, TOKENS), F32),
-        ],
-        flops=3 * 4 * SEG * SEG * HEAD_DIM,
-    )
-    mid_out_stat, mid_comb, mid_query, own, send_one, send_two, send_three = call(
+        [ordered, vt, state, acc],
+        [pltpu.VMEM((2, TOKENS), F32), pltpu.VMEM((HEAD_DIM, TOKENS), F32)],
+        flops=4 * SEG * SEG * HEAD_DIM,
+    )
+    mid_stat, mid_acc = call(
+        forward_kernel,
+        [shape((2, MID), F32), shape((HEAD_DIM, MID), F32)],
+        [mid, mid_stat, mid_acc, two, three],
+        flops=8 * 4 * SEG * SEG * HEAD_DIM,
+    )
+    mid_out_stat, mid_comb, mid_query, send_one, send_two, send_three = call(
         far_kernel,
         [
             shape((2, MID), F32),
             shape((HEAD_DIM, MID), BF),
             shape((HEAD_DIM, MID), F32),
-            shape((2, MID, HEAD_DIM), F32),
             shape((2, MID, HEAD_DIM), BF),
             shape((2, 128, HEAD_DIM), BF),
             shape((2, 128, HEAD_DIM), BF),
         ],
         [mid, mid_stat, mid_acc, one, two, three],
-        flops=3 * 4 * SEG * SEG * HEAD_DIM,
+        flops=2 * 4 * SEG * SEG * HEAD_DIM,
     )
     back_one = z_exchange(send_one, 1)
     back_two = z_exchange(send_two, 2)
@@ -409,18 +466,19 @@
     packed = pl.pallas_call(
         finish_kernel,
         grid=(1,),
-        in_specs=[upper_half, mid_block, mid_block, mid_block, inner_block, inner_block],
+        in_specs=[upper_half, mid_block, mid_block, inner_block, inner_block],
         out_specs=upper_half,
         out_shape=shape((PLANE, 4, ROWS, HEAD_DIM), BF),
         input_output_aliases={0: 0},
         compiler_params=PARAMS,
-    )(packed, mid_grad, own, back_one, back_two, back_three)
+    )(packed, mid_grad, back_one, back_two, back_three)
     return tuple(unpack(plane_exchange(packed)))
 
 
 def solution(mesh):
-    planes = Mesh(mesh.devices.reshape(-1, PLANE), ("zed", "plane"))
-    spec = P(("zed", "plane"), None)
+    axes = ("zed", "y_lo", "core", "y_hi", "x")
+    planes = Mesh(mesh.devices.reshape(-1, 2, 2, 2, 4), axes)
+    spec = P(axes, None)
     return jax.shard_map(
         per_device, mesh=planes, in_specs=(spec,) * 4, out_specs=(spec,) * 4, check_vma=False
     )

time: 72.8 us -> 72 us (0.989)
  Pallas kernels: 13.6 us -> 12.5 us
    pallas_call x3 -> x5, Pallas kernels: 10.6 us -> 9.52 us  [call(): pl.pallas_call(kernel, out_shape=outs, scratch_shapes=list(scratch), comp...]
  transfers between devices with their start and end apart: 6 -> 6, of which waited for: 1 -> 3; matrix products, arithmetic and copies ran while one was open for 0% -> 0% of each run, Pallas kernels for 12% -> 11%
where the time goes in v2:
time: 72 us; the launch traced here: 71.9 us
  blocking collectives  47.2 us (66%)
  Pallas kernels  12.5 us (17%)
  starting transfers between devices  8.66 us (12%)
  waiting for transfers between devices  2.78 us (4%)
  between operations  0.72 us (1%)
    all_to_all x2, blocking collectives, plane_exchange(): lax.all_to_all(packed, ('x', 'y_lo', 'y_hi', 'core'), split_axis=0, conca...  47.2 us
    pallas_call x5, Pallas kernels, call(): pl.pallas_call(kernel, out_shape=outs, scratch_shapes=list(scratch), comp...  9.52 us
    ppermute x6, starting transfers between devices, z_exchange(): return lax.ppermute(block, 'zed', [(at, at ^ apart) for at in range(count)])  8.66 us
    ppermute x6, waiting for transfers between devices, z_exchange(): return lax.ppermute(block, 'zed', [(at, at ^ apart) for at in range(count)])  2.78 us
  transfers between devices with their start and end apart: 6, of which 3 were waited for; matrix products, arithmetic and copies ran while one was open for 0% of the time, Pallas kernels for 11%

profile of v2, /device:TPU:1, one launch (start us, length us, event | category | flops | bytes accessed | tf_op | source)
XLA Modules:
  0.0 71.9 jit_solution(7752722767516695878)
XLA Ops:
  0.6 1.3 %shard_map.75 = bf16[32,4,32,128]{3,2,1,0:T(8,128)(2,1)S(1)} custom-call(bf16[32,4096]{1,0:T(8,128)(2,1)} %key_ref.1, bf16[32,4096]{1,0:T(8,128)(2,1)} %value_ref.1, bf16[32,4096]{1,0:T(8,128)(2,1)} %query_ref.1, bf16[32,4096]{1,0:T(8,128)(2,1)} %grad_ref.1), custom_call_target="tpu_custom_call" | custom-call | tf_op jit(solution)/shard_map/pallas_call | solution.py:355
  1.9 25.0 %all_to_all.10.got_ref = bf16[32,4,32,128]{3,2,1,0:T(8,128)(2,1)S(1)} all-to-all(bf16[32,4,32,128]{3,2,1,0:T(8,128)(2,1)S(1)} %shard_map.75), channel_id=1, replica_groups=mesh['zed'=8,'y_lo'=2,'core'=2,'y_hi'=2,'x'=4] {'x','y_lo','y_hi','core'}, dimensions={0} | all-to-all | bytes 2097152 | tf_op jit(solution)/shard_map/all_to_all | solution.py:381
  26.9 0.3 shard_map.78
  27.2 4.4 %collective-permute-start.1 = (bf16[2,128,128]{2,1,0:T(8,128)(2,1)S(1)}, bf16[2,128,128]{2,1,0:T(8,128)(2,1)S(1)}, u32[]{:S(2)}, u32[]{:S(2)}) collective-permute-start(bf16[2,128,128]{2,1,0:T(8,128)(2,1)S(1)} %slice.4), channel_id=1, source_target_pairs={{0,96},{32,64},{64,32},{96,0},{128,224},{160,192},{192,160},{224,1... | collective-permute-start | bytes 196616 | tf_op jit(solution)/shard_map/ppermute | solution.py:386
  31.6 0.0 collective-permute-start
  31.6 0.4 collective-permute-start.2
  32.0 2.4 %shard_map.76 = (bf16[4,1024,128]{2,1,0:T(8,128)(2,1)S(1)}, bf16[4,256,128]{2,1,0:T(8,128)(2,1)S(1)}, bf16[128,1024]{1,0:T(8,128)(2,1)S(1)}, f32[2,1024]{1,0:T(2,128)S(1)}, f32[128,1024]{1,0:T(8,128)S(1)}) custom-call(bf16[32,4,32,128]{3,2,1,0:T(8,128)(2,1)S(1)} %all_to_all.10.got_ref), custom_call_target="tpu_custom_call" | custom-call | flops 268435456 | bytes 2097152 | tf_op jit(solution)/shard_map/pallas_call | solution.py:345
  34.4 1.6 %shard_map.77 = (f32[2,1024]{1,0:T(2,128)S(1)}, bf16[128,1024]{1,0:T(8,128)(2,1)S(1)}, f32[2,256]{1,0:T(2,128)S(1)}, f32[128,256]{1,0:T(8,128)S(1)}) custom-call(bf16[4,1024,128]{2,1,0:T(8,128)(2,1)S(1)} %get-tuple-element.23.x_ref, bf16[128,1024]{1,0:T(8,128)(2,1)S(1)} %get-tuple-element.24.vt_ref, f32[2,1024]{1,0:T(2,128)S(1)} %get-tuple-element.25.state_in, ...), custom_call_target="tpu_custom_call" | custom-call | flops 134217728 | bytes 2097152 | tf_op jit(solution)/shard_map/pallas_call | solution.py:345
  36.0 0.0 collective-permute-done.1.three_ref
  36.0 0.9 %collective-permute-done.two_ref = bf16[2,128,128]{2,1,0:T(8,128)(2,1)S(1)} collective-permute-done((bf16[2,128,128]{2,1,0:T(8,128)(2,1)S(1)}, bf16[2,128,128]{2,1,0:T(8,128)(2,1)S(1)}, u32[]{:S(2)}, u32[]{:S(2)}) %collective-permute-start) | collective-permute-done | bytes 65568 | tf_op jit(solution)/shard_map/ppermute | solution.py:386
  36.9 0.4 shard_map.79
  37.4 0.6 collective-permute-done.2.one_ref
  38.0 1.3 %shard_map.80 = (f32[2,256]{1,0:T(2,128)S(1)}, bf16[128,256]{1,0:T(8,128)(2,1)S(1)}, f32[128,256]{1,0:T(8,128)S(1)}, bf16[2,256,128]{2,1,0:T(8,128)(2,1)S(1)}, b...) custom-call(bf16[4,256,128]{2,1,0:T(8,128)(2,1)S(1)} %get-tuple-element.29.mid_ref, ...), custom_call_target="tpu_custom_call" | custom-call | flops 268435456 | bytes 2097152 | tf_op jit(solution)/shard_map/pallas_call | solution.py:345
  39.3 1.7 %collective-permute-start.3 = (bf16[2,256,128]{2,1,0:T(8,128)(2,1)S(1)}, bf16[2,256,128]{2,1,0:T(8,128)(2,1)S(1)}, u32[]{:S(2)}, u32[]{:S(2)}) collective-permute-start(bf16[2,256,128]{2,1,0:T(8,128)(2,1)S(1)} %get-tuple-element.39), channel_id=1, source_target_pairs={{0,32},{32,0},{64,96},{96,64},{128,160},{160,128},{192,224},{224,1... | collective-permute-start | bytes 393224 | tf_op jit(solution)/shard_map/ppermute | solution.py:386
  40.9 1.6 %collective-permute-start.4 = (bf16[2,128,128]{2,1,0:T(8,128)(2,1)S(1)}, bf16[2,128,128]{2,1,0:T(8,128)(2,1)S(1)}, u32[]{:S(2)}, u32[]{:S(2)}) collective-permute-start(bf16[2,128,128]{2,1,0:T(8,128)(2,1)S(1)} %get-tuple-element.40), channel_id=1, source_target_pairs={{0,64},{32,96},{64,0},{96,32},{128,192},{160,224},{192,128},{224,1... | collective-permute-start | bytes 196616 | tf_op jit(solution)/shard_map/ppermute | solution.py:386
  42.5 0.6 collective-permute-start.5
  43.1 3.8 %shard_map.81 = (bf16[32,4,32,128]{3,2,1,0:T(8,128)(2,1)S(1)}, f32[2,256,128]{2,1,0:T(8,128)S(1)}) custom-call(bf16[4,1024,128]{2,1,0:T(8,128)(2,1)S(1)} %get-tuple-element.23.x_ref, f32[2,1024]{1,0:T(2,128)S(1)} %get-tuple-element.27.stat_ref, bf16[128,1024]{1,0:T(8,128)(2,1)S(1)} %get-tuple-element.28.comb_ref, ...), custom_call_target="tpu_custom_call" | custom-call | flops 1006632960 | bytes 2097152 | tf_op jit(solution)/shard_map/pallas_call | solution.py:345
  47.0 0.0 collective-permute-done.4.two_ref
  47.0 1.2 %collective-permute-done.5.three_ref = bf16[2,128,128]{2,1,0:T(8,128)(2,1)S(1)} collective-permute-done((bf16[2,128,128]{2,1,0:T(8,128)(2,1)S(1)}, bf16[2,128,128]{2,1,0:T(8,128)(2,1)S(1)}, u32[]{:S(2)}, u32[]{:S(2)}) %collective-permute-start.5) | collective-permute-done | bytes 65568 | tf_op jit(solution)/shard_map/ppermute | solution.py:386
  48.2 0.0 collective-permute-done.3.one_ref
  48.2 0.5 shard_map.82
  48.7 22.2 %all_to_all.11.in_ref = bf16[32,4,32,128]{3,2,1,0:T(8,128)(2,1)S(1)} all-to-all(bf16[32,4,32,128]{3,2,1,0:T(8,128)(2,1)S(1)} %shard_map.82), channel_id=1, replica_groups=mesh['zed'=8,'y_lo'=2,'core'=2,'y_hi'=2,'x'=4] {'x','y_lo','y_hi','core'}, dimensions={0} | all-to-all | bytes 2097152 | tf_op jit(solution)/shard_map/all_to_all | solution.py:381
  70.8 1.0 %shard_map.83 = (bf16[32,4096]{1,0:T(8,128)(2,1)}, bf16[32,4096]{1,0:T(8,128)(2,1)}, bf16[32,4096]{1,0:T(8,128)(2,1)}, bf16[32,4096]{1,0:T(8,128)(2,1)}) custom-call(bf16[32,4,32,128]{3,2,1,0:T(8,128)(2,1)S(1)} %all_to_all.11.in_ref), custom_call_target="tpu_custom_call" | custom-call | tf_op jit(solution)/shard_map/pallas_call | solution.py:368
  (1 shorter events, 0.0 us)
Async XLA Ops:
  27.2 8.8 %collective-permute-start.1 = (bf16[2,128,128]{2,1,0:T(8,128)(2,1)S(1)}, bf16[2,128,128]{2,1,0:T(8,128)(2,1)S(1)}, u32[]{:S(2)}, u32[]{:S(2)}) collective-permute-start(bf16[2,128,128]{2,1,0:T(8,128)(2,1)S(1)} %slice.4), channel_id=1, source_target_pairs={{0,96},{32,64},{64,32},{96,0},{128,224},{160,192},{192,160},{224,1... | collective-permute-start | bytes 196616 | tf_op jit(solution)/shard_map/ppermute | solution.py:386
  31.6 5.3 %collective-permute-start = (bf16[2,128,128]{2,1,0:T(8,128)(2,1)S(1)}, bf16[2,128,128]{2,1,0:T(8,128)(2,1)S(1)}, u32[]{:S(2)}, u32[]{:S(2)}) collective-permute-start(bf16[2,128,128]{2,1,0:T(8,128)(2,1)S(1)} %slice.4), channel_id=1, source_target_pairs={{0,64},{32,96},{64,0},{96,32},{128,192},{160,224},{192,128},{224,1... | collective-permute-start | bytes 196616 | tf_op jit(solution)/shard_map/ppermute | solution.py:386
  31.6 6.4 %collective-permute-start.2 = (bf16[2,256,128]{2,1,0:T(8,128)(2,1)S(1)}, bf16[2,256,128]{2,1,0:T(8,128)(2,1)S(1)}, u32[]{:S(2)}, u32[]{:S(2)}) collective-permute-start(bf16[2,256,128]{2,1,0:T(8,128)(2,1)S(1)} %shard_map.78), channel_id=1, source_target_pairs={{0,32},{32,0},{64,96},{96,64},{128,160},{160,128},{192,224},{224,1... | collective-permute-start | bytes 393224 | tf_op jit(solution)/shard_map/ppermute | solution.py:386
  39.3 8.9 %collective-permute-start.3 = (bf16[2,256,128]{2,1,0:T(8,128)(2,1)S(1)}, bf16[2,256,128]{2,1,0:T(8,128)(2,1)S(1)}, u32[]{:S(2)}, u32[]{:S(2)}) collective-permute-start(bf16[2,256,128]{2,1,0:T(8,128)(2,1)S(1)} %get-tuple-element.39), channel_id=1, source_target_pairs={{0,32},{32,0},{64,96},{96,64},{128,160},{160,128},{192,224},{224,1... | collective-permute-start | bytes 393224 | tf_op jit(solution)/shard_map/ppermute | solution.py:386
  40.9 6.0 %collective-permute-start.4 = (bf16[2,128,128]{2,1,0:T(8,128)(2,1)S(1)}, bf16[2,128,128]{2,1,0:T(8,128)(2,1)S(1)}, u32[]{:S(2)}, u32[]{:S(2)}) collective-permute-start(bf16[2,128,128]{2,1,0:T(8,128)(2,1)S(1)} %get-tuple-element.40), channel_id=1, source_target_pairs={{0,64},{32,96},{64,0},{96,32},{128,192},{160,224},{192,128},{224,1... | collective-permute-start | bytes 196616 | tf_op jit(solution)/shard_map/ppermute | solution.py:386
  42.5 5.7 %collective-permute-start.5 = (bf16[2,128,128]{2,1,0:T(8,128)(2,1)S(1)}, bf16[2,128,128]{2,1,0:T(8,128)(2,1)S(1)}, u32[]{:S(2)}, u32[]{:S(2)}) collective-permute-start(bf16[2,128,128]{2,1,0:T(8,128)(2,1)S(1)} %get-tuple-element.41), channel_id=1, source_target_pairs={{0,96},{32,64},{64,32},{96,0},{128,224},{160,192},{192,160},{224,1... | collective-permute-start | bytes 196616 | tf_op jit(solution)/shard_map/ppermute | solution.py:386

commit v3 on v2

--- a/solution.py
+++ b/solution.py
@@ -225,13 +225,12 @@
     return jnp.concatenate([whole[:64], whole[64:192] + part, whole[192:]], axis=0)
 
 
-def forward_kernel(mid_ref, stat_ref, acc_ref, two_ref, three_ref, out_stat_ref, out_acc_ref):
-    keys = jnp.concatenate([two_ref[0], three_ref[0]], axis=0)
-    values = jnp.concatenate([two_ref[1], three_ref[1]], axis=0)
-    peak, total, summed = forward_of(keys, flip(values), mid_ref[2, 64:192])
+def forward_kernel(mid_ref, stat_ref, acc_ref, one_ref, out_stat_ref, out_acc_ref):
+    state = (stat_ref[0:1], stat_ref[1:2], acc_ref[...])
+    state = merge(*state, *forward_of(one_ref[0], flip(one_ref[1]), mid_ref[2]))
+    peak, total, summed = forward_of(one_ref[0, 64:192], flip(one_ref[1, 64:192]), mid_ref[2, 64:192])
     out_stat_ref[0:1], out_stat_ref[1:2], out_acc_ref[...] = merge(
-        stat_ref[0:1], stat_ref[1:2], acc_ref[...],
-        widen(peak, NEG), widen(total, 0.0), widen(summed, 0.0),
+        *state, widen(peak, NEG), widen(total, 0.0), widen(summed, 0.0)
     )
 
 
@@ -242,9 +241,7 @@
     grads2 = mid_ref[3]
     queries3, grads3 = mid_ref[2, 64:192], mid_ref[3, 64:192]
     state = (stat_ref[0:1], stat_ref[1:2], acc_ref[...])
-    flipped = flip(one_ref[1])
-    state = merge(*state, *forward_of(one_ref[0], flipped, mid_ref[2]))
-    peak, total, summed = forward_of(one_ref[0, 64:192], flip(one_ref[1, 64:192]), queries3)
+    peak, total, summed = forward_of(keys3[128:], flip(values3[128:]), queries3)
     peak, total, acc = merge(*state, widen(peak, NEG), widen(total, 0.0), widen(summed, 0.0))
     combined = acc / total
     log_total = peak * RATE + jnp.log2(total)
@@ -428,7 +425,7 @@
     mid_stat, mid_acc = call(
         forward_kernel,
         [shape((2, MID), F32), shape((HEAD_DIM, MID), F32)],
-        [mid, mid_stat, mid_acc, two, three],
+        [mid, mid_stat, mid_acc, one],
         flops=8 * 4 * SEG * SEG * HEAD_DIM,
     )
     mid_out_stat, mid_comb, mid_query, send_one, send_two, send_three = call(

time: 72 us -> 71.5 us (level)
  transfers between devices with their start and end apart: 6 -> 6, of which waited for: 3 -> 2; matrix products, arithmetic and copies ran while one was open for 0% -> 0% of each run, Pallas kernels for 11% -> 12%
where the time goes in v3:
time: 71.5 us; the launch traced here: 71.4 us
  blocking collectives  47.2 us (66%)
  Pallas kernels  12.5 us (17%)
  starting transfers between devices  8.43 us (12%)
  waiting for transfers between devices  2.45 us (3%)
  between operations  0.74 us (1%)
    all_to_all x2, blocking collectives, plane_exchange(): lax.all_to_all(packed, ('x', 'y_lo', 'y_hi', 'core'), split_axis=0, conca...  47.2 us
    pallas_call x5, Pallas kernels, call(): pl.pallas_call(kernel, out_shape=outs, scratch_shapes=list(scratch), comp...  9.51 us
    ppermute x6, starting transfers between devices, z_exchange(): return lax.ppermute(block, 'zed', [(at, at ^ apart) for at in range(count)])  8.43 us
    ppermute x6, waiting for transfers between devices, z_exchange(): return lax.ppermute(block, 'zed', [(at, at ^ apart) for at in range(count)])  2.45 us
  transfers between devices with their start and end apart: 6, of which 2 were waited for; matrix products, arithmetic and copies ran while one was open for 0% of the time, Pallas kernels for 12%

profile of v3, /device:TPU:1, one launch (start us, length us, event | category | flops | bytes accessed | tf_op | source)
XLA Modules:
  0.0 71.4 jit_solution(6145584194402260072)
XLA Ops:
  0.6 1.3 %shard_map.75 = bf16[32,4,32,128]{3,2,1,0:T(8,128)(2,1)S(1)} custom-call(bf16[32,4096]{1,0:T(8,128)(2,1)} %key_ref.1, bf16[32,4096]{1,0:T(8,128)(2,1)} %value_ref.1, bf16[32,4096]{1,0:T(8,128)(2,1)} %query_ref.1, bf16[32,4096]{1,0:T(8,128)(2,1)} %grad_ref.1), custom_call_target="tpu_custom_call" | custom-call | tf_op jit(solution)/shard_map/pallas_call | solution.py:352
  1.9 25.0 %all_to_all.10.got_ref = bf16[32,4,32,128]{3,2,1,0:T(8,128)(2,1)S(1)} all-to-all(bf16[32,4,32,128]{3,2,1,0:T(8,128)(2,1)S(1)} %shard_map.75), channel_id=1, replica_groups=mesh['zed'=8,'y_lo'=2,'core'=2,'y_hi'=2,'x'=4] {'x','y_lo','y_hi','core'}, dimensions={0} | all-to-all | bytes 2097152 | tf_op jit(solution)/shard_map/all_to_all | solution.py:378
  26.9 0.3 shard_map.78
  27.2 1.7 %collective-permute-start = (bf16[2,256,128]{2,1,0:T(8,128)(2,1)S(1)}, bf16[2,256,128]{2,1,0:T(8,128)(2,1)S(1)}, u32[]{:S(2)}, u32[]{:S(2)}) collective-permute-start(bf16[2,256,128]{2,1,0:T(8,128)(2,1)S(1)} %shard_map.78), channel_id=1, source_target_pairs={{0,32},{32,0},{64,96},{96,64},{128,160},{160,128},{192,224},{224,1... | collective-permute-start | bytes 393224 | tf_op jit(solution)/shard_map/ppermute | solution.py:383
  28.9 2.8 %collective-permute-start.2 = (bf16[2,128,128]{2,1,0:T(8,128)(2,1)S(1)}, bf16[2,128,128]{2,1,0:T(8,128)(2,1)S(1)}, u32[]{:S(2)}, u32[]{:S(2)}) collective-permute-start(bf16[2,128,128]{2,1,0:T(8,128)(2,1)S(1)} %slice.4), channel_id=1, source_target_pairs={{0,96},{32,64},{64,32},{96,0},{128,224},{160,192},{192,160},{224,1... | collective-permute-start | bytes 196616 | tf_op jit(solution)/shard_map/ppermute | solution.py:383
  31.7 0.3 collective-permute-start.1
  32.0 2.4 %shard_map.76 = (bf16[4,1024,128]{2,1,0:T(8,128)(2,1)S(1)}, bf16[4,256,128]{2,1,0:T(8,128)(2,1)S(1)}, bf16[128,1024]{1,0:T(8,128)(2,1)S(1)}, f32[2,1024]{1,0:T(2,128)S(1)}, f32[128,1024]{1,0:T(8,128)S(1)}) custom-call(bf16[32,4,32,128]{3,2,1,0:T(8,128)(2,1)S(1)} %all_to_all.10.got_ref), custom_call_target="tpu_custom_call" | custom-call | flops 268435456 | bytes 2097152 | tf_op jit(solution)/shard_map/pallas_call | solution.py:342
  34.4 1.6 %shard_map.77 = (f32[2,1024]{1,0:T(2,128)S(1)}, bf16[128,1024]{1,0:T(8,128)(2,1)S(1)}, f32[2,256]{1,0:T(2,128)S(1)}, f32[128,256]{1,0:T(8,128)S(1)}) custom-call(bf16[4,1024,128]{2,1,0:T(8,128)(2,1)S(1)} %get-tuple-element.23.x_ref, bf16[128,1024]{1,0:T(8,128)(2,1)S(1)} %get-tuple-element.24.vt_ref, f32[2,1024]{1,0:T(2,128)S(1)} %get-tuple-element.25.state_in, ...), custom_call_target="tpu_custom_call" | custom-call | flops 134217728 | bytes 2097152 | tf_op jit(solution)/shard_map/pallas_call | solution.py:342
  36.0 0.0 collective-permute-done.one_ref
  36.0 0.7 shard_map.79
  36.7 0.1 collective-permute-done.2.three_ref
  36.8 2.4 %collective-permute-done.1.two_ref = bf16[2,128,128]{2,1,0:T(8,128)(2,1)S(1)} collective-permute-done((bf16[2,128,128]{2,1,0:T(8,128)(2,1)S(1)}, bf16[2,128,128]{2,1,0:T(8,128)(2,1)S(1)}, u32[]{:S(2)}, u32[]{:S(2)}) %collective-permute-start.1) | collective-permute-done | bytes 65568 | tf_op jit(solution)/shard_map/ppermute | solution.py:383
  39.1 1.0 %shard_map.80 = (f32[2,256]{1,0:T(2,128)S(1)}, bf16[128,256]{1,0:T(8,128)(2,1)S(1)}, f32[128,256]{1,0:T(8,128)S(1)}, bf16[2,256,128]{2,1,0:T(8,128)(2,1)S(1)}, b...) custom-call(bf16[4,256,128]{2,1,0:T(8,128)(2,1)S(1)} %get-tuple-element.29.mid_ref, ...), custom_call_target="tpu_custom_call" | custom-call | flops 268435456 | bytes 2097152 | tf_op jit(solution)/shard_map/pallas_call | solution.py:342
  40.1 0.1 collective-permute-start.3
  40.2 1.2 %collective-permute-start.4 = (bf16[2,128,128]{2,1,0:T(8,128)(2,1)S(1)}, bf16[2,128,128]{2,1,0:T(8,128)(2,1)S(1)}, u32[]{:S(2)}, u32[]{:S(2)}) collective-permute-start(bf16[2,128,128]{2,1,0:T(8,128)(2,1)S(1)} %get-tuple-element.40), channel_id=1, source_target_pairs={{0,64},{32,96},{64,0},{96,32},{128,192},{160,224},{192,128},{224,1... | collective-permute-start | bytes 196616 | tf_op jit(solution)/shard_map/ppermute | solution.py:383
  41.5 2.3 %collective-permute-start.5 = (bf16[2,128,128]{2,1,0:T(8,128)(2,1)S(1)}, bf16[2,128,128]{2,1,0:T(8,128)(2,1)S(1)}, u32[]{:S(2)}, u32[]{:S(2)}) collective-permute-start(bf16[2,128,128]{2,1,0:T(8,128)(2,1)S(1)} %get-tuple-element.41), channel_id=1, source_target_pairs={{0,96},{32,64},{64,32},{96,0},{128,224},{160,192},{192,160},{224,1... | collective-permute-start | bytes 196616 | tf_op jit(solution)/shard_map/ppermute | solution.py:383
  43.8 3.8 %shard_map.81 = (bf16[32,4,32,128]{3,2,1,0:T(8,128)(2,1)S(1)}, f32[2,256,128]{2,1,0:T(8,128)S(1)}) custom-call(bf16[4,1024,128]{2,1,0:T(8,128)(2,1)S(1)} %get-tuple-element.23.x_ref, f32[2,1024]{1,0:T(2,128)S(1)} %get-tuple-element.27.stat_ref, bf16[128,1024]{1,0:T(8,128)(2,1)S(1)} %get-tuple-element.28.comb_ref, ...), custom_call_target="tpu_custom_call" | custom-call | flops 1006632960 | bytes 2097152 | tf_op jit(solution)/shard_map/pallas_call | solution.py:342
  47.6 0.0 collective-permute-done.4.two_ref
  47.6 0.0 collective-permute-done.5.three_ref
  47.6 0.0 collective-permute-done.3.one_ref
  47.6 0.5 shard_map.82
  48.1 22.2 %all_to_all.11.in_ref = bf16[32,4,32,128]{3,2,1,0:T(8,128)(2,1)S(1)} all-to-all(bf16[32,4,32,128]{3,2,1,0:T(8,128)(2,1)S(1)} %shard_map.82), channel_id=1, replica_groups=mesh['zed'=8,'y_lo'=2,'core'=2,'y_hi'=2,'x'=4] {'x','y_lo','y_hi','core'}, dimensions={0} | all-to-all | bytes 2097152 | tf_op jit(solution)/shard_map/all_to_all | solution.py:378
  70.3 1.0 %shard_map.83 = (bf16[32,4096]{1,0:T(8,128)(2,1)}, bf16[32,4096]{1,0:T(8,128)(2,1)}, bf16[32,4096]{1,0:T(8,128)(2,1)}, bf16[32,4096]{1,0:T(8,128)(2,1)}) custom-call(bf16[32,4,32,128]{3,2,1,0:T(8,128)(2,1)S(1)} %all_to_all.11.in_ref), custom_call_target="tpu_custom_call" | custom-call | tf_op jit(solution)/shard_map/pallas_call | solution.py:365
  (1 shorter events, 0.0 us)
Async XLA Ops:
  27.2 8.8 %collective-permute-start = (bf16[2,256,128]{2,1,0:T(8,128)(2,1)S(1)}, bf16[2,256,128]{2,1,0:T(8,128)(2,1)S(1)}, u32[]{:S(2)}, u32[]{:S(2)}) collective-permute-start(bf16[2,256,128]{2,1,0:T(8,128)(2,1)S(1)} %shard_map.78), channel_id=1, source_target_pairs={{0,32},{32,0},{64,96},{96,64},{128,160},{160,128},{192,224},{224,1... | collective-permute-start | bytes 393224 | tf_op jit(solution)/shard_map/ppermute | solution.py:383
  28.9 7.9 %collective-permute-start.2 = (bf16[2,128,128]{2,1,0:T(8,128)(2,1)S(1)}, bf16[2,128,128]{2,1,0:T(8,128)(2,1)S(1)}, u32[]{:S(2)}, u32[]{:S(2)}) collective-permute-start(bf16[2,128,128]{2,1,0:T(8,128)(2,1)S(1)} %slice.4), channel_id=1, source_target_pairs={{0,96},{32,64},{64,32},{96,0},{128,224},{160,192},{192,160},{224,1... | collective-permute-start | bytes 196616 | tf_op jit(solution)/shard_map/ppermute | solution.py:383
  31.7 7.4 %collective-permute-start.1 = (bf16[2,128,128]{2,1,0:T(8,128)(2,1)S(1)}, bf16[2,128,128]{2,1,0:T(8,128)(2,1)S(1)}, u32[]{:S(2)}, u32[]{:S(2)}) collective-permute-start(bf16[2,128,128]{2,1,0:T(8,128)(2,1)S(1)} %slice.4), channel_id=1, source_target_pairs={{0,64},{32,96},{64,0},{96,32},{128,192},{160,224},{192,128},{224,1... | collective-permute-start | bytes 196616 | tf_op jit(solution)/shard_map/ppermute | solution.py:383
  40.1 7.5 %collective-permute-start.3 = (bf16[2,256,128]{2,1,0:T(8,128)(2,1)S(1)}, bf16[2,256,128]{2,1,0:T(8,128)(2,1)S(1)}, u32[]{:S(2)}, u32[]{:S(2)}) collective-permute-start(bf16[2,256,128]{2,1,0:T(8,128)(2,1)S(1)} %get-tuple-element.39), channel_id=1, source_target_pairs={{0,32},{32,0},{64,96},{96,64},{128,160},{160,128},{192,224},{224,1... | collective-permute-start | bytes 393224 | tf_op jit(solution)/shard_map/ppermute | solution.py:383
  40.2 7.4 %collective-permute-start.4 = (bf16[2,128,128]{2,1,0:T(8,128)(2,1)S(1)}, bf16[2,128,128]{2,1,0:T(8,128)(2,1)S(1)}, u32[]{:S(2)}, u32[]{:S(2)}) collective-permute-start(bf16[2,128,128]{2,1,0:T(8,128)(2,1)S(1)} %get-tuple-element.40), channel_id=1, source_target_pairs={{0,64},{32,96},{64,0},{96,32},{128,192},{160,224},{192,128},{224,1... | collective-permute-start | bytes 196616 | tf_op jit(solution)/shard_map/ppermute | solution.py:383
  41.5 6.2 %collective-permute-start.5 = (bf16[2,128,128]{2,1,0:T(8,128)(2,1)S(1)}, bf16[2,128,128]{2,1,0:T(8,128)(2,1)S(1)}, u32[]{:S(2)}, u32[]{:S(2)}) collective-permute-start(bf16[2,128,128]{2,1,0:T(8,128)(2,1)S(1)} %get-tuple-element.41), channel_id=1, source_target_pairs={{0,96},{32,64},{64,32},{96,0},{128,224},{160,192},{192,160},{224,1... | collective-permute-start | bytes 196616 | tf_op jit(solution)/shard_map/ppermute | solution.py:383

commit v4 on v3

--- a/solution.py
+++ b/solution.py
@@ -158,7 +158,7 @@
     lax.fori_loop(0, 4, body, 0, unroll=4)
 
 
-def second_kernel(x_ref, vt_ref, state_in, acc_in, stat_ref, comb_ref, mid_stat_ref, mid_acc_ref, state, acc):
+def second_kernel(x_ref, vt_ref, state_in, acc_in, stat_ref, comb_ref, mid_stat_ref, mid_acc_ref, flipped_ref, state, acc):
     state[...] = state_in[...]
     acc[...] = acc_in[...]
 
@@ -182,7 +182,9 @@
     combined = acc[...] / state[1:2]
     comb_ref[...] = combined.astype(BF)
     stat_ref[0:1] = state[0:1] * RATE + jnp.log2(state[1:2])
-    stat_ref[1:2] = jnp.sum(flip(x_ref[3]).astype(F32) * combined, axis=0, keepdims=True)
+    flipped = flip(x_ref[3])
+    flipped_ref[...] = flipped[:, LOW : LOW + MID]
+    stat_ref[1:2] = jnp.sum(flipped.astype(F32) * combined, axis=0, keepdims=True)
     middle = slice(LOW, LOW + MID)
     near = (state[0:1, middle], state[1:2, middle], acc[:, middle])
     near = merge(*near, *forward_of(x_ref[0, middle], vt_ref[:, middle], x_ref[2, middle]))
@@ -225,41 +227,55 @@
     return jnp.concatenate([whole[:64], whole[64:192] + part, whole[192:]], axis=0)
 
 
-def forward_kernel(mid_ref, stat_ref, acc_ref, one_ref, out_stat_ref, out_acc_ref):
+def forward_kernel(mid_ref, flipped_ref, stat_ref, acc_ref, one_ref, out_stat_ref, out_acc_ref):
     state = (stat_ref[0:1], stat_ref[1:2], acc_ref[...])
     state = merge(*state, *forward_of(one_ref[0], flip(one_ref[1]), mid_ref[2]))
     peak, total, summed = forward_of(one_ref[0, 64:192], flip(one_ref[1, 64:192]), mid_ref[2, 64:192])
-    out_stat_ref[0:1], out_stat_ref[1:2], out_acc_ref[...] = merge(
-        *state, widen(peak, NEG), widen(total, 0.0), widen(summed, 0.0)
-    )
+    peak, total, acc = merge(*state, widen(peak, NEG), widen(total, 0.0), widen(summed, 0.0))
+    out_stat_ref[0:1], out_stat_ref[1:2], out_acc_ref[...] = peak, total, acc
+    out_stat_ref[2:3] = jnp.sum(flipped_ref[...].astype(F32) * acc, axis=0, keepdims=True)
 
 
 def far_kernel(mid_ref, stat_ref, acc_ref, one_ref, two_ref, three_ref,
-               out_stat_ref, comb_ref, query_ref, send_one_ref, send_two_ref, send_three_ref):
-    keys3 = jnp.concatenate([one_ref[0, 64:192], two_ref[0], three_ref[0]], axis=0)
-    values3 = jnp.concatenate([one_ref[1, 64:192], two_ref[1], three_ref[1]], axis=0)
-    grads2 = mid_ref[3]
-    queries3, grads3 = mid_ref[2, 64:192], mid_ref[3, 64:192]
-    state = (stat_ref[0:1], stat_ref[1:2], acc_ref[...])
-    peak, total, summed = forward_of(keys3[128:], flip(values3[128:]), queries3)
-    peak, total, acc = merge(*state, widen(peak, NEG), widen(total, 0.0), widen(summed, 0.0))
-    combined = acc / total
-    log_total = peak * RATE + jnp.log2(total)
-    dot = jnp.sum(flip(grads2).astype(F32) * combined, axis=0, keepdims=True)
+               out_stat_ref, comb_ref, slope_ref, far_slope_ref, send_one_ref, send_two_ref, send_three_ref):
+    inner = slice(64, 192)
+    keys, values, queries, grads = one_ref[0], one_ref[1], mid_ref[2], mid_ref[3]
+    keys3 = jnp.concatenate([keys[inner], two_ref[0], three_ref[0]], axis=0)
+    values3 = jnp.concatenate([values[inner], two_ref[1], three_ref[1]], axis=0)
+    scores3, grads3 = nt(keys3, queries[inner]), nt(values3, grads[inner])
+    scores2, grads2 = nt(keys, queries), nt(values, grads)
+    new = scores3[128:]
+    peak3 = jnp.max(new, axis=0, keepdims=True)
+    weights3 = jnp.exp2((new - peak3) * RATE)
+    total3 = jnp.sum(weights3, axis=0, keepdims=True)
+    dot3 = jnp.sum(weights3 * grads3[128:], axis=0, keepdims=True)
+    summed3 = nn(flip(values3[128:]), weights3.astype(BF))
+    peak3 = widen(peak3, NEG)
+    best = jnp.maximum(stat_ref[0:1], peak3)
+    left = jnp.exp2((stat_ref[0:1] - best) * RATE)
+    right = jnp.exp2((peak3 - best) * RATE)
+    total = left * stat_ref[1:2] + right * widen(total3, 0.0)
+    dot = (left * stat_ref[2:3] + right * widen(dot3, 0.0)) / total
+    log_total = best * RATE + jnp.log2(total)
     out_stat_ref[0:1] = log_total
     out_stat_ref[1:2] = dot
-    comb_ref[...] = combined.astype(BF)
-    dq2, dk2, dv2 = backward_of(one_ref[0], one_ref[1], mid_ref[2], grads2, log_total, dot)
-    dq3, dk3, dv3 = backward_of(keys3, values3, queries3, grads3, narrow(log_total), narrow(dot))
-    query_ref[...] = dq2 + widen(dq3, 0.0)
+    probs3 = jnp.exp2(scores3 * RATE - narrow(log_total))
+    slopes3 = (probs3 * (grads3 - narrow(dot))).astype(BF)
+    probs2 = jnp.exp2(scores2 * RATE - log_total)
+    slopes2 = (probs2 * (grads2 - dot)).astype(BF)
+    dk3, dv3 = nn(slopes3, queries[inner]), nn(probs3.astype(BF), grads[inner])
+    dk2, dv2 = nn(slopes2, queries), nn(probs2.astype(BF), grads)
     for index, (near, far, scale) in enumerate(((dk2, dk3, SCALE), (dv2, dv3, 1.0))):
         send_one_ref[index] = (join(near, far[:128]) * scale).astype(BF)
         send_two_ref[index] = (far[128:256] * scale).astype(BF)
         send_three_ref[index] = (far[256:] * scale).astype(BF)
-
-
-def back_kernel(x_ref, stat_ref, comb_ref, mid_stat_ref, mid_comb_ref, mid_query_ref,
-                out_ref, mid_grad_ref, kt, stat, dq, dk, dv):
+    slope_ref[...] = slopes2
+    far_slope_ref[...] = slopes3
+    comb_ref[...] = ((left * acc_ref[...] + right * widen(summed3, 0.0)) / total).astype(BF)
+
+
+def back_kernel(x_ref, stat_ref, comb_ref, mid_stat_ref, mid_comb_ref, one_ref, two_ref, three_ref, slope_ref, far_slope_ref,
+                out_ref, mid_grad_ref, place_ref, kt, stat, dq, dk, dv):
     offset = head_offset()
     kt[...] = flip(x_ref[0])
     stat[...] = stat_ref[...]
@@ -294,7 +310,12 @@
         dv[cut] += value_part
     mid_grad_ref[0] = dk[LOW : LOW + MID] * SCALE
     mid_grad_ref[1] = dv[LOW : LOW + MID]
-    dq[:, LOW : LOW + MID] += mid_query_ref[...]
+    keys3 = jnp.concatenate([one_ref[0, 64:192], two_ref[0], three_ref[0]], axis=0)
+    dq[:, LOW : LOW + MID] += nn(flip(one_ref[0]), slope_ref[...]) + widen(
+        nn(flip(keys3), far_slope_ref[...]), 0.0
+    )
+    place_ref[0] = unordering(offset, 0, LOW, 128)
+    place_ref[1] = unordering(offset, 1, 0, 128)
     query = (dq[...] * SCALE).astype(BF)
     comb = jnp.concatenate(
         [comb_ref[:, :LOW], mid_comb_ref[...], comb_ref[:, LOW + MID :]], axis=1
@@ -311,8 +332,7 @@
         put_half(out_ref, half, 3, plain[:, HEAD_DIM:])
 
 
-def finish_kernel(in_ref, mid_grad_ref, one_ref, two_ref, three_ref, out_ref):
-    offset = head_offset()
+def finish_kernel(in_ref, mid_grad_ref, place_ref, one_ref, two_ref, three_ref, out_ref):
     grads = []
     for index in range(2):
         near = mid_grad_ref[index] + one_ref[index].astype(F32)
@@ -321,7 +341,7 @@
     pair = jnp.concatenate(grads, axis=1)
     for half in range(2):
         cut = slice(half * 128, half * 128 + 128)
-        plain = nn(unordering(offset, half, LOW if half == 0 else 0, 128), pair[cut]).astype(BF)
+        plain = nn(place_ref[half], pair[cut]).astype(BF)
         for index in range(2):
             part = plain[:, index * HEAD_DIM : (index + 1) * HEAD_DIM]
             put_half(out_ref, half, index, half_of(in_ref, half, index) + part)
@@ -410,13 +430,14 @@
         [got],
         flops=2 * 4 * SEG * SEG * HEAD_DIM,
     )
-    stat, comb, mid_stat, mid_acc = call(
+    stat, comb, mid_stat, mid_acc, flipped = call(
         second_kernel,
         [
             shape((2, TOKENS), F32),
             shape((HEAD_DIM, TOKENS), BF),
             shape((2, MID), F32),
             shape((HEAD_DIM, MID), F32),
+            shape((HEAD_DIM, MID), BF),
         ],
         [ordered, vt, state, acc],
         [pltpu.VMEM((2, TOKENS), F32), pltpu.VMEM((HEAD_DIM, TOKENS), F32)],
@@ -424,16 +445,17 @@
     )
     mid_stat, mid_acc = call(
         forward_kernel,
-        [shape((2, MID), F32), shape((HEAD_DIM, MID), F32)],
-        [mid, mid_stat, mid_acc, one],
+        [shape((3, MID), F32), shape((HEAD_DIM, MID), F32)],
+        [mid, flipped, mid_stat, mid_acc, one],
         flops=8 * 4 * SEG * SEG * HEAD_DIM,
     )
-    mid_out_stat, mid_comb, mid_query, send_one, send_two, send_three = call(
+    mid_out_stat, mid_comb, slope, far_slope, send_one, send_two, send_three = call(
         far_kernel,
         [
             shape((2, MID), F32),
             shape((HEAD_DIM, MID), BF),
-            shape((HEAD_DIM, MID), F32),
+            shape((MID, MID), BF),
+            shape((384, 128), BF),
             shape((2, MID, HEAD_DIM), BF),
             shape((2, 128, HEAD_DIM), BF),
             shape((2, 128, HEAD_DIM), BF),
@@ -444,10 +466,14 @@
     back_one = z_exchange(send_one, 1)
     back_two = z_exchange(send_two, 2)
     back_three = z_exchange(send_three, 3)
-    packed, mid_grad = call(
+    packed, mid_grad, place = call(
         back_kernel,
-        [shape((PLANE, 4, ROWS, HEAD_DIM), BF), shape((2, MID, HEAD_DIM), F32)],
-        [ordered, stat, comb, mid_out_stat, mid_comb, mid_query],
+        [
+            shape((PLANE, 4, ROWS, HEAD_DIM), BF),
+            shape((2, MID, HEAD_DIM), F32),
+            shape((2, SEG, 128), BF),
+        ],
+        [ordered, stat, comb, mid_out_stat, mid_comb, one, two, three, slope, far_slope],
         [
             pltpu.VMEM((HEAD_DIM, TOKENS), BF),
             pltpu.VMEM((2, TOKENS), F32),
@@ -459,16 +485,17 @@
     )
     upper_half = pl.BlockSpec((PLANE, 2, ROWS, HEAD_DIM), lambda i: (0, 1, 0, 0))
     mid_block = pl.BlockSpec((2, MID, HEAD_DIM), lambda i: (0, 0, 0))
+    place_block = pl.BlockSpec((2, SEG, 128), lambda i: (0, 0, 0))
     inner_block = pl.BlockSpec((2, 128, HEAD_DIM), lambda i: (0, 0, 0))
     packed = pl.pallas_call(
         finish_kernel,
         grid=(1,),
-        in_specs=[upper_half, mid_block, mid_block, inner_block, inner_block],
+        in_specs=[upper_half, mid_block, place_block, mid_block, inner_block, inner_block],
         out_specs=upper_half,
         out_shape=shape((PLANE, 4, ROWS, HEAD_DIM), BF),
         input_output_aliases={0: 0},
         compiler_params=PARAMS,
-    )(packed, mid_grad, back_one, back_two, back_three)
+    )(packed, mid_grad, place, back_one, back_two, back_three)
     return tuple(unpack(plane_exchange(packed)))
 
 

time: 71.5 us -> 71.3 us (level)
  transfers between devices with their start and end apart: 6 -> 6, of which waited for: 2 -> 1; matrix products, arithmetic and copies ran while one was open for 0% -> 0% of each run, Pallas kernels for 12% -> 12%
where the time goes in v4:
time: 71.3 us; the launch traced here: 71.1 us
  blocking collectives  47.2 us (66%)
  Pallas kernels  12.3 us (17%)
  starting transfers between devices  8.43 us (12%)
  waiting for transfers between devices  2.43 us (3%)
  between operations  0.73 us (1%)
    all_to_all x2, blocking collectives, plane_exchange(): lax.all_to_all(packed, ('x', 'y_lo', 'y_hi', 'core'), split_axis=0, conca...  47.2 us
    pallas_call x5, Pallas kernels, call(): pl.pallas_call(kernel, out_shape=outs, scratch_shapes=list(scratch), comp...  9.32 us
    ppermute x6, starting transfers between devices, z_exchange(): return lax.ppermute(block, 'zed', [(at, at ^ apart) for at in range(count)])  8.43 us
    ppermute x6, waiting for transfers between devices, z_exchange(): return lax.ppermute(block, 'zed', [(at, at ^ apart) for at in range(count)])  2.43 us
  transfers between devices with their start and end apart: 6, of which 1 were waited for; matrix products, arithmetic and copies ran while one was open for 0% of the time, Pallas kernels for 12%

profile of v4, /device:TPU:1, one launch (start us, length us, event | category | flops | bytes accessed | tf_op | source)
XLA Modules:
  0.0 71.1 jit_solution(12156799366580739796)
XLA Ops:
  0.6 1.3 %shard_map.75 = bf16[32,4,32,128]{3,2,1,0:T(8,128)(2,1)S(1)} custom-call(bf16[32,4096]{1,0:T(8,128)(2,1)} %key_ref.1, bf16[32,4096]{1,0:T(8,128)(2,1)} %value_ref.1, bf16[32,4096]{1,0:T(8,128)(2,1)} %query_ref.1, bf16[32,4096]{1,0:T(8,128)(2,1)} %grad_ref.1), custom_call_target="tpu_custom_call" | custom-call | tf_op jit(solution)/shard_map/pallas_call | solution.py:372
  1.9 25.0 %all_to_all.10.got_ref = bf16[32,4,32,128]{3,2,1,0:T(8,128)(2,1)S(1)} all-to-all(bf16[32,4,32,128]{3,2,1,0:T(8,128)(2,1)S(1)} %shard_map.75), channel_id=1, replica_groups=mesh['zed'=8,'y_lo'=2,'core'=2,'y_hi'=2,'x'=4] {'x','y_lo','y_hi','core'}, dimensions={0} | all-to-all | bytes 2097152 | tf_op jit(solution)/shard_map/all_to_all | solution.py:398
  26.9 0.3 shard_map.78
  27.2 1.7 %collective-permute-start = (bf16[2,256,128]{2,1,0:T(8,128)(2,1)S(1)}, bf16[2,256,128]{2,1,0:T(8,128)(2,1)S(1)}, u32[]{:S(2)}, u32[]{:S(2)}) collective-permute-start(bf16[2,256,128]{2,1,0:T(8,128)(2,1)S(1)} %shard_map.78), channel_id=1, source_target_pairs={{0,32},{32,0},{64,96},{96,64},{128,160},{160,128},{192,224},{224,1... | collective-permute-start | bytes 393224 | tf_op jit(solution)/shard_map/ppermute | solution.py:403
  28.9 2.8 %collective-permute-start.2 = (bf16[2,128,128]{2,1,0:T(8,128)(2,1)S(1)}, bf16[2,128,128]{2,1,0:T(8,128)(2,1)S(1)}, u32[]{:S(2)}, u32[]{:S(2)}) collective-permute-start(bf16[2,128,128]{2,1,0:T(8,128)(2,1)S(1)} %slice.4), channel_id=1, source_target_pairs={{0,96},{32,64},{64,32},{96,0},{128,224},{160,192},{192,160},{224,1... | collective-permute-start | bytes 196616 | tf_op jit(solution)/shard_map/ppermute | solution.py:403
  31.7 0.3 collective-permute-start.1
  32.0 2.4 %shard_map.76 = (bf16[4,1024,128]{2,1,0:T(8,128)(2,1)S(1)}, bf16[4,256,128]{2,1,0:T(8,128)(2,1)S(1)}, bf16[128,1024]{1,0:T(8,128)(2,1)S(1)}, f32[2,1024]{1,0:T(2,128)S(1)}, f32[128,1024]{1,0:T(8,128)S(1)}) custom-call(bf16[32,4,32,128]{3,2,1,0:T(8,128)(2,1)S(1)} %all_to_all.10.got_ref), custom_call_target="tpu_custom_call" | custom-call | flops 268435456 | bytes 2097152 | tf_op jit(solution)/shard_map/pallas_call | solution.py:362
  34.4 1.6 %shard_map.77 = (f32[2,1024]{1,0:T(2,128)S(1)}, bf16[128,1024]{1,0:T(8,128)(2,1)S(1)}, f32[2,256]{1,0:T(2,128)S(1)}, f32[128,256]{1,0:T(8,128)S(1)}, bf16[128,256]{1,0:T(8,128)(2,1)S(1)}) custom-call(bf16[4,1024,128]{2,1,0:T(8,128)(2,1)S(1)} %get-tuple-element.26.x_ref, bf16[128,1024]{1,0:T(8,128)(2,1)S(1)} %get-tuple-element.27.vt_ref, ...), custom_call_target="tpu_custom_call" | custom-call | flops 134217728 | bytes 2097152 | tf_op jit(solution)/shard_map/pallas_call | solution.py:362
  36.0 0.0 collective-permute-done.one_ref
  36.0 0.7 %shard_map.79 = (f32[3,256]{1,0:T(4,128)S(1)}, f32[128,256]{1,0:T(8,128)S(1)}) custom-call(bf16[4,256,128]{2,1,0:T(8,128)(2,1)S(1)} %get-tuple-element.32.mid_ref, bf16[128,256]{1,0:T(8,128)(2,1)S(1)} %get-tuple-element.33.flipped_ref, f32[2,256]{1,0:T(2,128)S(1)} %get-tuple-element.34.stat_ref, f32[128,256]{1,0:T(8,128)S(1)} %get-tuple-element.35.acc_ref, ...), custom_call_target="tpu_custom_call" | custom-call | flops 1073741824 | bytes 2097152 | tf_op jit(solution)/shard_map/pallas_call | solution.py:362
  36.7 0.0 collective-permute-done.2.three_ref
  36.8 2.4 %collective-permute-done.1.two_ref = bf16[2,128,128]{2,1,0:T(8,128)(2,1)S(1)} collective-permute-done((bf16[2,128,128]{2,1,0:T(8,128)(2,1)S(1)}, bf16[2,128,128]{2,1,0:T(8,128)(2,1)S(1)}, u32[]{:S(2)}, u32[]{:S(2)}) %collective-permute-start.1) | collective-permute-done | bytes 65568 | tf_op jit(solution)/shard_map/ppermute | solution.py:403
  39.1 0.7 %shard_map.80 = (f32[2,256]{1,0:T(2,128)S(1)}, bf16[128,256]{1,0:T(8,128)(2,1)S(1)}, bf16[256,256]{1,0:T(8,128)(2,1)S(1)}, bf16[384,128]{1,0:T(8,128)(2,1)S(1)},...) custom-call(bf16[4,256,128]{2,1,0:T(8,128)(2,1)S(1)} %get-tuple-element.32.mid_, ...), custom_call_target="tpu_custom_call" | custom-call | flops 268435456 | bytes 2097152 | tf_op jit(solution)/shard_map/pallas_call | solution.py:362
  39.9 0.1 collective-permute-start.3
  40.0 1.2 %collective-permute-start.4 = (bf16[2,128,128]{2,1,0:T(8,128)(2,1)S(1)}, bf16[2,128,128]{2,1,0:T(8,128)(2,1)S(1)}, u32[]{:S(2)}, u32[]{:S(2)}) collective-permute-start(bf16[2,128,128]{2,1,0:T(8,128)(2,1)S(1)} %get-tuple-element.46), channel_id=1, source_target_pairs={{0,64},{32,96},{64,0},{96,32},{128,192},{160,224},{192,128},{224,1... | collective-permute-start | bytes 196616 | tf_op jit(solution)/shard_map/ppermute | solution.py:403
  41.2 2.3 %collective-permute-start.5 = (bf16[2,128,128]{2,1,0:T(8,128)(2,1)S(1)}, bf16[2,128,128]{2,1,0:T(8,128)(2,1)S(1)}, u32[]{:S(2)}, u32[]{:S(2)}) collective-permute-start(bf16[2,128,128]{2,1,0:T(8,128)(2,1)S(1)} %get-tuple-element.47), channel_id=1, source_target_pairs={{0,96},{32,64},{64,32},{96,0},{128,224},{160,192},{192,160},{224,1... | collective-permute-start | bytes 196616 | tf_op jit(solution)/shard_map/ppermute | solution.py:403
  43.5 3.9 %shard_map.81 = (bf16[32,4,32,128]{3,2,1,0:T(8,128)(2,1)S(1)}, f32[2,256,128]{2,1,0:T(8,128)S(1)}, bf16[2,512,128]{2,1,0:T(8,128)(2,1)S(1)}) custom-call(bf16[4,1024,128]{2,1,0:T(8,128)(2,1)S(1)} %get-tuple-element.26.x_ref, f32[2,1024]{1,0:T(2,128)S(1)} %get-tuple-element.30.stat_ref, bf16[128,1024]{1,0:T(8,128)(2,1)S(1)} %get-tuple-element.31.comb_ref, ...), custom_call_target="tpu_custom_call" | custom-call | flops 1006632960 | bytes 2097152 | tf_op jit(solution)/shard_map/pallas_call | solution.py:362
  47.4 0.0 collective-permute-done.4.two_ref
  47.4 0.0 collective-permute-done.5.three_ref
  47.4 0.0 collective-permute-done.3.one_ref
  47.4 0.4 shard_map.82
  47.8 22.2 %all_to_all.11.in_ref = bf16[32,4,32,128]{3,2,1,0:T(8,128)(2,1)S(1)} all-to-all(bf16[32,4,32,128]{3,2,1,0:T(8,128)(2,1)S(1)} %shard_map.82), channel_id=1, replica_groups=mesh['zed'=8,'y_lo'=2,'core'=2,'y_hi'=2,'x'=4] {'x','y_lo','y_hi','core'}, dimensions={0} | all-to-all | bytes 2097152 | tf_op jit(solution)/shard_map/all_to_all | solution.py:398
  70.0 1.0 %shard_map.83 = (bf16[32,4096]{1,0:T(8,128)(2,1)}, bf16[32,4096]{1,0:T(8,128)(2,1)}, bf16[32,4096]{1,0:T(8,128)(2,1)}, bf16[32,4096]{1,0:T(8,128)(2,1)}) custom-call(bf16[32,4,32,128]{3,2,1,0:T(8,128)(2,1)S(1)} %all_to_all.11.in_ref), custom_call_target="tpu_custom_call" | custom-call | tf_op jit(solution)/shard_map/pallas_call | solution.py:385
  (1 shorter events, 0.0 us)
Async XLA Ops:
  27.2 8.8 %collective-permute-start = (bf16[2,256,128]{2,1,0:T(8,128)(2,1)S(1)}, bf16[2,256,128]{2,1,0:T(8,128)(2,1)S(1)}, u32[]{:S(2)}, u32[]{:S(2)}) collective-permute-start(bf16[2,256,128]{2,1,0:T(8,128)(2,1)S(1)} %shard_map.78), channel_id=1, source_target_pairs={{0,32},{32,0},{64,96},{96,64},{128,160},{160,128},{192,224},{224,1... | collective-permute-start | bytes 393224 | tf_op jit(solution)/shard_map/ppermute | solution.py:403
  28.9 7.9 %collective-permute-start.2 = (bf16[2,128,128]{2,1,0:T(8,128)(2,1)S(1)}, bf16[2,128,128]{2,1,0:T(8,128)(2,1)S(1)}, u32[]{:S(2)}, u32[]{:S(2)}) collective-permute-start(bf16[2,128,128]{2,1,0:T(8,128)(2,1)S(1)} %slice.4), channel_id=1, source_target_pairs={{0,96},{32,64},{64,32},{96,0},{128,224},{160,192},{192,160},{224,1... | collective-permute-start | bytes 196616 | tf_op jit(solution)/shard_map/ppermute | solution.py:403
  31.7 7.4 %collective-permute-start.1 = (bf16[2,128,128]{2,1,0:T(8,128)(2,1)S(1)}, bf16[2,128,128]{2,1,0:T(8,128)(2,1)S(1)}, u32[]{:S(2)}, u32[]{:S(2)}) collective-permute-start(bf16[2,128,128]{2,1,0:T(8,128)(2,1)S(1)} %slice.4), channel_id=1, source_target_pairs={{0,64},{32,96},{64,0},{96,32},{128,192},{160,224},{192,128},{224,1... | collective-permute-start | bytes 196616 | tf_op jit(solution)/shard_map/ppermute | solution.py:403
  39.9 7.5 %collective-permute-start.3 = (bf16[2,256,128]{2,1,0:T(8,128)(2,1)S(1)}, bf16[2,256,128]{2,1,0:T(8,128)(2,1)S(1)}, u32[]{:S(2)}, u32[]{:S(2)}) collective-permute-start(bf16[2,256,128]{2,1,0:T(8,128)(2,1)S(1)} %get-tuple-element.45), channel_id=1, source_target_pairs={{0,32},{32,0},{64,96},{96,64},{128,160},{160,128},{192,224},{224,1... | collective-permute-start | bytes 393224 | tf_op jit(solution)/shard_map/ppermute | solution.py:403
  40.0 7.4 %collective-permute-start.4 = (bf16[2,128,128]{2,1,0:T(8,128)(2,1)S(1)}, bf16[2,128,128]{2,1,0:T(8,128)(2,1)S(1)}, u32[]{:S(2)}, u32[]{:S(2)}) collective-permute-start(bf16[2,128,128]{2,1,0:T(8,128)(2,1)S(1)} %get-tuple-element.46), channel_id=1, source_target_pairs={{0,64},{32,96},{64,0},{96,32},{128,192},{160,224},{192,128},{224,1... | collective-permute-start | bytes 196616 | tf_op jit(solution)/shard_map/ppermute | solution.py:403
  41.2 6.2 %collective-permute-start.5 = (bf16[2,128,128]{2,1,0:T(8,128)(2,1)S(1)}, bf16[2,128,128]{2,1,0:T(8,128)(2,1)S(1)}, u32[]{:S(2)}, u32[]{:S(2)}) collective-permute-start(bf16[2,128,128]{2,1,0:T(8,128)(2,1)S(1)} %get-tuple-element.47), channel_id=1, source_target_pairs={{0,96},{32,64},{64,32},{96,0},{128,224},{160,192},{192,160},{224,1... | collective-permute-start | bytes 196616 | tf_op jit(solution)/shard_map/ppermute | solution.py:403

commit v5 on v4

--- a/solution.py
+++ b/solution.py
@@ -236,7 +236,7 @@
     out_stat_ref[2:3] = jnp.sum(flipped_ref[...].astype(F32) * acc, axis=0, keepdims=True)
 
 
-def far_kernel(mid_ref, stat_ref, acc_ref, one_ref, two_ref, three_ref,
+def far_kernel(mid_ref, stat_ref, acc_ref, one_ref, three_ref, two_ref,
                out_stat_ref, comb_ref, slope_ref, far_slope_ref, send_one_ref, send_two_ref, send_three_ref):
     inner = slice(64, 192)
     keys, values, queries, grads = one_ref[0], one_ref[1], mid_ref[2], mid_ref[3]
@@ -274,7 +274,7 @@
     comb_ref[...] = ((left * acc_ref[...] + right * widen(summed3, 0.0)) / total).astype(BF)
 
 
-def back_kernel(x_ref, stat_ref, comb_ref, mid_stat_ref, mid_comb_ref, one_ref, two_ref, three_ref, slope_ref, far_slope_ref,
+def back_kernel(x_ref, stat_ref, comb_ref, mid_stat_ref, mid_comb_ref, one_ref, three_ref, two_ref, slope_ref, far_slope_ref,
                 out_ref, mid_grad_ref, place_ref, kt, stat, dq, dk, dv):
     offset = head_offset()
     kt[...] = flip(x_ref[0])
@@ -339,12 +339,13 @@
         far = two_ref[index].astype(F32) + three_ref[index].astype(F32)
         grads.append(join(near, far).astype(BF))
     pair = jnp.concatenate(grads, axis=1)
+    out_ref[:, 0:2] = in_ref[:, 0:2]
     for half in range(2):
         cut = slice(half * 128, half * 128 + 128)
         plain = nn(place_ref[half], pair[cut]).astype(BF)
         for index in range(2):
             part = plain[:, index * HEAD_DIM : (index + 1) * HEAD_DIM]
-            put_half(out_ref, half, index, half_of(in_ref, half, index) + part)
+            put_half(out_ref, half, index + 2, half_of(in_ref, half, index + 2) + part)
 
 
 def shape(dims, kind):
@@ -405,19 +406,11 @@
 
 def per_device(query_rows, key_rows, value_rows, grad_rows):
     got = plane_exchange(pack([key_rows, value_rows, query_rows, grad_rows]))
-    half_block = pl.BlockSpec((PLANE, 2, ROWS, HEAD_DIM), lambda i: (0, 0, 0, 0))
-    near = pl.pallas_call(
-        select_kernel,
-        grid=(1,),
-        in_specs=[half_block],
-        out_specs=pl.BlockSpec((2, MID, HEAD_DIM), lambda i: (0, 0, 0)),
-        out_shape=shape((2, MID, HEAD_DIM), BF),
-        compiler_params=PARAMS,
-    )(got)
+    near = call(select_kernel, shape((2, MID, HEAD_DIM), BF), [got])
     inner = near[:, 64:192]
     one = z_exchange(near, 1)
+    three = z_exchange(inner, 3)
     two = z_exchange(inner, 2)
-    three = z_exchange(inner, 3)
     ordered, mid, vt, state, acc = call(
         first_kernel,
         [
@@ -460,7 +453,7 @@
             shape((2, 128, HEAD_DIM), BF),
             shape((2, 128, HEAD_DIM), BF),
         ],
-        [mid, mid_stat, mid_acc, one, two, three],
+        [mid, mid_stat, mid_acc, one, three, two],
         flops=2 * 4 * SEG * SEG * HEAD_DIM,
     )
     back_one = z_exchange(send_one, 1)
@@ -473,7 +466,7 @@
             shape((2, MID, HEAD_DIM), F32),
             shape((2, SEG, 128), BF),
         ],
-        [ordered, stat, comb, mid_out_stat, mid_comb, one, two, three, slope, far_slope],
+        [ordered, stat, comb, mid_out_stat, mid_comb, one, three, two, slope, far_slope],
         [
             pltpu.VMEM((HEAD_DIM, TOKENS), BF),
             pltpu.VMEM((2, TOKENS), F32),
@@ -483,19 +476,11 @@
         ],
         flops=3 * 10 * SEG * SEG * HEAD_DIM,
     )
-    upper_half = pl.BlockSpec((PLANE, 2, ROWS, HEAD_DIM), lambda i: (0, 1, 0, 0))
-    mid_block = pl.BlockSpec((2, MID, HEAD_DIM), lambda i: (0, 0, 0))
-    place_block = pl.BlockSpec((2, SEG, 128), lambda i: (0, 0, 0))
-    inner_block = pl.BlockSpec((2, 128, HEAD_DIM), lambda i: (0, 0, 0))
-    packed = pl.pallas_call(
+    packed = call(
         finish_kernel,
-        grid=(1,),
-        in_specs=[upper_half, mid_block, place_block, mid_block, inner_block, inner_block],
-        out_specs=upper_half,
-        out_shape=shape((PLANE, 4, ROWS, HEAD_DIM), BF),
-        input_output_aliases={0: 0},
-        compiler_params=PARAMS,
-    )(packed, mid_grad, place, back_one, back_two, back_three)
+        shape((PLANE, 4, ROWS, HEAD_DIM), BF),
+        [packed, mid_grad, place, back_one, back_two, back_three],
+    )
     return tuple(unpack(plane_exchange(packed)))
 
 

time: 71.3 us -> 71.1 us (level)
    pallas_call x5 -> x7, Pallas kernels: 9.32 us -> 9.87 us  [call(): pl.pallas_call(kernel, out_shape=outs, scratch_shapes=list(scratch), comp...]
  transfers between devices with their start and end apart: 6 -> 6, of which waited for: 1 -> 2; matrix products, arithmetic and copies ran while one was open for 0% -> 0% of each run, Pallas kernels for 12% -> 12%
where the time goes in v5:
time: 71.1 us; the launch traced here: 70.9 us
  blocking collectives  47.5 us (67%)
  Pallas kernels  12.2 us (17%)
  starting transfers between devices  8.34 us (12%)
  waiting for transfers between devices  2.16 us (3%)
  between operations  0.72 us (1%)
    all_to_all x2, blocking collectives, plane_exchange(): lax.all_to_all(packed, ('x', 'y_lo', 'y_hi', 'core'), split_axis=0, conca...  47.5 us
    pallas_call x7, Pallas kernels, call(): pl.pallas_call(kernel, out_shape=outs, scratch_shapes=list(scratch), comp...  9.87 us
    ppermute x6, starting transfers between devices, z_exchange(): return lax.ppermute(block, 'zed', [(at, at ^ apart) for at in range(count)])  8.34 us
    ppermute x6, waiting for transfers between devices, z_exchange(): return lax.ppermute(block, 'zed', [(at, at ^ apart) for at in range(count)])  2.16 us
  transfers between devices with their start and end apart: 6, of which 2 were waited for; matrix products, arithmetic and copies ran while one was open for 0% of the time, Pallas kernels for 12%

profile of v5, /device:TPU:1, one launch (start us, length us, event | category | flops | bytes accessed | tf_op | source)
XLA Modules:
  0.0 70.9 jit_solution(14681264531508284097)
XLA Ops:
  0.6 1.3 %shard_map.75 = bf16[32,4,32,128]{3,2,1,0:T(8,128)(2,1)S(1)} custom-call(bf16[32,4096]{1,0:T(8,128)(2,1)} %key_ref.1, bf16[32,4096]{1,0:T(8,128)(2,1)} %value_ref.1, bf16[32,4096]{1,0:T(8,128)(2,1)} %query_ref.1, bf16[32,4096]{1,0:T(8,128)(2,1)} %grad_ref.1), custom_call_target="tpu_custom_call" | custom-call | tf_op jit(solution)/shard_map/pallas_call | solution.py:373
  1.9 25.0 %all_to_all.10.got_ref = bf16[32,4,32,128]{3,2,1,0:T(8,128)(2,1)S(1)} all-to-all(bf16[32,4,32,128]{3,2,1,0:T(8,128)(2,1)S(1)} %shard_map.75), channel_id=1, replica_groups=mesh['zed'=8,'y_lo'=2,'core'=2,'y_hi'=2,'x'=4] {'x','y_lo','y_hi','core'}, dimensions={0} | all-to-all | bytes 2097152 | tf_op jit(solution)/shard_map/all_to_all | solution.py:399
  26.9 0.2 shard_map.78
  27.1 1.7 %collective-permute-start = (bf16[2,256,128]{2,1,0:T(8,128)(2,1)S(1)}, bf16[2,256,128]{2,1,0:T(8,128)(2,1)S(1)}, u32[]{:S(2)}, u32[]{:S(2)}) collective-permute-start(bf16[2,256,128]{2,1,0:T(8,128)(2,1)S(1)} %shard_map.78), channel_id=1, source_target_pairs={{0,32},{32,0},{64,96},{96,64},{128,160},{160,128},{192,224},{224,1... | collective-permute-start | bytes 393224 | tf_op jit(solution)/shard_map/ppermute | solution.py:404
  28.9 3.0 %collective-permute-start.2 = (bf16[2,128,128]{2,1,0:T(8,128)(2,1)S(1)}, bf16[2,128,128]{2,1,0:T(8,128)(2,1)S(1)}, u32[]{:S(2)}, u32[]{:S(2)}) collective-permute-start(bf16[2,128,128]{2,1,0:T(8,128)(2,1)S(1)} %slice.4), channel_id=1, source_target_pairs={{0,64},{32,96},{64,0},{96,32},{128,192},{160,224},{192,128},{224,1... | collective-permute-start | bytes 196616 | tf_op jit(solution)/shard_map/ppermute | solution.py:404
  31.9 0.0 collective-permute-start.1
  31.9 2.4 %shard_map.76 = (bf16[4,1024,128]{2,1,0:T(8,128)(2,1)S(1)}, bf16[4,256,128]{2,1,0:T(8,128)(2,1)S(1)}, bf16[128,1024]{1,0:T(8,128)(2,1)S(1)}, f32[2,1024]{1,0:T(2,128)S(1)}, f32[128,1024]{1,0:T(8,128)S(1)}) custom-call(bf16[32,4,32,128]{3,2,1,0:T(8,128)(2,1)S(1)} %all_to_all.10.got_ref), custom_call_target="tpu_custom_call" | custom-call | flops 268435456 | bytes 2097152 | tf_op jit(solution)/shard_map/pallas_call | solution.py:363
  34.3 1.6 %shard_map.77 = (f32[2,1024]{1,0:T(2,128)S(1)}, bf16[128,1024]{1,0:T(8,128)(2,1)S(1)}, f32[2,256]{1,0:T(2,128)S(1)}, f32[128,256]{1,0:T(8,128)S(1)}, bf16[128,256]{1,0:T(8,128)(2,1)S(1)}) custom-call(bf16[4,1024,128]{2,1,0:T(8,128)(2,1)S(1)} %get-tuple-element.26.x_ref, bf16[128,1024]{1,0:T(8,128)(2,1)S(1)} %get-tuple-element.27.vt_ref, ...), custom_call_target="tpu_custom_call" | custom-call | flops 134217728 | bytes 2097152 | tf_op jit(solution)/shard_map/pallas_call | solution.py:363
  35.9 0.0 collective-permute-done.one_ref
  35.9 0.7 %shard_map.79 = (f32[3,256]{1,0:T(4,128)S(1)}, f32[128,256]{1,0:T(8,128)S(1)}) custom-call(bf16[4,256,128]{2,1,0:T(8,128)(2,1)S(1)} %get-tuple-element.32.mid_ref, bf16[128,256]{1,0:T(8,128)(2,1)S(1)} %get-tuple-element.33.flipped_ref, f32[2,256]{1,0:T(2,128)S(1)} %get-tuple-element.34.stat_ref, f32[128,256]{1,0:T(8,128)S(1)} %get-tuple-element.35.acc_ref, ...), custom_call_target="tpu_custom_call" | custom-call | flops 1073741824 | bytes 2097152 | tf_op jit(solution)/shard_map/pallas_call | solution.py:363
  36.6 0.0 collective-permute-done.2.two_ref
  36.6 1.5 %collective-permute-done.1.three_ref = bf16[2,128,128]{2,1,0:T(8,128)(2,1)S(1)} collective-permute-done((bf16[2,128,128]{2,1,0:T(8,128)(2,1)S(1)}, bf16[2,128,128]{2,1,0:T(8,128)(2,1)S(1)}, u32[]{:S(2)}, u32[]{:S(2)}) %collective-permute-start.1) | collective-permute-done | bytes 65568 | tf_op jit(solution)/shard_map/ppermute | solution.py:404
  38.1 0.7 %shard_map.80 = (f32[2,256]{1,0:T(2,128)S(1)}, bf16[128,256]{1,0:T(8,128)(2,1)S(1)}, bf16[256,256]{1,0:T(8,128)(2,1)S(1)}, bf16[384,128]{1,0:T(8,128)(2,1)S(1)},...) custom-call(bf16[4,256,128]{2,1,0:T(8,128)(2,1)S(1)} %get-tuple-element.32.mid_, ...), custom_call_target="tpu_custom_call" | custom-call | flops 268435456 | bytes 2097152 | tf_op jit(solution)/shard_map/pallas_call | solution.py:363
  38.8 0.1 collective-permute-start.3
  38.9 2.1 %collective-permute-start.4 = (bf16[2,128,128]{2,1,0:T(8,128)(2,1)S(1)}, bf16[2,128,128]{2,1,0:T(8,128)(2,1)S(1)}, u32[]{:S(2)}, u32[]{:S(2)}) collective-permute-start(bf16[2,128,128]{2,1,0:T(8,128)(2,1)S(1)} %get-tuple-element.46), channel_id=1, source_target_pairs={{0,64},{32,96},{64,0},{96,32},{128,192},{160,224},{192,128},{224,1... | collective-permute-start | bytes 196616 | tf_op jit(solution)/shard_map/ppermute | solution.py:404
  41.0 1.5 %collective-permute-start.5 = (bf16[2,128,128]{2,1,0:T(8,128)(2,1)S(1)}, bf16[2,128,128]{2,1,0:T(8,128)(2,1)S(1)}, u32[]{:S(2)}, u32[]{:S(2)}) collective-permute-start(bf16[2,128,128]{2,1,0:T(8,128)(2,1)S(1)} %get-tuple-element.47), channel_id=1, source_target_pairs={{0,96},{32,64},{64,32},{96,0},{128,224},{160,192},{192,160},{224,1... | collective-permute-start | bytes 196616 | tf_op jit(solution)/shard_map/ppermute | solution.py:404
  42.5 3.9 %shard_map.81 = (bf16[32,4,32,128]{3,2,1,0:T(8,128)(2,1)S(1)}, f32[2,256,128]{2,1,0:T(8,128)S(1)}, bf16[2,512,128]{2,1,0:T(8,128)(2,1)S(1)}) custom-call(bf16[4,1024,128]{2,1,0:T(8,128)(2,1)S(1)} %get-tuple-element.26.x_ref, f32[2,1024]{1,0:T(2,128)S(1)} %get-tuple-element.30.stat_ref, bf16[128,1024]{1,0:T(8,128)(2,1)S(1)} %get-tuple-element.31.comb_ref, ...), custom_call_target="tpu_custom_call" | custom-call | flops 1006632960 | bytes 2097152 | tf_op jit(solution)/shard_map/pallas_call | solution.py:363
  46.4 0.0 collective-permute-done.4.two_ref
  46.4 0.7 collective-permute-done.5.three_ref
  47.0 0.0 collective-permute-done.3.one_ref
  47.0 0.3 shard_map.82
  47.4 22.5 %all_to_all.11.in_ref = bf16[32,4,32,128]{3,2,1,0:T(8,128)(2,1)S(1)} all-to-all(bf16[32,4,32,128]{3,2,1,0:T(8,128)(2,1)S(1)} %shard_map.82), channel_id=1, replica_groups=mesh['zed'=8,'y_lo'=2,'core'=2,'y_hi'=2,'x'=4] {'x','y_lo','y_hi','core'}, dimensions={0} | all-to-all | bytes 2097152 | tf_op jit(solution)/shard_map/all_to_all | solution.py:399
  69.9 1.0 %shard_map.83 = (bf16[32,4096]{1,0:T(8,128)(2,1)}, bf16[32,4096]{1,0:T(8,128)(2,1)}, bf16[32,4096]{1,0:T(8,128)(2,1)}, bf16[32,4096]{1,0:T(8,128)(2,1)}) custom-call(bf16[32,4,32,128]{3,2,1,0:T(8,128)(2,1)S(1)} %all_to_all.11.in_ref), custom_call_target="tpu_custom_call" | custom-call | tf_op jit(solution)/shard_map/pallas_call | solution.py:386
  (1 shorter events, 0.0 us)
Async XLA Ops:
  27.1 8.7 %collective-permute-start = (bf16[2,256,128]{2,1,0:T(8,128)(2,1)S(1)}, bf16[2,256,128]{2,1,0:T(8,128)(2,1)S(1)}, u32[]{:S(2)}, u32[]{:S(2)}) collective-permute-start(bf16[2,256,128]{2,1,0:T(8,128)(2,1)S(1)} %shard_map.78), channel_id=1, source_target_pairs={{0,32},{32,0},{64,96},{96,64},{128,160},{160,128},{192,224},{224,1... | collective-permute-start | bytes 393224 | tf_op jit(solution)/shard_map/ppermute | solution.py:404
  28.9 7.7 %collective-permute-start.2 = (bf16[2,128,128]{2,1,0:T(8,128)(2,1)S(1)}, bf16[2,128,128]{2,1,0:T(8,128)(2,1)S(1)}, u32[]{:S(2)}, u32[]{:S(2)}) collective-permute-start(bf16[2,128,128]{2,1,0:T(8,128)(2,1)S(1)} %slice.4), channel_id=1, source_target_pairs={{0,64},{32,96},{64,0},{96,32},{128,192},{160,224},{192,128},{224,1... | collective-permute-start | bytes 196616 | tf_op jit(solution)/shard_map/ppermute | solution.py:404
  31.9 6.2 %collective-permute-start.1 = (bf16[2,128,128]{2,1,0:T(8,128)(2,1)S(1)}, bf16[2,128,128]{2,1,0:T(8,128)(2,1)S(1)}, u32[]{:S(2)}, u32[]{:S(2)}) collective-permute-start(bf16[2,128,128]{2,1,0:T(8,128)(2,1)S(1)} %slice.4), channel_id=1, source_target_pairs={{0,96},{32,64},{64,32},{96,0},{128,224},{160,192},{192,160},{224,1... | collective-permute-start | bytes 196616 | tf_op jit(solution)/shard_map/ppermute | solution.py:404
  38.8 8.2 %collective-permute-start.3 = (bf16[2,256,128]{2,1,0:T(8,128)(2,1)S(1)}, bf16[2,256,128]{2,1,0:T(8,128)(2,1)S(1)}, u32[]{:S(2)}, u32[]{:S(2)}) collective-permute-start(bf16[2,256,128]{2,1,0:T(8,128)(2,1)S(1)} %get-tuple-element.45), channel_id=1, source_target_pairs={{0,32},{32,0},{64,96},{96,64},{128,160},{160,128},{192,224},{224,1... | collective-permute-start | bytes 393224 | tf_op jit(solution)/shard_map/ppermute | solution.py:404
  38.9 7.4 %collective-permute-start.4 = (bf16[2,128,128]{2,1,0:T(8,128)(2,1)S(1)}, bf16[2,128,128]{2,1,0:T(8,128)(2,1)S(1)}, u32[]{:S(2)}, u32[]{:S(2)}) collective-permute-start(bf16[2,128,128]{2,1,0:T(8,128)(2,1)S(1)} %get-tuple-element.46), channel_id=1, source_target_pairs={{0,64},{32,96},{64,0},{96,32},{128,192},{160,224},{192,128},{224,1... | collective-permute-start | bytes 196616 | tf_op jit(solution)/shard_map/ppermute | solution.py:404
  41.0 6.0 %collective-permute-start.5 = (bf16[2,128,128]{2,1,0:T(8,128)(2,1)S(1)}, bf16[2,128,128]{2,1,0:T(8,128)(2,1)S(1)}, u32[]{:S(2)}, u32[]{:S(2)}) collective-permute-start(bf16[2,128,128]{2,1,0:T(8,128)(2,1)S(1)} %get-tuple-element.47), channel_id=1, source_target_pairs={{0,96},{32,64},{64,32},{96,0},{128,224},{160,192},{192,160},{224,1... | collective-permute-start | bytes 196616 | tf_op jit(solution)/shard_map/ppermute | solution.py:404

commit v6 on v5

--- a/solution.py
+++ b/solution.py
@@ -236,8 +236,8 @@
     out_stat_ref[2:3] = jnp.sum(flipped_ref[...].astype(F32) * acc, axis=0, keepdims=True)
 
 
-def far_kernel(mid_ref, stat_ref, acc_ref, one_ref, three_ref, two_ref,
-               out_stat_ref, comb_ref, slope_ref, far_slope_ref, send_one_ref, send_two_ref, send_three_ref):
+def far_kernel(mid_ref, stat_ref, one_ref, three_ref, two_ref,
+               out_stat_ref, weight_ref, slope_ref, far_slope_ref, send_one_ref, send_two_ref, send_three_ref):
     inner = slice(64, 192)
     keys, values, queries, grads = one_ref[0], one_ref[1], mid_ref[2], mid_ref[3]
     keys3 = jnp.concatenate([keys[inner], two_ref[0], three_ref[0]], axis=0)
@@ -249,7 +249,7 @@
     weights3 = jnp.exp2((new - peak3) * RATE)
     total3 = jnp.sum(weights3, axis=0, keepdims=True)
     dot3 = jnp.sum(weights3 * grads3[128:], axis=0, keepdims=True)
-    summed3 = nn(flip(values3[128:]), weights3.astype(BF))
+    weight_ref[...] = weights3.astype(BF)
     peak3 = widen(peak3, NEG)
     best = jnp.maximum(stat_ref[0:1], peak3)
     left = jnp.exp2((stat_ref[0:1] - best) * RATE)
@@ -259,6 +259,8 @@
     log_total = best * RATE + jnp.log2(total)
     out_stat_ref[0:1] = log_total
     out_stat_ref[1:2] = dot
+    out_stat_ref[2:3] = left / total
+    out_stat_ref[3:4] = right / total
     probs3 = jnp.exp2(scores3 * RATE - narrow(log_total))
     slopes3 = (probs3 * (grads3 - narrow(dot))).astype(BF)
     probs2 = jnp.exp2(scores2 * RATE - log_total)
@@ -271,15 +273,14 @@
         send_three_ref[index] = (far[256:] * scale).astype(BF)
     slope_ref[...] = slopes2
     far_slope_ref[...] = slopes3
-    comb_ref[...] = ((left * acc_ref[...] + right * widen(summed3, 0.0)) / total).astype(BF)
-
-
-def back_kernel(x_ref, stat_ref, comb_ref, mid_stat_ref, mid_comb_ref, one_ref, three_ref, two_ref, slope_ref, far_slope_ref,
+
+
+def back_kernel(x_ref, stat_ref, comb_ref, mid_stat_ref, mid_acc_ref, weight_ref, one_ref, three_ref, two_ref, slope_ref, far_slope_ref,
                 out_ref, mid_grad_ref, place_ref, kt, stat, dq, dk, dv):
     offset = head_offset()
     kt[...] = flip(x_ref[0])
     stat[...] = stat_ref[...]
-    stat[:, LOW : LOW + MID] = mid_stat_ref[...]
+    stat[:, LOW : LOW + MID] = mid_stat_ref[0:2]
     dq[...] = jnp.zeros_like(dq)
     dk[...] = jnp.zeros_like(dk)
     dv[...] = jnp.zeros_like(dv)
@@ -311,6 +312,10 @@
     mid_grad_ref[0] = dk[LOW : LOW + MID] * SCALE
     mid_grad_ref[1] = dv[LOW : LOW + MID]
     keys3 = jnp.concatenate([one_ref[0, 64:192], two_ref[0], three_ref[0]], axis=0)
+    distant = jnp.concatenate([two_ref[1], three_ref[1]], axis=0)
+    mid_comb = mid_stat_ref[2:3] * mid_acc_ref[...] + mid_stat_ref[3:4] * widen(
+        nn(flip(distant), weight_ref[...]), 0.0
+    )
     dq[:, LOW : LOW + MID] += nn(flip(one_ref[0]), slope_ref[...]) + widen(
         nn(flip(keys3), far_slope_ref[...]), 0.0
     )
@@ -318,7 +323,7 @@
     place_ref[1] = unordering(offset, 1, 0, 128)
     query = (dq[...] * SCALE).astype(BF)
     comb = jnp.concatenate(
-        [comb_ref[:, :LOW], mid_comb_ref[...], comb_ref[:, LOW + MID :]], axis=1
+        [comb_ref[:, :LOW], mid_comb.astype(BF), comb_ref[:, LOW + MID :]], axis=1
     )
     both = jnp.concatenate([comb, query], axis=0)
     for half in range(2):
@@ -442,18 +447,18 @@
         [mid, flipped, mid_stat, mid_acc, one],
         flops=8 * 4 * SEG * SEG * HEAD_DIM,
     )
-    mid_out_stat, mid_comb, slope, far_slope, send_one, send_two, send_three = call(
+    mid_out_stat, weight, slope, far_slope, send_one, send_two, send_three = call(
         far_kernel,
         [
-            shape((2, MID), F32),
-            shape((HEAD_DIM, MID), BF),
+            shape((4, MID), F32),
+            shape((MID, 128), BF),
             shape((MID, MID), BF),
             shape((384, 128), BF),
             shape((2, MID, HEAD_DIM), BF),
             shape((2, 128, HEAD_DIM), BF),
             shape((2, 128, HEAD_DIM), BF),
         ],
-        [mid, mid_stat, mid_acc, one, three, two],
+        [mid, mid_stat, one, three, two],
         flops=2 * 4 * SEG * SEG * HEAD_DIM,
     )
     back_one = z_exchange(send_one, 1)
@@ -466,7 +471,7 @@
             shape((2, MID, HEAD_DIM), F32),
             shape((2, SEG, 128), BF),
         ],
-        [ordered, stat, comb, mid_out_stat, mid_comb, one, three, two, slope, far_slope],
+        [ordered, stat, comb, mid_out_stat, mid_acc, weight, one, three, two, slope, far_slope],
         [
             pltpu.VMEM((HEAD_DIM, TOKENS), BF),
             pltpu.VMEM((2, TOKENS), F32),

time: 71.1 us -> 71.1 us (level)
  no operation moved by 1% of the time
where the time goes in v6:
time: 71.1 us; the launch traced here: 70.9 us
  blocking collectives  47.5 us (67%)
  Pallas kernels  12.2 us (17%)
  starting transfers between devices  8.34 us (12%)
  waiting for transfers between devices  2.1 us (3%)
  between operations  0.72 us (1%)
    all_to_all x2, blocking collectives, plane_exchange(): lax.all_to_all(packed, ('x', 'y_lo', 'y_hi', 'core'), split_axis=0, conca...  47.5 us
    pallas_call x7, Pallas kernels, call(): pl.pallas_call(kernel, out_shape=outs, scratch_shapes=list(scratch), comp...  9.9 us
    ppermute x6, starting transfers between devices, z_exchange(): return lax.ppermute(block, 'zed', [(at, at ^ apart) for at in range(count)])  8.34 us
    ppermute x6, waiting for transfers between devices, z_exchange(): return lax.ppermute(block, 'zed', [(at, at ^ apart) for at in range(count)])  2.1 us
  transfers between devices with their start and end apart: 6, of which 2 were waited for; matrix products, arithmetic and copies ran while one was open for 0% of the time, Pallas kernels for 12%

profile of v6, /device:TPU:1, one launch (start us, length us, event | category | flops | bytes accessed | tf_op | source)
XLA Modules:
  0.0 70.9 jit_solution(7768567878737399580)
XLA Ops:
  0.6 1.3 %shard_map.75 = bf16[32,4,32,128]{3,2,1,0:T(8,128)(2,1)S(1)} custom-call(bf16[32,4096]{1,0:T(8,128)(2,1)} %key_ref.1, bf16[32,4096]{1,0:T(8,128)(2,1)} %value_ref.1, bf16[32,4096]{1,0:T(8,128)(2,1)} %query_ref.1, bf16[32,4096]{1,0:T(8,128)(2,1)} %grad_ref.1), custom_call_target="tpu_custom_call" | custom-call | tf_op jit(solution)/shard_map/pallas_call | solution.py:378
  1.9 25.0 %all_to_all.10.got_ref = bf16[32,4,32,128]{3,2,1,0:T(8,128)(2,1)S(1)} all-to-all(bf16[32,4,32,128]{3,2,1,0:T(8,128)(2,1)S(1)} %shard_map.75), channel_id=1, replica_groups=mesh['zed'=8,'y_lo'=2,'core'=2,'y_hi'=2,'x'=4] {'x','y_lo','y_hi','core'}, dimensions={0} | all-to-all | bytes 2097152 | tf_op jit(solution)/shard_map/all_to_all | solution.py:404
  26.9 0.2 shard_map.78
  27.1 1.7 %collective-permute-start = (bf16[2,256,128]{2,1,0:T(8,128)(2,1)S(1)}, bf16[2,256,128]{2,1,0:T(8,128)(2,1)S(1)}, u32[]{:S(2)}, u32[]{:S(2)}) collective-permute-start(bf16[2,256,128]{2,1,0:T(8,128)(2,1)S(1)} %shard_map.78), channel_id=1, source_target_pairs={{0,32},{32,0},{64,96},{96,64},{128,160},{160,128},{192,224},{224,1... | collective-permute-start | bytes 393224 | tf_op jit(solution)/shard_map/ppermute | solution.py:409
  28.9 3.0 %collective-permute-start.2 = (bf16[2,128,128]{2,1,0:T(8,128)(2,1)S(1)}, bf16[2,128,128]{2,1,0:T(8,128)(2,1)S(1)}, u32[]{:S(2)}, u32[]{:S(2)}) collective-permute-start(bf16[2,128,128]{2,1,0:T(8,128)(2,1)S(1)} %slice.4), channel_id=1, source_target_pairs={{0,64},{32,96},{64,0},{96,32},{128,192},{160,224},{192,128},{224,1... | collective-permute-start | bytes 196616 | tf_op jit(solution)/shard_map/ppermute | solution.py:409
  31.9 0.0 collective-permute-start.1
  31.9 2.4 %shard_map.76 = (bf16[4,1024,128]{2,1,0:T(8,128)(2,1)S(1)}, bf16[4,256,128]{2,1,0:T(8,128)(2,1)S(1)}, bf16[128,1024]{1,0:T(8,128)(2,1)S(1)}, f32[2,1024]{1,0:T(2,128)S(1)}, f32[128,1024]{1,0:T(8,128)S(1)}) custom-call(bf16[32,4,32,128]{3,2,1,0:T(8,128)(2,1)S(1)} %all_to_all.10.got_ref), custom_call_target="tpu_custom_call" | custom-call | flops 268435456 | bytes 2097152 | tf_op jit(solution)/shard_map/pallas_call | solution.py:368
  34.3 1.6 %shard_map.77 = (f32[2,1024]{1,0:T(2,128)S(1)}, bf16[128,1024]{1,0:T(8,128)(2,1)S(1)}, f32[2,256]{1,0:T(2,128)S(1)}, f32[128,256]{1,0:T(8,128)S(1)}, bf16[128,256]{1,0:T(8,128)(2,1)S(1)}) custom-call(bf16[4,1024,128]{2,1,0:T(8,128)(2,1)S(1)} %get-tuple-element.26.x_ref, bf16[128,1024]{1,0:T(8,128)(2,1)S(1)} %get-tuple-element.27.vt_ref, ...), custom_call_target="tpu_custom_call" | custom-call | flops 134217728 | bytes 2097152 | tf_op jit(solution)/shard_map/pallas_call | solution.py:368
  35.9 0.0 collective-permute-done.one_ref
  35.9 0.7 %shard_map.79 = (f32[3,256]{1,0:T(4,128)S(1)}, f32[128,256]{1,0:T(8,128)S(1)}) custom-call(bf16[4,256,128]{2,1,0:T(8,128)(2,1)S(1)} %get-tuple-element.32.mid_ref, bf16[128,256]{1,0:T(8,128)(2,1)S(1)} %get-tuple-element.33.flipped_ref, f32[2,256]{1,0:T(2,128)S(1)} %get-tuple-element.34.stat_ref, f32[128,256]{1,0:T(8,128)S(1)} %get-tuple-element.35.acc_ref, ...), custom_call_target="tpu_custom_call" | custom-call | flops 1073741824 | bytes 2097152 | tf_op jit(solution)/shard_map/pallas_call | solution.py:368
  36.6 0.0 collective-permute-done.2.two_ref
  36.6 1.5 %collective-permute-done.1.three_ref = bf16[2,128,128]{2,1,0:T(8,128)(2,1)S(1)} collective-permute-done((bf16[2,128,128]{2,1,0:T(8,128)(2,1)S(1)}, bf16[2,128,128]{2,1,0:T(8,128)(2,1)S(1)}, u32[]{:S(2)}, u32[]{:S(2)}) %collective-permute-start.1) | collective-permute-done | bytes 65568 | tf_op jit(solution)/shard_map/ppermute | solution.py:409
  38.1 0.7 shard_map.80
  38.8 0.1 collective-permute-start.3
  38.9 2.1 %collective-permute-start.4 = (bf16[2,128,128]{2,1,0:T(8,128)(2,1)S(1)}, bf16[2,128,128]{2,1,0:T(8,128)(2,1)S(1)}, u32[]{:S(2)}, u32[]{:S(2)}) collective-permute-start(bf16[2,128,128]{2,1,0:T(8,128)(2,1)S(1)} %get-tuple-element.46), channel_id=1, source_target_pairs={{0,64},{32,96},{64,0},{96,32},{128,192},{160,224},{192,128},{224,1... | collective-permute-start | bytes 196616 | tf_op jit(solution)/shard_map/ppermute | solution.py:409
  40.9 1.5 %collective-permute-start.5 = (bf16[2,128,128]{2,1,0:T(8,128)(2,1)S(1)}, bf16[2,128,128]{2,1,0:T(8,128)(2,1)S(1)}, u32[]{:S(2)}, u32[]{:S(2)}) collective-permute-start(bf16[2,128,128]{2,1,0:T(8,128)(2,1)S(1)} %get-tuple-element.47), channel_id=1, source_target_pairs={{0,96},{32,64},{64,32},{96,0},{128,224},{160,192},{192,160},{224,1... | collective-permute-start | bytes 196616 | tf_op jit(solution)/shard_map/ppermute | solution.py:409
  42.4 3.9 %shard_map.81 = (bf16[32,4,32,128]{3,2,1,0:T(8,128)(2,1)S(1)}, f32[2,256,128]{2,1,0:T(8,128)S(1)}, bf16[2,512,128]{2,1,0:T(8,128)(2,1)S(1)}) custom-call(bf16[4,1024,128]{2,1,0:T(8,128)(2,1)S(1)} %get-tuple-element.26.x_ref, f32[2,1024]{1,0:T(2,128)S(1)} %get-tuple-element.30.stat_ref, bf16[128,1024]{1,0:T(8,128)(2,1)S(1)} %get-tuple-element.31.comb_ref, ...), custom_call_target="tpu_custom_call" | custom-call | flops 1006632960 | bytes 2097152 | tf_op jit(solution)/shard_map/pallas_call | solution.py:368
  46.4 0.0 collective-permute-done.4.two_ref
  46.4 0.6 collective-permute-done.5.three_ref
  47.0 0.0 collective-permute-done.3.one_ref
  47.0 0.3 shard_map.82
  47.3 22.5 %all_to_all.11.in_ref = bf16[32,4,32,128]{3,2,1,0:T(8,128)(2,1)S(1)} all-to-all(bf16[32,4,32,128]{3,2,1,0:T(8,128)(2,1)S(1)} %shard_map.82), channel_id=1, replica_groups=mesh['zed'=8,'y_lo'=2,'core'=2,'y_hi'=2,'x'=4] {'x','y_lo','y_hi','core'}, dimensions={0} | all-to-all | bytes 2097152 | tf_op jit(solution)/shard_map/all_to_all | solution.py:404
  69.9 1.0 %shard_map.83 = (bf16[32,4096]{1,0:T(8,128)(2,1)}, bf16[32,4096]{1,0:T(8,128)(2,1)}, bf16[32,4096]{1,0:T(8,128)(2,1)}, bf16[32,4096]{1,0:T(8,128)(2,1)}) custom-call(bf16[32,4,32,128]{3,2,1,0:T(8,128)(2,1)S(1)} %all_to_all.11.in_ref), custom_call_target="tpu_custom_call" | custom-call | tf_op jit(solution)/shard_map/pallas_call | solution.py:391
  (1 shorter events, 0.0 us)
Async XLA Ops:
  27.1 8.7 %collective-permute-start = (bf16[2,256,128]{2,1,0:T(8,128)(2,1)S(1)}, bf16[2,256,128]{2,1,0:T(8,128)(2,1)S(1)}, u32[]{:S(2)}, u32[]{:S(2)}) collective-permute-start(bf16[2,256,128]{2,1,0:T(8,128)(2,1)S(1)} %shard_map.78), channel_id=1, source_target_pairs={{0,32},{32,0},{64,96},{96,64},{128,160},{160,128},{192,224},{224,1... | collective-permute-start | bytes 393224 | tf_op jit(solution)/shard_map/ppermute | solution.py:409
  28.9 7.7 %collective-permute-start.2 = (bf16[2,128,128]{2,1,0:T(8,128)(2,1)S(1)}, bf16[2,128,128]{2,1,0:T(8,128)(2,1)S(1)}, u32[]{:S(2)}, u32[]{:S(2)}) collective-permute-start(bf16[2,128,128]{2,1,0:T(8,128)(2,1)S(1)} %slice.4), channel_id=1, source_target_pairs={{0,64},{32,96},{64,0},{96,32},{128,192},{160,224},{192,128},{224,1... | collective-permute-start | bytes 196616 | tf_op jit(solution)/shard_map/ppermute | solution.py:409
  31.9 6.2 %collective-permute-start.1 = (bf16[2,128,128]{2,1,0:T(8,128)(2,1)S(1)}, bf16[2,128,128]{2,1,0:T(8,128)(2,1)S(1)}, u32[]{:S(2)}, u32[]{:S(2)}) collective-permute-start(bf16[2,128,128]{2,1,0:T(8,128)(2,1)S(1)} %slice.4), channel_id=1, source_target_pairs={{0,96},{32,64},{64,32},{96,0},{128,224},{160,192},{192,160},{224,1... | collective-permute-start | bytes 196616 | tf_op jit(solution)/shard_map/ppermute | solution.py:409
  38.8 8.2 %collective-permute-start.3 = (bf16[2,256,128]{2,1,0:T(8,128)(2,1)S(1)}, bf16[2,256,128]{2,1,0:T(8,128)(2,1)S(1)}, u32[]{:S(2)}, u32[]{:S(2)}) collective-permute-start(bf16[2,256,128]{2,1,0:T(8,128)(2,1)S(1)} %get-tuple-element.45), channel_id=1, source_target_pairs={{0,32},{32,0},{64,96},{96,64},{128,160},{160,128},{192,224},{224,1... | collective-permute-start | bytes 393224 | tf_op jit(solution)/shard_map/ppermute | solution.py:409
  38.9 7.5 %collective-permute-start.4 = (bf16[2,128,128]{2,1,0:T(8,128)(2,1)S(1)}, bf16[2,128,128]{2,1,0:T(8,128)(2,1)S(1)}, u32[]{:S(2)}, u32[]{:S(2)}) collective-permute-start(bf16[2,128,128]{2,1,0:T(8,128)(2,1)S(1)} %get-tuple-element.46), channel_id=1, source_target_pairs={{0,64},{32,96},{64,0},{96,32},{128,192},{160,224},{192,128},{224,1... | collective-permute-start | bytes 196616 | tf_op jit(solution)/shard_map/ppermute | solution.py:409
  40.9 6.0 %collective-permute-start.5 = (bf16[2,128,128]{2,1,0:T(8,128)(2,1)S(1)}, bf16[2,128,128]{2,1,0:T(8,128)(2,1)S(1)}, u32[]{:S(2)}, u32[]{:S(2)}) collective-permute-start(bf16[2,128,128]{2,1,0:T(8,128)(2,1)S(1)} %get-tuple-element.47), channel_id=1, source_target_pairs={{0,96},{32,64},{64,32},{96,0},{128,224},{160,192},{192,160},{224,1... | collective-permute-start | bytes 196616 | tf_op jit(solution)/shard_map/ppermute | solution.py:409

commit v7 on v6

--- a/solution.py
+++ b/solution.py
@@ -227,23 +227,25 @@
     return jnp.concatenate([whole[:64], whole[64:192] + part, whole[192:]], axis=0)
 
 
-def forward_kernel(mid_ref, flipped_ref, stat_ref, acc_ref, one_ref, out_stat_ref, out_acc_ref):
+def forward_kernel(mid_ref, flipped_ref, stat_ref, acc_ref, one_ref, out_stat_ref, out_acc_ref, score_ref, product_ref):
     state = (stat_ref[0:1], stat_ref[1:2], acc_ref[...])
     state = merge(*state, *forward_of(one_ref[0], flip(one_ref[1]), mid_ref[2]))
+    score_ref[...] = nt(one_ref[0], mid_ref[2])
+    product_ref[...] = nt(one_ref[1], mid_ref[3])
     peak, total, summed = forward_of(one_ref[0, 64:192], flip(one_ref[1, 64:192]), mid_ref[2, 64:192])
     peak, total, acc = merge(*state, widen(peak, NEG), widen(total, 0.0), widen(summed, 0.0))
     out_stat_ref[0:1], out_stat_ref[1:2], out_acc_ref[...] = peak, total, acc
     out_stat_ref[2:3] = jnp.sum(flipped_ref[...].astype(F32) * acc, axis=0, keepdims=True)
 
 
-def far_kernel(mid_ref, stat_ref, one_ref, three_ref, two_ref,
+def far_kernel(mid_ref, stat_ref, score_ref, product_ref, one_ref, three_ref, two_ref,
                out_stat_ref, weight_ref, slope_ref, far_slope_ref, send_one_ref, send_two_ref, send_three_ref):
     inner = slice(64, 192)
     keys, values, queries, grads = one_ref[0], one_ref[1], mid_ref[2], mid_ref[3]
     keys3 = jnp.concatenate([keys[inner], two_ref[0], three_ref[0]], axis=0)
     values3 = jnp.concatenate([values[inner], two_ref[1], three_ref[1]], axis=0)
     scores3, grads3 = nt(keys3, queries[inner]), nt(values3, grads[inner])
-    scores2, grads2 = nt(keys, queries), nt(values, grads)
+    scores2, grads2 = score_ref[...], product_ref[...]
     new = scores3[128:]
     peak3 = jnp.max(new, axis=0, keepdims=True)
     weights3 = jnp.exp2((new - peak3) * RATE)
@@ -441,9 +443,14 @@
         [pltpu.VMEM((2, TOKENS), F32), pltpu.VMEM((HEAD_DIM, TOKENS), F32)],
         flops=4 * SEG * SEG * HEAD_DIM,
     )
-    mid_stat, mid_acc = call(
+    mid_stat, mid_acc, score, product = call(
         forward_kernel,
-        [shape((3, MID), F32), shape((HEAD_DIM, MID), F32)],
+        [
+            shape((3, MID), F32),
+            shape((HEAD_DIM, MID), F32),
+            shape((MID, MID), F32),
+            shape((MID, MID), F32),
+        ],
         [mid, flipped, mid_stat, mid_acc, one],
         flops=8 * 4 * SEG * SEG * HEAD_DIM,
     )
@@ -458,7 +465,7 @@
             shape((2, 128, HEAD_DIM), BF),
             shape((2, 128, HEAD_DIM), BF),
         ],
-        [mid, mid_stat, one, three, two],
+        [mid, mid_stat, score, product, one, three, two],
         flops=2 * 4 * SEG * SEG * HEAD_DIM,
     )
     back_one = z_exchange(send_one, 1)

time: 71.1 us -> 71.1 us (level)
  no operation moved by 1% of the time
where the time goes in v7:
time: 71.1 us; the launch traced here: 70.9 us
  blocking collectives  47.5 us (67%)
  Pallas kernels  12 us (17%)
  starting transfers between devices  8.34 us (12%)
  waiting for transfers between devices  2.28 us (3%)
  between operations  0.73 us (1%)
    all_to_all x2, blocking collectives, plane_exchange(): lax.all_to_all(packed, ('x', 'y_lo', 'y_hi', 'core'), split_axis=0, conca...  47.5 us
    pallas_call x7, Pallas kernels, call(): pl.pallas_call(kernel, out_shape=outs, scratch_shapes=list(scratch), comp...  9.7 us
    ppermute x6, starting transfers between devices, z_exchange(): return lax.ppermute(block, 'zed', [(at, at ^ apart) for at in range(count)])  8.34 us
    ppermute x6, waiting for transfers between devices, z_exchange(): return lax.ppermute(block, 'zed', [(at, at ^ apart) for at in range(count)])  2.28 us
  transfers between devices with their start and end apart: 6, of which 2 were waited for; matrix products, arithmetic and copies ran while one was open for 0% of the time, Pallas kernels for 12%

profile of v7, /device:TPU:1, one launch (start us, length us, event | category | flops | bytes accessed | tf_op | source)
XLA Modules:
  0.0 70.9 jit_solution(1595896140001963163)
XLA Ops:
  0.6 1.3 %shard_map.75 = bf16[32,4,32,128]{3,2,1,0:T(8,128)(2,1)S(1)} custom-call(bf16[32,4096]{1,0:T(8,128)(2,1)} %key_ref.1, bf16[32,4096]{1,0:T(8,128)(2,1)} %value_ref.1, bf16[32,4096]{1,0:T(8,128)(2,1)} %query_ref.1, bf16[32,4096]{1,0:T(8,128)(2,1)} %grad_ref.1), custom_call_target="tpu_custom_call" | custom-call | tf_op jit(solution)/shard_map/pallas_call | solution.py:380
  1.9 25.0 %all_to_all.10.got_ref = bf16[32,4,32,128]{3,2,1,0:T(8,128)(2,1)S(1)} all-to-all(bf16[32,4,32,128]{3,2,1,0:T(8,128)(2,1)S(1)} %shard_map.75), channel_id=1, replica_groups=mesh['zed'=8,'y_lo'=2,'core'=2,'y_hi'=2,'x'=4] {'x','y_lo','y_hi','core'}, dimensions={0} | all-to-all | bytes 2097152 | tf_op jit(solution)/shard_map/all_to_all | solution.py:406
  26.9 0.2 shard_map.78
  27.1 1.7 %collective-permute-start = (bf16[2,256,128]{2,1,0:T(8,128)(2,1)S(1)}, bf16[2,256,128]{2,1,0:T(8,128)(2,1)S(1)}, u32[]{:S(2)}, u32[]{:S(2)}) collective-permute-start(bf16[2,256,128]{2,1,0:T(8,128)(2,1)S(1)} %shard_map.78), channel_id=1, source_target_pairs={{0,32},{32,0},{64,96},{96,64},{128,160},{160,128},{192,224},{224,1... | collective-permute-start | bytes 393224 | tf_op jit(solution)/shard_map/ppermute | solution.py:411
  28.9 3.0 %collective-permute-start.2 = (bf16[2,128,128]{2,1,0:T(8,128)(2,1)S(1)}, bf16[2,128,128]{2,1,0:T(8,128)(2,1)S(1)}, u32[]{:S(2)}, u32[]{:S(2)}) collective-permute-start(bf16[2,128,128]{2,1,0:T(8,128)(2,1)S(1)} %slice.4), channel_id=1, source_target_pairs={{0,64},{32,96},{64,0},{96,32},{128,192},{160,224},{192,128},{224,1... | collective-permute-start | bytes 196616 | tf_op jit(solution)/shard_map/ppermute | solution.py:411
  31.9 0.0 collective-permute-start.1
  31.9 2.4 %shard_map.76 = (bf16[4,1024,128]{2,1,0:T(8,128)(2,1)S(1)}, bf16[4,256,128]{2,1,0:T(8,128)(2,1)S(1)}, bf16[128,1024]{1,0:T(8,128)(2,1)S(1)}, f32[2,1024]{1,0:T(2,128)S(1)}, f32[128,1024]{1,0:T(8,128)S(1)}) custom-call(bf16[32,4,32,128]{3,2,1,0:T(8,128)(2,1)S(1)} %all_to_all.10.got_ref), custom_call_target="tpu_custom_call" | custom-call | flops 268435456 | bytes 2097152 | tf_op jit(solution)/shard_map/pallas_call | solution.py:370
  34.3 1.6 %shard_map.77 = (f32[2,1024]{1,0:T(2,128)S(1)}, bf16[128,1024]{1,0:T(8,128)(2,1)S(1)}, f32[2,256]{1,0:T(2,128)S(1)}, f32[128,256]{1,0:T(8,128)S(1)}, bf16[128,256]{1,0:T(8,128)(2,1)S(1)}) custom-call(bf16[4,1024,128]{2,1,0:T(8,128)(2,1)S(1)} %get-tuple-element.28.x_ref, bf16[128,1024]{1,0:T(8,128)(2,1)S(1)} %get-tuple-element.29.vt_ref, ...), custom_call_target="tpu_custom_call" | custom-call | flops 134217728 | bytes 2097152 | tf_op jit(solution)/shard_map/pallas_call | solution.py:370
  35.9 0.0 collective-permute-done.one_ref
  35.9 0.5 shard_map.79
  36.4 0.0 collective-permute-done.2.two_ref
  36.4 1.7 %collective-permute-done.1.three_ref = bf16[2,128,128]{2,1,0:T(8,128)(2,1)S(1)} collective-permute-done((bf16[2,128,128]{2,1,0:T(8,128)(2,1)S(1)}, bf16[2,128,128]{2,1,0:T(8,128)(2,1)S(1)}, u32[]{:S(2)}, u32[]{:S(2)}) %collective-permute-start.1) | collective-permute-done | bytes 65568 | tf_op jit(solution)/shard_map/ppermute | solution.py:411
  38.1 0.7 shard_map.80
  38.8 0.1 collective-permute-start.3
  38.9 1.9 %collective-permute-start.4 = (bf16[2,128,128]{2,1,0:T(8,128)(2,1)S(1)}, bf16[2,128,128]{2,1,0:T(8,128)(2,1)S(1)}, u32[]{:S(2)}, u32[]{:S(2)}) collective-permute-start(bf16[2,128,128]{2,1,0:T(8,128)(2,1)S(1)} %get-tuple-element.50), channel_id=1, source_target_pairs={{0,64},{32,96},{64,0},{96,32},{128,192},{160,224},{192,128},{224,1... | collective-permute-start | bytes 196616 | tf_op jit(solution)/shard_map/ppermute | solution.py:411
  40.8 1.7 %collective-permute-start.5 = (bf16[2,128,128]{2,1,0:T(8,128)(2,1)S(1)}, bf16[2,128,128]{2,1,0:T(8,128)(2,1)S(1)}, u32[]{:S(2)}, u32[]{:S(2)}) collective-permute-start(bf16[2,128,128]{2,1,0:T(8,128)(2,1)S(1)} %get-tuple-element.51), channel_id=1, source_target_pairs={{0,96},{32,64},{64,32},{96,0},{128,224},{160,192},{192,160},{224,1... | collective-permute-start | bytes 196616 | tf_op jit(solution)/shard_map/ppermute | solution.py:411
  42.4 3.9 %shard_map.81 = (bf16[32,4,32,128]{3,2,1,0:T(8,128)(2,1)S(1)}, f32[2,256,128]{2,1,0:T(8,128)S(1)}, bf16[2,512,128]{2,1,0:T(8,128)(2,1)S(1)}) custom-call(bf16[4,1024,128]{2,1,0:T(8,128)(2,1)S(1)} %get-tuple-element.28.x_ref, f32[2,1024]{1,0:T(2,128)S(1)} %get-tuple-element.32.stat_ref, bf16[128,1024]{1,0:T(8,128)(2,1)S(1)} %get-tuple-element.33.comb_ref, ...), custom_call_target="tpu_custom_call" | custom-call | flops 1006632960 | bytes 2097152 | tf_op jit(solution)/shard_map/pallas_call | solution.py:370
  46.4 0.0 collective-permute-done.4.two_ref
  46.4 0.6 collective-permute-done.5.three_ref
  47.0 0.0 collective-permute-done.3.one_ref
  47.0 0.3 shard_map.82
  47.3 22.5 %all_to_all.11.in_ref = bf16[32,4,32,128]{3,2,1,0:T(8,128)(2,1)S(1)} all-to-all(bf16[32,4,32,128]{3,2,1,0:T(8,128)(2,1)S(1)} %shard_map.82), channel_id=1, replica_groups=mesh['zed'=8,'y_lo'=2,'core'=2,'y_hi'=2,'x'=4] {'x','y_lo','y_hi','core'}, dimensions={0} | all-to-all | bytes 2097152 | tf_op jit(solution)/shard_map/all_to_all | solution.py:406
  69.9 1.0 %shard_map.83 = (bf16[32,4096]{1,0:T(8,128)(2,1)}, bf16[32,4096]{1,0:T(8,128)(2,1)}, bf16[32,4096]{1,0:T(8,128)(2,1)}, bf16[32,4096]{1,0:T(8,128)(2,1)}) custom-call(bf16[32,4,32,128]{3,2,1,0:T(8,128)(2,1)S(1)} %all_to_all.11.in_ref), custom_call_target="tpu_custom_call" | custom-call | tf_op jit(solution)/shard_map/pallas_call | solution.py:393
  (1 shorter events, 0.0 us)
Async XLA Ops:
  27.1 8.7 %collective-permute-start = (bf16[2,256,128]{2,1,0:T(8,128)(2,1)S(1)}, bf16[2,256,128]{2,1,0:T(8,128)(2,1)S(1)}, u32[]{:S(2)}, u32[]{:S(2)}) collective-permute-start(bf16[2,256,128]{2,1,0:T(8,128)(2,1)S(1)} %shard_map.78), channel_id=1, source_target_pairs={{0,32},{32,0},{64,96},{96,64},{128,160},{160,128},{192,224},{224,1... | collective-permute-start | bytes 393224 | tf_op jit(solution)/shard_map/ppermute | solution.py:411
  28.9 7.5 %collective-permute-start.2 = (bf16[2,128,128]{2,1,0:T(8,128)(2,1)S(1)}, bf16[2,128,128]{2,1,0:T(8,128)(2,1)S(1)}, u32[]{:S(2)}, u32[]{:S(2)}) collective-permute-start(bf16[2,128,128]{2,1,0:T(8,128)(2,1)S(1)} %slice.4), channel_id=1, source_target_pairs={{0,64},{32,96},{64,0},{96,32},{128,192},{160,224},{192,128},{224,1... | collective-permute-start | bytes 196616 | tf_op jit(solution)/shard_map/ppermute | solution.py:411
  31.9 6.2 %collective-permute-start.1 = (bf16[2,128,128]{2,1,0:T(8,128)(2,1)S(1)}, bf16[2,128,128]{2,1,0:T(8,128)(2,1)S(1)}, u32[]{:S(2)}, u32[]{:S(2)}) collective-permute-start(bf16[2,128,128]{2,1,0:T(8,128)(2,1)S(1)} %slice.4), channel_id=1, source_target_pairs={{0,96},{32,64},{64,32},{96,0},{128,224},{160,192},{192,160},{224,1... | collective-permute-start | bytes 196616 | tf_op jit(solution)/shard_map/ppermute | solution.py:411
  38.8 8.2 %collective-permute-start.3 = (bf16[2,256,128]{2,1,0:T(8,128)(2,1)S(1)}, bf16[2,256,128]{2,1,0:T(8,128)(2,1)S(1)}, u32[]{:S(2)}, u32[]{:S(2)}) collective-permute-start(bf16[2,256,128]{2,1,0:T(8,128)(2,1)S(1)} %get-tuple-element.49), channel_id=1, source_target_pairs={{0,32},{32,0},{64,96},{96,64},{128,160},{160,128},{192,224},{224,1... | collective-permute-start | bytes 393224 | tf_op jit(solution)/shard_map/ppermute | solution.py:411
  38.9 7.5 %collective-permute-start.4 = (bf16[2,128,128]{2,1,0:T(8,128)(2,1)S(1)}, bf16[2,128,128]{2,1,0:T(8,128)(2,1)S(1)}, u32[]{:S(2)}, u32[]{:S(2)}) collective-permute-start(bf16[2,128,128]{2,1,0:T(8,128)(2,1)S(1)} %get-tuple-element.50), channel_id=1, source_target_pairs={{0,64},{32,96},{64,0},{96,32},{128,192},{160,224},{192,128},{224,1... | collective-permute-start | bytes 196616 | tf_op jit(solution)/shard_map/ppermute | solution.py:411
  40.8 6.2 %collective-permute-start.5 = (bf16[2,128,128]{2,1,0:T(8,128)(2,1)S(1)}, bf16[2,128,128]{2,1,0:T(8,128)(2,1)S(1)}, u32[]{:S(2)}, u32[]{:S(2)}) collective-permute-start(bf16[2,128,128]{2,1,0:T(8,128)(2,1)S(1)} %get-tuple-element.51), channel_id=1, source_target_pairs={{0,96},{32,64},{64,32},{96,0},{128,224},{160,192},{192,160},{224,1... | collective-permute-start | bytes 196616 | tf_op jit(solution)/shard_map/ppermute | solution.py:411

commit v8 on v7

--- a/solution.py
+++ b/solution.py
@@ -242,15 +242,15 @@
                out_stat_ref, weight_ref, slope_ref, far_slope_ref, send_one_ref, send_two_ref, send_three_ref):
     inner = slice(64, 192)
     keys, values, queries, grads = one_ref[0], one_ref[1], mid_ref[2], mid_ref[3]
-    keys3 = jnp.concatenate([keys[inner], two_ref[0], three_ref[0]], axis=0)
-    values3 = jnp.concatenate([values[inner], two_ref[1], three_ref[1]], axis=0)
+    keys3 = jnp.concatenate([two_ref[0], three_ref[0]], axis=0)
+    values3 = jnp.concatenate([two_ref[1], three_ref[1]], axis=0)
     scores3, grads3 = nt(keys3, queries[inner]), nt(values3, grads[inner])
     scores2, grads2 = score_ref[...], product_ref[...]
-    new = scores3[128:]
+    new = scores3
     peak3 = jnp.max(new, axis=0, keepdims=True)
     weights3 = jnp.exp2((new - peak3) * RATE)
     total3 = jnp.sum(weights3, axis=0, keepdims=True)
-    dot3 = jnp.sum(weights3 * grads3[128:], axis=0, keepdims=True)
+    dot3 = jnp.sum(weights3 * grads3, axis=0, keepdims=True)
     weight_ref[...] = weights3.astype(BF)
     peak3 = widen(peak3, NEG)
     best = jnp.maximum(stat_ref[0:1], peak3)
@@ -266,13 +266,17 @@
     probs3 = jnp.exp2(scores3 * RATE - narrow(log_total))
     slopes3 = (probs3 * (grads3 - narrow(dot))).astype(BF)
     probs2 = jnp.exp2(scores2 * RATE - log_total)
+    row = lax.broadcasted_iota(jnp.int32, (MID, 1), 0)
+    lane = lax.broadcasted_iota(jnp.int32, (1, MID), 1)
+    both = jnp.where((row >= 64) & (row < 192), 1.0, 0.0) * jnp.where((lane >= 64) & (lane < 192), 1.0, 0.0)
+    probs2 = probs2 * (1.0 + both)
     slopes2 = (probs2 * (grads2 - dot)).astype(BF)
     dk3, dv3 = nn(slopes3, queries[inner]), nn(probs3.astype(BF), grads[inner])
     dk2, dv2 = nn(slopes2, queries), nn(probs2.astype(BF), grads)
     for index, (near, far, scale) in enumerate(((dk2, dk3, SCALE), (dv2, dv3, 1.0))):
-        send_one_ref[index] = (join(near, far[:128]) * scale).astype(BF)
-        send_two_ref[index] = (far[128:256] * scale).astype(BF)
-        send_three_ref[index] = (far[256:] * scale).astype(BF)
+        send_one_ref[index] = (near * scale).astype(BF)
+        send_two_ref[index] = (far[:128] * scale).astype(BF)
+        send_three_ref[index] = (far[128:] * scale).astype(BF)
     slope_ref[...] = slopes2
     far_slope_ref[...] = slopes3
 
@@ -313,7 +317,7 @@
         dv[cut] += value_part
     mid_grad_ref[0] = dk[LOW : LOW + MID] * SCALE
     mid_grad_ref[1] = dv[LOW : LOW + MID]
-    keys3 = jnp.concatenate([one_ref[0, 64:192], two_ref[0], three_ref[0]], axis=0)
+    keys3 = jnp.concatenate([two_ref[0], three_ref[0]], axis=0)
     distant = jnp.concatenate([two_ref[1], three_ref[1]], axis=0)
     mid_comb = mid_stat_ref[2:3] * mid_acc_ref[...] + mid_stat_ref[3:4] * widen(
         nn(flip(distant), weight_ref[...]), 0.0
@@ -460,7 +464,7 @@
             shape((4, MID), F32),
             shape((MID, 128), BF),
             shape((MID, MID), BF),
-            shape((384, 128), BF),
+            shape((256, 128), BF),
             shape((2, MID, HEAD_DIM), BF),
             shape((2, 128, HEAD_DIM), BF),
             shape((2, 128, HEAD_DIM), BF),

time: 71.1 us -> 71 us (level)
  no operation moved by 1% of the time
where the time goes in v8:
time: 71 us; the launch traced here: 70.9 us
  blocking collectives  47.5 us (67%)
  Pallas kernels  12 us (17%)
  starting transfers between devices  8.34 us (12%)
  waiting for transfers between devices  2.29 us (3%)
  between operations  0.73 us (1%)
    all_to_all x2, blocking collectives, plane_exchange(): lax.all_to_all(packed, ('x', 'y_lo', 'y_hi', 'core'), split_axis=0, conca...  47.5 us
    pallas_call x7, Pallas kernels, call(): pl.pallas_call(kernel, out_shape=outs, scratch_shapes=list(scratch), comp...  9.65 us
    ppermute x6, starting transfers between devices, z_exchange(): return lax.ppermute(block, 'zed', [(at, at ^ apart) for at in range(count)])  8.34 us
    ppermute x6, waiting for transfers between devices, z_exchange(): return lax.ppermute(block, 'zed', [(at, at ^ apart) for at in range(count)])  2.29 us
  transfers between devices with their start and end apart: 6, of which 2 were waited for; matrix products, arithmetic and copies ran while one was open for 0% of the time, Pallas kernels for 12%

profile of v8, /device:TPU:1, one launch (start us, length us, event | category | flops | bytes accessed | tf_op | source)
XLA Modules:
  0.0 70.9 jit_solution(5747551047765156003)
XLA Ops:
  0.6 1.3 %shard_map.75 = bf16[32,4,32,128]{3,2,1,0:T(8,128)(2,1)S(1)} custom-call(bf16[32,4096]{1,0:T(8,128)(2,1)} %key_ref.1, bf16[32,4096]{1,0:T(8,128)(2,1)} %value_ref.1, bf16[32,4096]{1,0:T(8,128)(2,1)} %query_ref.1, bf16[32,4096]{1,0:T(8,128)(2,1)} %grad_ref.1), custom_call_target="tpu_custom_call" | custom-call | tf_op jit(solution)/shard_map/pallas_call | solution.py:384
  1.9 25.0 %all_to_all.10.got_ref = bf16[32,4,32,128]{3,2,1,0:T(8,128)(2,1)S(1)} all-to-all(bf16[32,4,32,128]{3,2,1,0:T(8,128)(2,1)S(1)} %shard_map.75), channel_id=1, replica_groups=mesh['zed'=8,'y_lo'=2,'core'=2,'y_hi'=2,'x'=4] {'x','y_lo','y_hi','core'}, dimensions={0} | all-to-all | bytes 2097152 | tf_op jit(solution)/shard_map/all_to_all | solution.py:410
  26.9 0.2 shard_map.78
  27.1 1.7 %collective-permute-start = (bf16[2,256,128]{2,1,0:T(8,128)(2,1)S(1)}, bf16[2,256,128]{2,1,0:T(8,128)(2,1)S(1)}, u32[]{:S(2)}, u32[]{:S(2)}) collective-permute-start(bf16[2,256,128]{2,1,0:T(8,128)(2,1)S(1)} %shard_map.78), channel_id=1, source_target_pairs={{0,32},{32,0},{64,96},{96,64},{128,160},{160,128},{192,224},{224,1... | collective-permute-start | bytes 393224 | tf_op jit(solution)/shard_map/ppermute | solution.py:415
  28.9 3.0 %collective-permute-start.2 = (bf16[2,128,128]{2,1,0:T(8,128)(2,1)S(1)}, bf16[2,128,128]{2,1,0:T(8,128)(2,1)S(1)}, u32[]{:S(2)}, u32[]{:S(2)}) collective-permute-start(bf16[2,128,128]{2,1,0:T(8,128)(2,1)S(1)} %slice.4), channel_id=1, source_target_pairs={{0,64},{32,96},{64,0},{96,32},{128,192},{160,224},{192,128},{224,1... | collective-permute-start | bytes 196616 | tf_op jit(solution)/shard_map/ppermute | solution.py:415
  31.9 0.0 collective-permute-start.1
  31.9 2.4 %shard_map.76 = (bf16[4,1024,128]{2,1,0:T(8,128)(2,1)S(1)}, bf16[4,256,128]{2,1,0:T(8,128)(2,1)S(1)}, bf16[128,1024]{1,0:T(8,128)(2,1)S(1)}, f32[2,1024]{1,0:T(2,128)S(1)}, f32[128,1024]{1,0:T(8,128)S(1)}) custom-call(bf16[32,4,32,128]{3,2,1,0:T(8,128)(2,1)S(1)} %all_to_all.10.got_ref), custom_call_target="tpu_custom_call" | custom-call | flops 268435456 | bytes 2097152 | tf_op jit(solution)/shard_map/pallas_call | solution.py:374
  34.3 1.6 %shard_map.77 = (f32[2,1024]{1,0:T(2,128)S(1)}, bf16[128,1024]{1,0:T(8,128)(2,1)S(1)}, f32[2,256]{1,0:T(2,128)S(1)}, f32[128,256]{1,0:T(8,128)S(1)}, bf16[128,256]{1,0:T(8,128)(2,1)S(1)}) custom-call(bf16[4,1024,128]{2,1,0:T(8,128)(2,1)S(1)} %get-tuple-element.28.x_ref, bf16[128,1024]{1,0:T(8,128)(2,1)S(1)} %get-tuple-element.29.vt_ref, ...), custom_call_target="tpu_custom_call" | custom-call | flops 134217728 | bytes 2097152 | tf_op jit(solution)/shard_map/pallas_call | solution.py:374
  35.9 0.0 collective-permute-done.one_ref
  35.9 0.5 shard_map.79
  36.4 0.0 collective-permute-done.2.two_ref
  36.4 1.7 %collective-permute-done.1.three_ref = bf16[2,128,128]{2,1,0:T(8,128)(2,1)S(1)} collective-permute-done((bf16[2,128,128]{2,1,0:T(8,128)(2,1)S(1)}, bf16[2,128,128]{2,1,0:T(8,128)(2,1)S(1)}, u32[]{:S(2)}, u32[]{:S(2)}) %collective-permute-start.1) | collective-permute-done | bytes 65568 | tf_op jit(solution)/shard_map/ppermute | solution.py:415
  38.1 0.7 shard_map.80
  38.7 0.1 collective-permute-start.3
  38.8 1.9 %collective-permute-start.4 = (bf16[2,128,128]{2,1,0:T(8,128)(2,1)S(1)}, bf16[2,128,128]{2,1,0:T(8,128)(2,1)S(1)}, u32[]{:S(2)}, u32[]{:S(2)}) collective-permute-start(bf16[2,128,128]{2,1,0:T(8,128)(2,1)S(1)} %get-tuple-element.50), channel_id=1, source_target_pairs={{0,64},{32,96},{64,0},{96,32},{128,192},{160,224},{192,128},{224,1... | collective-permute-start | bytes 196616 | tf_op jit(solution)/shard_map/ppermute | solution.py:415
  40.7 1.7 %collective-permute-start.5 = (bf16[2,128,128]{2,1,0:T(8,128)(2,1)S(1)}, bf16[2,128,128]{2,1,0:T(8,128)(2,1)S(1)}, u32[]{:S(2)}, u32[]{:S(2)}) collective-permute-start(bf16[2,128,128]{2,1,0:T(8,128)(2,1)S(1)} %get-tuple-element.51), channel_id=1, source_target_pairs={{0,96},{32,64},{64,32},{96,0},{128,224},{160,192},{192,160},{224,1... | collective-permute-start | bytes 196616 | tf_op jit(solution)/shard_map/ppermute | solution.py:415
  42.4 3.9 %shard_map.81 = (bf16[32,4,32,128]{3,2,1,0:T(8,128)(2,1)S(1)}, f32[2,256,128]{2,1,0:T(8,128)S(1)}, bf16[2,512,128]{2,1,0:T(8,128)(2,1)S(1)}) custom-call(bf16[4,1024,128]{2,1,0:T(8,128)(2,1)S(1)} %get-tuple-element.28.x_ref, f32[2,1024]{1,0:T(2,128)S(1)} %get-tuple-element.32.stat_ref, bf16[128,1024]{1,0:T(8,128)(2,1)S(1)} %get-tuple-element.33.comb_ref, ...), custom_call_target="tpu_custom_call" | custom-call | flops 1006632960 | bytes 2097152 | tf_op jit(solution)/shard_map/pallas_call | solution.py:374
  46.3 0.0 collective-permute-done.4.two_ref
  46.3 0.6 collective-permute-done.5.three_ref
  46.9 0.0 collective-permute-done.3.one_ref
  46.9 0.3 shard_map.82
  47.3 22.5 %all_to_all.11.in_ref = bf16[32,4,32,128]{3,2,1,0:T(8,128)(2,1)S(1)} all-to-all(bf16[32,4,32,128]{3,2,1,0:T(8,128)(2,1)S(1)} %shard_map.82), channel_id=1, replica_groups=mesh['zed'=8,'y_lo'=2,'core'=2,'y_hi'=2,'x'=4] {'x','y_lo','y_hi','core'}, dimensions={0} | all-to-all | bytes 2097152 | tf_op jit(solution)/shard_map/all_to_all | solution.py:410
  69.8 1.0 %shard_map.83 = (bf16[32,4096]{1,0:T(8,128)(2,1)}, bf16[32,4096]{1,0:T(8,128)(2,1)}, bf16[32,4096]{1,0:T(8,128)(2,1)}, bf16[32,4096]{1,0:T(8,128)(2,1)}) custom-call(bf16[32,4,32,128]{3,2,1,0:T(8,128)(2,1)S(1)} %all_to_all.11.in_ref), custom_call_target="tpu_custom_call" | custom-call | tf_op jit(solution)/shard_map/pallas_call | solution.py:397
  (1 shorter events, 0.0 us)
Async XLA Ops:
  27.1 8.7 %collective-permute-start = (bf16[2,256,128]{2,1,0:T(8,128)(2,1)S(1)}, bf16[2,256,128]{2,1,0:T(8,128)(2,1)S(1)}, u32[]{:S(2)}, u32[]{:S(2)}) collective-permute-start(bf16[2,256,128]{2,1,0:T(8,128)(2,1)S(1)} %shard_map.78), channel_id=1, source_target_pairs={{0,32},{32,0},{64,96},{96,64},{128,160},{160,128},{192,224},{224,1... | collective-permute-start | bytes 393224 | tf_op jit(solution)/shard_map/ppermute | solution.py:415
  28.9 7.5 %collective-permute-start.2 = (bf16[2,128,128]{2,1,0:T(8,128)(2,1)S(1)}, bf16[2,128,128]{2,1,0:T(8,128)(2,1)S(1)}, u32[]{:S(2)}, u32[]{:S(2)}) collective-permute-start(bf16[2,128,128]{2,1,0:T(8,128)(2,1)S(1)} %slice.4), channel_id=1, source_target_pairs={{0,64},{32,96},{64,0},{96,32},{128,192},{160,224},{192,128},{224,1... | collective-permute-start | bytes 196616 | tf_op jit(solution)/shard_map/ppermute | solution.py:415
  31.9 6.2 %collective-permute-start.1 = (bf16[2,128,128]{2,1,0:T(8,128)(2,1)S(1)}, bf16[2,128,128]{2,1,0:T(8,128)(2,1)S(1)}, u32[]{:S(2)}, u32[]{:S(2)}) collective-permute-start(bf16[2,128,128]{2,1,0:T(8,128)(2,1)S(1)} %slice.4), channel_id=1, source_target_pairs={{0,96},{32,64},{64,32},{96,0},{128,224},{160,192},{192,160},{224,1... | collective-permute-start | bytes 196616 | tf_op jit(solution)/shard_map/ppermute | solution.py:415
  38.7 8.2 %collective-permute-start.3 = (bf16[2,256,128]{2,1,0:T(8,128)(2,1)S(1)}, bf16[2,256,128]{2,1,0:T(8,128)(2,1)S(1)}, u32[]{:S(2)}, u32[]{:S(2)}) collective-permute-start(bf16[2,256,128]{2,1,0:T(8,128)(2,1)S(1)} %get-tuple-element.49), channel_id=1, source_target_pairs={{0,32},{32,0},{64,96},{96,64},{128,160},{160,128},{192,224},{224,1... | collective-permute-start | bytes 393224 | tf_op jit(solution)/shard_map/ppermute | solution.py:415
  38.8 7.5 %collective-permute-start.4 = (bf16[2,128,128]{2,1,0:T(8,128)(2,1)S(1)}, bf16[2,128,128]{2,1,0:T(8,128)(2,1)S(1)}, u32[]{:S(2)}, u32[]{:S(2)}) collective-permute-start(bf16[2,128,128]{2,1,0:T(8,128)(2,1)S(1)} %get-tuple-element.50), channel_id=1, source_target_pairs={{0,64},{32,96},{64,0},{96,32},{128,192},{160,224},{192,128},{224,1... | collective-permute-start | bytes 196616 | tf_op jit(solution)/shard_map/ppermute | solution.py:415
  40.7 6.2 %collective-permute-start.5 = (bf16[2,128,128]{2,1,0:T(8,128)(2,1)S(1)}, bf16[2,128,128]{2,1,0:T(8,128)(2,1)S(1)}, u32[]{:S(2)}, u32[]{:S(2)}) collective-permute-start(bf16[2,128,128]{2,1,0:T(8,128)(2,1)S(1)} %get-tuple-element.51), channel_id=1, source_target_pairs={{0,96},{32,64},{64,32},{96,0},{128,224},{160,192},{192,160},{224,1... | collective-permute-start | bytes 196616 | tf_op jit(solution)/shard_map/ppermute | solution.py:415
